TPU v7x, 32 devices: a whole 2x2x4 slice. The times are simulated.
32 devices in a mesh: groups: 2 (over y), aux: 4 (over z), orb: 4 (over x, core).
Axes of the slice: x: 2, y: 2, z: 4, core: 2. Of those that a mesh axis runs over, the one named last changes fastest.
Arguments:
- tiles: bfloat16 [512, 128, 128], P(('groups', 'aux')), parts along dimension 0, may hold values from -0.25 to 0.25
- slot_aux: int32 [8, 64], P('groups'), parts along dimension 0, may hold values from 0 to 31
- slot_basis: int32 [8, 64], P('groups'), parts along dimension 0, may hold values from 0 to 239, as said below
- slot_count: int32 [8], P('groups'), parts along dimension 0, may hold values from 8 to 64
- orbitals: bfloat16 [61440, 2048], P(('groups', 'aux'), 'orb'), parts along dimension 0, may hold values from -6 to 6
- fit_rows: bfloat16 [8192, 4096], P(('groups', 'aux')), parts along dimension 0, may hold values from -1 to 1
Outputs:
- exchange: float32 [4096, 2048], P(('groups', 'aux'), 'orb'), parts along dimension 0
There are 2 independent parts, one for each index of `groups`. A program takes and returns all parts, laid end to end along the dimension named above; each array names one. Nothing has to cross between parts.
Inputs may be any that keep to these rules, and one draw needn't show every extreme that they name: `slot_basis`: within each row, the first slot_count entries never fall.
All inputs are finite; a program needn't handle non-finite values.
Results may differ from a plain program's by a relative error of at most 0.0031.
Values may be sent and summed in bfloat16 or wider, within the bound.
No kernel may reach another device: no remote copies, remote signals or barrier semaphores. Data moves between devices by JAX's collectives and lax.ppermute only.
A program may use at most 192 MiB of HBM per device.

v0:
```python
import functools
import math

import jax
import jax.numpy as jnp
from jax import lax
from jax.experimental import pallas as pl
from jax.experimental.pallas import tpu as pltpu
from jax.sharding import PartitionSpec as P

LANES = 128
CHUNKS = 16
LAG = 2
UNROLL = 2


def rotation(size, by):
    return [(i, (i + by) % size) for i in range(size)]


def flipped(size, bit):
    return [(i, i ^ bit) for i in range(size)]


def over_members(array, axis, size, first=None):
    held = {0: array} | (first or {})
    bit = size // 4 if first else size // 2
    while bit:
        held |= {e | bit: lax.ppermute(a, axis, flipped(size, bit)) for e, a in held.items()}
        bit //= 2
    return [held[e] for e in range(size)]


def spread_kernel(planes, across, cap, place, table_aux, table_basis, begins, counts, own_tiles, *refs):
    received = refs[:-10]
    overflow, orbitals, sums, own, panels, held, chosen, owners, bases, arrived = refs[-10:]
    slots, tile = own_tiles.shape[:2]
    part = cap // across
    position, member, rounds = place[0], place[1], place[2]
    local_bases = panels.shape[0] // tile
    groups = sums.shape[0]

    early = [
        pltpu.make_async_copy(own_tiles, own, arrived.at[len(received)]),
        pltpu.make_async_copy(orbitals, panels, arrived.at[len(received) + 1]),
    ]
    for copy in early:
        copy.start()
    copies, at = [], 0
    for n, tiles in enumerate(received):
        copies.append(pltpu.make_async_copy(tiles, held.at[pl.ds(at, tiles.shape[0])], arrived.at[n]))
        at += tiles.shape[0]
    for copy in copies:
        copy.start()

    def clear(n, _):
        for g in range(groups):
            sums[g, pl.ds(pl.multiple_of(n * tile, tile), tile), :] = jnp.zeros((tile, LANES), jnp.float32)
        return 0

    lax.fori_loop(0, sums.shape[1] // tile, clear, 0)

    def rows_of(source, slot):
        return table_aux[source, slot] * tile, (table_basis[source, slot] - position * local_bases) * tile

    def ranges(turn, side, source):
        first = begins[source, position] + turn * cap
        last = jnp.minimum(first + cap, begins[source, position] + counts[source, position])
        begin = jnp.minimum(first, slots - cap) + side * part
        return begin, jnp.clip(first - begin, 0, part), jnp.clip(last - begin, 0, part)

    def term_of(block, base):
        panel = panels[pl.ds(pl.multiple_of(base, tile), tile), :]
        return jnp.dot(block, panel, preferred_element_type=jnp.float32)

    def add(owner, term):
        for g in range(groups):
            sums[g, pl.ds(pl.multiple_of(owner, tile), tile), :] += term[:, g * LANES : (g + 1) * LANES]

    def note_part(n, count):
        e, q = n // (planes - 1), lax.rem(n, planes - 1)
        source = lax.rem(position + (planes - 1 - q), planes)
        begin, low, high = ranges(0, member ^ e, source)

        def note(i, count):
            chosen[count] = n * part + i
            owners[count], bases[count] = rows_of(source, begin + i)
            return count + 1

        return lax.fori_loop(low, high, note, count)

    count = lax.fori_loop(0, across * (planes - 1), note_part, jnp.int32(0))
    for i in range(UNROLL - 1):
        chosen[count + i] = 0
        owners[count + i] = 0
        bases[count + i] = 0

    for copy in early:
        copy.wait()
    own_first = begins[position, position]
    own_count = counts[position, position]

    def several_own(n, _):
        terms = []
        for i in range(UNROLL):
            used = n * UNROLL + i < own_count
            slot = jnp.minimum(own_first + n * UNROLL + i, slots - 1)
            owner, base = rows_of(position, slot)
            term = term_of(own[slot], jnp.where(used, base, 0))
            terms.append((owner, jnp.where(used, term, 0.0)))
        for owner, term in terms:
            add(owner, term)
        return 0

    lax.fori_loop(0, (own_count + UNROLL - 1) // UNROLL, several_own, 0)
    for copy in copies:
        copy.wait()

    def several(n, _):
        terms = []
        for i in range(UNROLL):
            at = n * UNROLL + i
            term = term_of(held[chosen[at]], bases[at])
            terms.append((owners[at], jnp.where(at < count, term, 0.0)))
        for owner, term in terms:
            add(owner, term)
        return 0

    lax.fori_loop(0, (count + UNROLL - 1) // UNROLL, several, 0)

    def late_round(turn, _):
        def late_part(n, _):
            e, q = n // (planes - 1), lax.rem(n, planes - 1)
            source = lax.rem(position + (planes - 1 - q), planes)
            begin, low, high = ranges(turn, member ^ e, source)

            def late_one(i, _):
                pltpu.sync_copy(overflow.at[turn - 1, e, q * part + i], held.at[0])
                owner, base = rows_of(source, begin + i)
                add(owner, term_of(held[0], base))
                return 0

            return lax.fori_loop(low, high, late_one, 0)

        return lax.fori_loop(0, across * (planes - 1), late_part, 0)

    lax.fori_loop(1, rounds, late_round, 0)


def spread(place, tables, tiles, received, overflow, orbitals, rows, planes, across, cap):
    slots, tile = tiles.shape[:2]
    most = sum(r.shape[0] for r in received)
    smem = pl.BlockSpec(memory_space=pltpu.SMEM)
    vmem = pl.BlockSpec(memory_space=pltpu.VMEM)
    hbm = pl.BlockSpec(memory_space=pltpu.HBM)
    return pl.pallas_call(
        functools.partial(spread_kernel, planes, across, cap),
        out_shape=jax.ShapeDtypeStruct((orbitals.shape[1] // LANES, rows, LANES), jnp.float32),
        in_specs=[smem] * 5 + [hbm] * (1 + len(received) + 2),
        out_specs=vmem,
        scratch_shapes=[
            pltpu.VMEM(tiles.shape, tiles.dtype),
            pltpu.VMEM(orbitals.shape, orbitals.dtype),
            pltpu.VMEM((most, tile, tile), tiles.dtype),
            pltpu.SMEM((most + UNROLL,), jnp.int32),
            pltpu.SMEM((most + UNROLL,), jnp.int32),
            pltpu.SMEM((most + UNROLL,), jnp.int32),
            pltpu.SemaphoreType.DMA((len(received) + 2,)),
        ],
        compiler_params=pltpu.CompilerParams(vmem_limit_bytes=52 * 1024 * 1024),
        cost_estimate=pl.CostEstimate(
            flops=2 * slots * tile * tile * orbitals.shape[1],
            bytes_accessed=24 * 1024 * 1024,
            transcendentals=0,
        ),
    )(place, *tables, tiles, *received, overflow, orbitals)


def largest_kernel(steps, tiles, source, largest, panels, blocks, arrived):
    size = source.shape[0] // steps
    lanes = tiles.shape[-1]

    def piece(n):
        rows = pl.ds(n * size, size)
        return pltpu.make_async_copy(source.at[rows], panels.at[rows], arrived.at[n])

    whole = pltpu.make_async_copy(tiles, blocks, arrived.at[steps])
    whole.start()
    for n in range(steps):
        piece(n).start()
    whole.wait()

    def most_of_tile(n, most):
        return jnp.maximum(most, jnp.max(jnp.abs(blocks[n].reshape(-1, 16, lanes)), axis=0))

    most = lax.fori_loop(0, tiles.shape[0], most_of_tile, jnp.zeros((16, lanes), tiles.dtype))
    largest[0] = most.astype(jnp.float32)
    part = math.gcd(size, 240)

    def most_of_rows(n, most):
        block = panels[pl.ds(pl.multiple_of(n * part, part), part), :]
        return jnp.maximum(most, jnp.max(jnp.abs(block.reshape(-1, 16, source.shape[1])), axis=0))

    most = jnp.zeros((16, source.shape[1]), source.dtype)
    for n in range(steps):
        piece(n).wait()
        most = lax.fori_loop(n * (size // part), (n + 1) * (size // part), most_of_rows, most)
    across = most[:, :lanes]
    for g in range(1, source.shape[1] // lanes):
        across = jnp.maximum(across, most[:, g * lanes : (g + 1) * lanes])
    largest[1] = across.astype(jnp.float32)


def largest_of(tiles, orbitals):
    steps = 8
    hbm = pl.BlockSpec(memory_space=pltpu.HBM)
    return pl.pallas_call(
        functools.partial(largest_kernel, steps),
        out_shape=jax.ShapeDtypeStruct((2, 16, tiles.shape[-1]), jnp.float32),
        in_specs=[hbm, hbm],
        out_specs=pl.BlockSpec(memory_space=pltpu.VMEM),
        scratch_shapes=[
            pltpu.VMEM(orbitals.shape, orbitals.dtype),
            pltpu.VMEM(tiles.shape, tiles.dtype),
            pltpu.SemaphoreType.DMA((steps + 1,)),
        ],
        compiler_params=pltpu.CompilerParams(vmem_limit_bytes=52 * 1024 * 1024),
        cost_estimate=pl.CostEstimate(flops=0, bytes_accessed=10 * 1024 * 1024, transcendentals=0),
    )(tiles, orbitals)


def unfilled(shape, dtype):
    return pl.pallas_call(
        lambda out: None,
        out_shape=jax.ShapeDtypeStruct(shape, dtype),
        out_specs=pl.BlockSpec(memory_space=pltpu.HBM),
    )()


def all_planes(partial, consume, at_step, groups, rows, planes, position, scale):
    half = planes // 2
    per_group = CHUNKS // groups
    size = rows // per_group
    hops = planes - 1
    mirrored = hops - position
    in_left = position < half
    even = position % 2 == 0
    far = jnp.maximum(position, mirrored)
    got, paid = {}, {}
    total_steps = CHUNKS + LAG * hops

    def own_rows(s, rank):
        chunks = [s - LAG * r for r in range(half)]
        if not any(0 <= c < CHUNKS for c in chunks):
            return None
        at = jnp.clip(s - LAG * rank, 0, CHUNKS - 1) * size
        return lax.dynamic_slice_in_dim(partial, at, size, 0)

    def payload(s, rank, before, crossing):
        rows = own_rows(s, rank)
        total = None if rows is None else rows * scale
        if before is not None:
            crossing = jnp.where(rank == half, crossing.astype(jnp.float32), 0.0)
            added = crossing if total is None else jnp.where(rank < half, total, crossing)
            total = before.astype(jnp.float32) + added
        return total.astype(jnp.float16)

    def payloads(s):
        right_before = left_before = right_paid = left_paid = None
        if s - LAG in got:
            over_even, over_odd = got[s - LAG]
            right_before, left_before = jnp.where(even, over_odd, over_even), jnp.where(even, over_even, over_odd)
            over_even, over_odd = paid[s - LAG]
            right_paid, left_paid = jnp.where(even, over_even, over_odd), jnp.where(even, over_odd, over_even)
        right = payload(s, position, right_before, left_paid)
        left = payload(s, mirrored, left_before, right_paid)
        return jnp.where(even, right, left), jnp.where(even, left, right)

    def finished(group):
        pieces = []
        for k in range(group * per_group, (group + 1) * per_group):
            chunk = None
            for r in range(half, planes):
                over_even, over_odd = paid[k + LAG * r]
                this = jnp.where(in_left == even, over_odd, over_even)
                chunk = this if chunk is None else jnp.where(far == r, this, chunk)
            pieces.append(chunk)
        whole = jnp.concatenate(pieces, axis=0).astype(jnp.float32)
        return lax.optimization_barrier((whole * (1.0 / scale)).astype(jnp.bfloat16))

    waiting = []
    for s in range(total_steps):
        if s - LAG in got:
            got[s - LAG], *_ = lax.optimization_barrier((got[s - LAG], paid[s - 1], *waiting))
            waiting = []
        paid[s] = payloads(s)
        links = ([], [])
        for i in range(hops):
            if 0 <= s - LAG * i < CHUNKS:
                links[i % 2].append((i, i + 1))
            if 0 <= s - LAG * (hops - 1 - i) < CHUNKS:
                links[i % 2].append((i + 1, i))
        if links[0] or links[1]:
            got[s] = tuple(
                lax.ppermute(p, "aux", pairs) if pairs else jnp.zeros_like(p) for p, pairs in zip(paid[s], links)
            )
        group, rest = divmod(s - LAG * hops + 1, per_group)
        if group > 0 and rest == 0:
            waiting.append(consume(group - 1, finished(group - 1)))
        waiting += at_step(total_steps - s)


def shards(tiles, slot_aux, slot_basis, slot_count, orbitals, fit_rows, *, groups, planes, across):
    position = lax.axis_index("aux")
    member = lax.axis_index("orb")
    slots, tile = tiles.shape[:2]
    aux_rows = fit_rows.shape[1]
    width = orbitals.shape[1]
    local_bases = orbitals.shape[0] // tile
    cap = min(slots, across * -(-7 * slots // (4 * planes * across)))
    part = cap // across
    later = -(-slots // cap) - 1

    live = jnp.arange(slots, dtype=jnp.int32)[None, :] < slot_count[:, None]
    target = jnp.where(live, slot_basis // local_bases, planes)
    plane_ids = jnp.arange(planes, dtype=jnp.int32)
    begins = jnp.sum(target[:, None, :] < plane_ids[None, :, None], axis=2, dtype=jnp.int32)
    counts = jnp.sum(target[:, None, :] == plane_ids[None, :, None], axis=2, dtype=jnp.int32)
    away = jnp.where(plane_ids[:, None] == plane_ids[None, :], 0, counts)
    rounds = (jnp.max(away) + cap - 1) // cap
    send_first = lax.dynamic_index_in_dim(begins, position, 0, keepdims=False)

    def exchange(turn):
        chosen = []
        for by in range(1, planes):
            first = send_first[(position + by) % planes] + turn * cap
            begin = jnp.minimum(first, slots - cap) + member * part
            chosen.append(lax.dynamic_slice_in_dim(tiles, begin, part, 0))
        return lax.optimization_barrier(chosen)

    def over_planes(chosen):
        return [lax.ppermute(c, "aux", rotation(planes, by)) for by, c in enumerate(chosen, 1)]

    def bound_of(largest):
        largest = jnp.broadcast_to(jnp.max(largest, axis=(1, 2))[:, None], (2, LANES))
        return [largest] + [lax.ppermute(largest, "aux", rotation(planes, by)) for by in range(1, planes)]

    chosen = exchange(jnp.int32(0))
    all_tiles, all_orbitals, rounds, _ = lax.optimization_barrier((tiles, orbitals, rounds, chosen))
    largest = largest_of(all_tiles, all_orbitals)
    most = rounds
    for by in range(1, groups):
        most = jnp.maximum(most, lax.ppermute(rounds, "groups", rotation(groups, by)))
    if planes == 4:
        first_hop = flipped(across, across // 2)
        sent, hopped = [lax.ppermute(chosen[0], "aux", rotation(planes, 1))], []
        later_tiles, sent[0], largest = lax.optimization_barrier((chosen[1], sent[0], largest))
        others = bound_of(largest)
        sent.append(lax.ppermute(later_tiles, "aux", rotation(planes, 2)))
        hopped.append(lax.ppermute(sent[0], "orb", first_hop))
        later_tiles, sent[1], hopped[0], others = lax.optimization_barrier((chosen[2], sent[1], hopped[0], others))
        sent.append(lax.ppermute(later_tiles, "aux", rotation(planes, 3)))
        hopped.append(lax.ppermute(sent[1], "orb", first_hop))
        sent[2], hopped[1], most = lax.optimization_barrier((sent[2], hopped[1], most))
        hopped.append(lax.ppermute(sent[2], "orb", first_hop))
        held = [over_members(a, "orb", across, {across // 2: h}) for a, h in zip(sent, hopped)]
        received = [h[e] for e in range(across) for h in held]
    else:
        others = bound_of(largest)
        received = over_members(jnp.concatenate(over_planes(chosen), axis=0), "orb", across)
    largest = functools.reduce(jnp.maximum, others)
    bound = tile * jnp.sum(counts).astype(jnp.float32) * largest[0, 0] * largest[1, 0]
    scale = 32768.0 / jnp.maximum(bound, 1e-30)

    def more(state):
        turn, kept = state
        arrived = jnp.concatenate(over_planes(exchange(turn)), axis=0)
        tiles_now = jnp.stack(over_members(arrived, "orb", across))
        return turn + 1, lax.dynamic_update_index_in_dim(kept, tiles_now, turn - 1, 0)

    batch = (planes - 1) * part
    empty = unfilled((max(later, 1), across, batch, tile, tile), tiles.dtype)
    _, overflow = lax.while_loop(lambda state: state[0] < most, more, (jnp.int32(1), empty))
    place = jnp.stack([position, member, most]).astype(jnp.int32)

    tables = (slot_aux, slot_basis, begins, counts)
    partial = spread(place, tables, tiles, received, overflow, orbitals, aux_rows, planes, across, cap)
    partial = partial.reshape(-1, LANES)
    column_groups = width // LANES
    fitted, wide = [], []
    square = planes == across
    blocks = {}

    def product(left, right):
        return jnp.einsum("pj,pi->ji", left, right, preferred_element_type=jnp.float32)

    def scatter(parts):
        stacked = jnp.stack(parts)

        def to(plane):
            return lax.dynamic_index_in_dim(stacked, plane ^ member, 0, keepdims=False)

        sent = [to((position + by) % planes).astype(jnp.bfloat16) for by in range(1, planes)]
        return [to(position)] + [lax.ppermute(t, "aux", rotation(planes, by)) for by, t in enumerate(sent, 1)], sent

    def total(terms):
        return sum((t.astype(jnp.float32) for t in terms[1:]), terms[0])

    def consume(g, rounded):
        last = g == column_groups - 1
        if square and last:
            rounded, _ = lax.optimization_barrier((rounded, blocks["corner_sent"]))
        own = jnp.dot(fit_rows, rounded, preferred_element_type=jnp.float32).astype(jnp.bfloat16)
        if square and last:
            blocks["upper"], _ = scatter([product(w, own) for w in blocks["early"]])
        fitted.append(own)
        if square:
            wide.append(over_members(own, "orb", across))
        if square and g == column_groups - 2:
            blocks["early"] = [jnp.concatenate([w[e] for w in wide], axis=1) for e in range(across)]
            inner = jnp.concatenate(fitted, axis=1)
            blocks["terms"] = [product(w, inner) for w in blocks["early"]]
        return own

    def at_step(steps_left):
        if "terms" in blocks and "corner" not in blocks and steps_left <= 3:
            blocks["corner"], blocks["corner_sent"] = scatter(blocks["terms"])
            return list(blocks["terms"])
        return []

    all_planes(partial, consume, at_step, column_groups, aux_rows, planes, position, scale)
    fitted = jnp.concatenate(fitted, axis=1)
    if square:
        lower = total(scatter([product(w, fitted) for w in wide[-1]])[0])
        upper = jnp.concatenate([total(blocks["corner"]), total(blocks["upper"])], axis=1)
        return jnp.concatenate([upper, lower], axis=0)
    wide = lax.all_gather(fitted, "orb", axis=1, tiled=True)
    return lax.psum_scatter(product(wide, fitted), "aux", scatter_dimension=0, tiled=True)


def solution(mesh):
    body = functools.partial(
        shards,
        groups=mesh.shape["groups"],
        planes=mesh.shape["aux"],
        across=mesh.shape["orb"],
    )
    return jax.shard_map(
        body,
        mesh=mesh,
        in_specs=(
            P(("groups", "aux"), None, None),
            P("groups", None),
            P("groups", None),
            P("groups"),
            P(("groups", "aux"), "orb"),
            P(("groups", "aux"), None),
        ),
        out_specs=P(("groups", "aux"), "orb"),
        check_vma=False,
    )
```

profile of v0, /device:TPU:13, one launch (start us, length us, event | category | flops | bytes accessed | tf_op | source)
XLA Modules:
  0.0 255.4 jit_solution(2425785399723198311)
XLA Ops:
  5.4 1.3 collective-permute-start.6
  8.1 4.0 %shard_map.64 = f32[2,16,128]{2,1,0:T(8,128)S(1)} custom-call(bf16[64,128,128]{2,1,0:T(8,128)(2,1)} %own_tiles.1, bf16[7680,512]{1,0:T(8,128)(2,1)} %refs_13_.1), custom_call_target="tpu_custom_call" | custom-call | bytes 10485760 | tf_op jit(solution)/shard_map/pallas_call | solution.py:217
  12.1 2.2 collective-permute-start.7
  16.6 1.5 collective-permute-start.10
  18.1 6.4 %collective-permute-done.9 = f32[2,128]{1,0:T(2,128)S(1)} collective-permute-done((f32[2,128]{1,0:T(2,128)S(1)}, f32[2,128]{1,0:T(2,128)S(1)}, u32[]{:S(2)}, u32[]{:S(2)}) %collective-permute-start.9) | collective-permute-done | bytes 1056 | tf_op jit(solution)/shard_map/ppermute | solution.py:346
  25.3 1.5 collective-permute-start.12
  31.3 2.0 collective-permute-start.15
  34.3 2.0 collective-permute-start.16
  36.9 2.1 collective-permute-done.18.refs_8_
  39.0 2.4 collective-permute-start.21
  44.3 13.5 %shard_map.66 = f32[4,4096,128]{2,1,0:T(8,128)} custom-call(s32[3]{0:T(128)S(1)} %pad_add_fusion.place, s32[4,64]{1,0:T(4,128)S(1)} %copy-done.1, s32[4,64]{1,0:T(4,128)S(1)} %copy-done, s32[4,4]{1,0:T(4,128)S(1)} %get-tuple-element.327.begins, s32[4,4]{1,0:T(4,128)S(1)} %get-tuple-element.326.counts, bf16[64,128,128]{2,1,0:T(8,128)(2,1)} %get-tuple-element.576, ...), custom_call_target="tpu_custom_call" | custom-call | flops 1073741824 | bytes 25165824 | tf_op jit(solution)/shard_map/pallas_call | solution.py:156
  57.8 2.0 broadcast_select_fusion.41
  62.5 7.1 %collective-permute-done.22 = f16[1024,128]{1,0:T(8,128)(2,1)S(1)} collective-permute-done((f16[1024,128]{1,0:T(8,128)(2,1)S(1)}, f16[1024,128]{1,0:T(8,128)(2,1)S(1)}, u32[]{:S(2)}, u32[]{:S(2)}) %collective-permute-start.22) | collective-permute-done | bytes 262176 | tf_op jit(solution)/shard_map/ppermute | solution.py:305
  69.7 1.8 broadcast_select_fusion.35
  71.5 1.6 collective-permute-start.23
  73.1 2.4 collective-permute-start.24
  75.5 1.6 broadcast_select_fusion.33
  78.6 2.9 %collective-permute-start.29 = (f16[1024,128]{1,0:T(8,128)(2,1)S(1)}, f16[1024,128]{1,0:T(8,128)(2,1)S(1)}, u32[]{:S(2)}, u32[]{:S(2)}) collective-permute-start(f16[1024,128]{1,0:T(8,128)(2,1)S(1)} %broadcast_select_fusion.32), channel_id=1, source_target_pairs={{4,8},{8,4},{5,9},{9,5},{6,10},{10,6},{7,11},{11,7},{20,24},{24,20... | collective-permute-start | bytes 786440 | tf_op jit(solution)/shard_map/ppermute | solution.py:305
  81.6 1.6 broadcast_select_fusion.29
  83.4 2.9 %collective-permute-start.27 = (f16[1024,128]{1,0:T(8,128)(2,1)S(1)}, f16[1024,128]{1,0:T(8,128)(2,1)S(1)}, u32[]{:S(2)}, u32[]{:S(2)}) collective-permute-start(f16[1024,128]{1,0:T(8,128)(2,1)S(1)} %get-tuple-element.392), channel_id=1, source_target_pairs={{4,8},{8,4},{5,9},{9,5},{6,10},{10,6},{7,11},{11,7},{20,24},{24,20... | collective-permute-start | bytes 786440 | tf_op jit(solution)/shard_map/ppermute | solution.py:305
  88.1 2.2 collective-permute-start.31
  90.3 1.7 collective-permute-done.26
  93.5 3.0 %collective-permute-start.33 = (f16[1024,128]{1,0:T(8,128)(2,1)S(1)}, f16[1024,128]{1,0:T(8,128)(2,1)S(1)}, u32[]{:S(2)}, u32[]{:S(2)}) collective-permute-start(f16[1024,128]{1,0:T(8,128)(2,1)S(1)} %get-tuple-element.378), channel_id=1, source_target_pairs={{4,8},{8,4},{5,9},{9,5},{6,10},{10,6},{7,11},{11,7},{20,24},{24,20... | collective-permute-start | bytes 786440 | tf_op jit(solution)/shard_map/ppermute | solution.py:305
  99.1 3.1 %collective-permute-start.35 = (f16[1024,128]{1,0:T(8,128)(2,1)S(1)}, f16[1024,128]{1,0:T(8,128)(2,1)S(1)}, u32[]{:S(2)}, u32[]{:S(2)}) collective-permute-start(f16[1024,128]{1,0:T(8,128)(2,1)S(1)} %get-tuple-element.382), channel_id=1, source_target_pairs={{4,8},{8,4},{5,9},{9,5},{6,10},{10,6},{7,11},{11,7},{20,24},{24,20... | collective-permute-start | bytes 786440 | tf_op jit(solution)/shard_map/ppermute | solution.py:305
  104.1 3.4 %collective-permute-start.37 = (f16[1024,128]{1,0:T(8,128)(2,1)S(1)}, f16[1024,128]{1,0:T(8,128)(2,1)S(1)}, u32[]{:S(2)}, u32[]{:S(2)}) collective-permute-start(f16[1024,128]{1,0:T(8,128)(2,1)S(1)} %get-tuple-element.384), channel_id=1, source_target_pairs={{4,8},{8,4},{5,9},{9,5},{6,10},{10,6},{7,11},{11,7},{20,24},{24,20... | collective-permute-start | bytes 786440 | tf_op jit(solution)/shard_map/ppermute | solution.py:305
  109.9 2.9 %fusion.1 = bf16[1024,128]{0,1:T(8,128)(2,1)S(1)} fusion(bf16[4096,128]{1,0:T(8,128)(2,1)S(1)} %multiply_convert_fusion.3, bf16[1024,4096]{1,0:T(8,128)(2,1)S(1)} %bitcast.125), kind=kOutput, calls=%fused_computation.21 | convolution fusion | flops 1073872896 | bytes 9699328 | tf_op jit(solution)/shard_map/dot_general | solution.py:413
  112.8 5.5 %collective-permute-start.52 = (bf16[1024,128]{0,1:T(8,128)(2,1)S(1)}, bf16[1024,128]{0,1:T(8,128)(2,1)S(1)}, u32[]{:S(2)}, u32[]{:S(2)}) collective-permute-start(bf16[1024,128]{0,1:T(8,128)(2,1)S(1)} %fusion.1), channel_id=1, source_target_pairs={{0,1},{1,0},{2,3},{3,2},{4,5},{5,4},{6,7},{7,6},{8,9},{9,8},{10,11... | collective-permute-start | bytes 786440 | tf_op jit(solution)/shard_map/ppermute | solution.py:29
  119.1 2.7 %collective-permute-start.39 = (f16[1024,128]{1,0:T(8,128)(2,1)S(1)}, f16[1024,128]{1,0:T(8,128)(2,1)S(1)}, u32[]{:S(2)}, u32[]{:S(2)}) collective-permute-start(f16[1024,128]{1,0:T(8,128)(2,1)S(1)} %get-tuple-element.387), channel_id=1, source_target_pairs={{4,8},{8,4},{5,9},{9,5},{6,10},{10,6},{7,11},{11,7},{20,24},{24,20... | collective-permute-start | bytes 786440 | tf_op jit(solution)/shard_map/ppermute | solution.py:305
  122.5 4.1 %collective-permute-done.38 = f16[1024,128]{1,0:T(8,128)(2,1)S(1)} collective-permute-done((f16[1024,128]{1,0:T(8,128)(2,1)S(1)}, f16[1024,128]{1,0:T(8,128)(2,1)S(1)}, u32[]{:S(2)}, u32[]{:S(2)}) %collective-permute-start.38) | collective-permute-done | bytes 262176 | tf_op jit(solution)/shard_map/ppermute | solution.py:305
  126.7 2.7 %collective-permute-start.41 = (f16[1024,128]{1,0:T(8,128)(2,1)S(1)}, f16[1024,128]{1,0:T(8,128)(2,1)S(1)}, u32[]{:S(2)}, u32[]{:S(2)}) collective-permute-start(f16[1024,128]{1,0:T(8,128)(2,1)S(1)} %get-tuple-element.366), channel_id=1, source_target_pairs={{4,8},{8,4},{5,9},{9,5},{6,10},{10,6},{7,11},{11,7},{20,24},{24,20... | collective-permute-start | bytes 786440 | tf_op jit(solution)/shard_map/ppermute | solution.py:305
  130.1 2.6 %collective-permute-start.43 = (f16[1024,128]{1,0:T(8,128)(2,1)S(1)}, f16[1024,128]{1,0:T(8,128)(2,1)S(1)}, u32[]{:S(2)}, u32[]{:S(2)}) collective-permute-start(f16[1024,128]{1,0:T(8,128)(2,1)S(1)} %get-tuple-element.370), channel_id=1, source_target_pairs={{4,8},{8,4},{5,9},{9,5},{6,10},{10,6},{7,11},{11,7},{20,24},{24,20... | collective-permute-start | bytes 786440 | tf_op jit(solution)/shard_map/ppermute | solution.py:305
  132.7 2.6 %collective-permute-start.58 = (bf16[1024,128]{0,1:T(8,128)(2,1)S(1)}, bf16[1024,128]{0,1:T(8,128)(2,1)S(1)}, u32[]{:S(2)}, u32[]{:S(2)}) collective-permute-start(bf16[1024,128]{0,1:T(8,128)(2,1)S(1)} %collective-permute-done.55), channel_id=1, source_target_pairs={{0,1},{1,0},{2,3},{3,2},{4,5},{5,4},{6,7},{7,6},{8,9},{9,8},{10,11... | collective-permute-start | bytes 786440 | tf_op jit(solution)/shard_map/ppermute | solution.py:29
  136.0 2.7 %collective-permute-start.45 = (f16[1024,128]{1,0:T(8,128)(2,1)S(1)}, f16[1024,128]{1,0:T(8,128)(2,1)S(1)}, u32[]{:S(2)}, u32[]{:S(2)}) collective-permute-start(f16[1024,128]{1,0:T(8,128)(2,1)S(1)} %get-tuple-element.372), channel_id=1, source_target_pairs={{4,8},{8,4},{5,9},{9,5},{6,10},{10,6},{7,11},{11,7},{20,24},{24,20... | collective-permute-start | bytes 786440 | tf_op jit(solution)/shard_map/ppermute | solution.py:305
  138.7 1.5 collective-permute-done.43
  141.3 2.9 %fusion.2 = bf16[1024,128]{0,1:T(8,128)(2,1)S(1)} fusion(bf16[4096,128]{1,0:T(8,128)(2,1)S(1)} %multiply_convert_fusion.2, bf16[1024,4096]{1,0:T(8,128)(2,1)S(1)} %bitcast.125), kind=kOutput, calls=%fused_computation.22 | convolution fusion | flops 1073872896 | bytes 9699328 | tf_op jit(solution)/shard_map/dot_general | solution.py:413
  144.2 4.5 %collective-permute-start.53 = (bf16[1024,128]{0,1:T(8,128)(2,1)S(1)}, bf16[1024,128]{0,1:T(8,128)(2,1)S(1)}, u32[]{:S(2)}, u32[]{:S(2)}) collective-permute-start(bf16[1024,128]{0,1:T(8,128)(2,1)S(1)} %fusion.2), channel_id=1, source_target_pairs={{0,1},{1,0},{2,3},{3,2},{4,5},{5,4},{6,7},{7,6},{8,9},{9,8},{10,11... | collective-permute-start | bytes 786440 | tf_op jit(solution)/shard_map/ppermute | solution.py:29
  149.3 2.3 collective-permute-start.47
  152.4 4.5 %collective-permute-done.46 = f16[1024,128]{1,0:T(8,128)(2,1)S(1)} collective-permute-done((f16[1024,128]{1,0:T(8,128)(2,1)S(1)}, f16[1024,128]{1,0:T(8,128)(2,1)S(1)}, u32[]{:S(2)}, u32[]{:S(2)}) %collective-permute-start.46) | collective-permute-done | bytes 262176 | tf_op jit(solution)/shard_map/ppermute | solution.py:305
  156.8 2.3 collective-permute-start.49
  159.9 2.9 %collective-permute-start.51 = (f16[1024,128]{1,0:T(8,128)(2,1)S(1)}, f16[1024,128]{1,0:T(8,128)(2,1)S(1)}, u32[]{:S(2)}, u32[]{:S(2)}) collective-permute-start(f16[1024,128]{1,0:T(8,128)(2,1)S(1)} %get-tuple-element.358), channel_id=1, source_target_pairs={{4,8},{8,4},{5,9},{9,5},{6,10},{10,6},{7,11},{11,7},{20,24},{24,20... | collective-permute-start | bytes 786440 | tf_op jit(solution)/shard_map/ppermute | solution.py:305
  162.9 2.6 %collective-permute-start.59 = (bf16[1024,128]{0,1:T(8,128)(2,1)S(1)}, bf16[1024,128]{0,1:T(8,128)(2,1)S(1)}, u32[]{:S(2)}, u32[]{:S(2)}) collective-permute-start(bf16[1024,128]{0,1:T(8,128)(2,1)S(1)} %collective-permute-done.56), channel_id=1, source_target_pairs={{0,1},{1,0},{2,3},{3,2},{4,5},{5,4},{6,7},{7,6},{8,9},{9,8},{10,11... | collective-permute-start | bytes 786440 | tf_op jit(solution)/shard_map/ppermute | solution.py:29
  166.1 1.3 collective-permute-start.64
  167.4 2.9 %collective-permute-start.65 = (f16[1024,128]{1,0:T(8,128)(2,1)S(1)}, f16[1024,128]{1,0:T(8,128)(2,1)S(1)}, u32[]{:S(2)}, u32[]{:S(2)}) collective-permute-start(f16[1024,128]{1,0:T(8,128)(2,1)S(1)} %get-tuple-element.360), channel_id=1, source_target_pairs={{4,8},{8,4},{5,9},{9,5},{6,10},{10,6},{7,11},{11,7},{20,24},{24,20... | collective-permute-start | bytes 786440 | tf_op jit(solution)/shard_map/ppermute | solution.py:305
  171.4 2.9 %fusion.3 = bf16[1024,128]{0,1:T(8,128)(2,1)S(1)} fusion(bf16[4096,128]{1,0:T(8,128)(2,1)S(1)} %multiply_convert_fusion.1, bf16[1024,4096]{1,0:T(8,128)(2,1)S(1)} %bitcast.125), kind=kOutput, calls=%fused_computation.23 | convolution fusion | flops 1073872896 | bytes 9699328 | tf_op jit(solution)/shard_map/dot_general | solution.py:413
  174.3 3.8 %collective-permute-start.54 = (bf16[1024,128]{0,1:T(8,128)(2,1)S(1)}, bf16[1024,128]{0,1:T(8,128)(2,1)S(1)}, u32[]{:S(2)}, u32[]{:S(2)}) collective-permute-start(bf16[1024,128]{0,1:T(8,128)(2,1)S(1)} %fusion.3), channel_id=1, source_target_pairs={{0,1},{1,0},{2,3},{3,2},{4,5},{5,4},{6,7},{7,6},{8,9},{9,8},{10,11... | collective-permute-start | bytes 786440 | tf_op jit(solution)/shard_map/ppermute | solution.py:29
  178.1 1.6 collective-permute-start.57
  179.7 1.3 collective-permute-start.66
  181.6 2.5 collective-permute-start.67
  184.7 1.3 collective-permute-start.68
  186.6 4.4 %collective-permute-done.67 = f16[1024,128]{1,0:T(8,128)(2,1)S(1)} collective-permute-done((f16[1024,128]{1,0:T(8,128)(2,1)S(1)}, f16[1024,128]{1,0:T(8,128)(2,1)S(1)}, u32[]{:S(2)}, u32[]{:S(2)}) %collective-permute-start.67) | collective-permute-done | bytes 262176 | tf_op jit(solution)/shard_map/ppermute | solution.py:305
  191.6 1.3 collective-permute-start.69
  198.6 2.9 %convolution_convert_fusion = bf16[128,1024]{1,0:T(8,128)(2,1)S(1)} fusion(bf16[4096,128]{1,0:T(8,128)(2,1)S(1)} %multiply_convert_fusion, bf16[1024,4096]{1,0:T(8,128)(2,1)S(1)} %bitcast.125), kind=kOutput, calls=%fused_computation.13 | convolution fusion | flops 1073872896 | bytes 9699328 | tf_op jit(solution)/shard_map/dot_general | solution.py:413
  202.0 1.9 collective-permute-start.73
  205.5 2.2 collective-permute-start.72
  208.8 2.3 collective-permute-start.70
  212.2 2.9 %collective-permute-done.71 = bf16[384,128]{0,1:T(8,128)(2,1)S(1)} collective-permute-done((bf16[384,128]{0,1:T(8,128)(2,1)S(1)}, bf16[384,128]{0,1:T(8,128)(2,1)S(1)}, u32[]{:S(2)}, u32[]{:S(2)}) %collective-permute-start.71) | collective-permute-done | bytes 98336 | tf_op jit(solution)/shard_map/ppermute | solution.py:404
  215.1 3.2 %collective-permute-start.62 = (bf16[384,384]{0,1:T(8,128)(2,1)S(1)}, bf16[384,384]{0,1:T(8,128)(2,1)S(1)}, u32[]{:S(2)}, u32[]{:S(2)}) collective-permute-start(bf16[384,384]{0,1:T(8,128)(2,1)S(1)} %get-tuple-element.434), channel_id=1, source_target_pairs={{0,8},{4,12},{8,0},{12,4},{1,9},{5,13},{9,1},{13,5},{2,10},{6,14},... | collective-permute-start | bytes 884744 | tf_op jit(solution)/shard_map/ppermute | solution.py:404
  218.4 11.5 %collective-permute-done.70 = bf16[384,128]{0,1:T(8,128)(2,1)S(1)} collective-permute-done((bf16[384,128]{0,1:T(8,128)(2,1)S(1)}, bf16[384,128]{0,1:T(8,128)(2,1)S(1)}, u32[]{:S(2)}, u32[]{:S(2)}) %collective-permute-start.70) | collective-permute-done | bytes 98336 | tf_op jit(solution)/shard_map/ppermute | solution.py:404
  229.9 2.3 collective-permute-start.61
  232.3 1.5 collective-permute-start.75
  237.3 11.0 %collective-permute-done.61 = bf16[384,384]{0,1:T(8,128)(2,1)S(1)} collective-permute-done((bf16[384,384]{0,1:T(8,128)(2,1)S(1)}, bf16[384,384]{0,1:T(8,128)(2,1)S(1)}, u32[]{:S(2)}, u32[]{:S(2)}) %collective-permute-start.61) | collective-permute-done | bytes 294944 | tf_op jit(solution)/shard_map/ppermute | solution.py:404
  248.4 3.7 %collective-permute-done.78 = bf16[128,512]{0,1:T(8,128)(2,1)S(1)} collective-permute-done((bf16[128,512]{0,1:T(8,128)(2,1)S(1)}, bf16[128,512]{0,1:T(8,128)(2,1)S(1)}, u32[]{:S(2)}, u32[]{:S(2)}) %collective-permute-start.78) | collective-permute-done | bytes 131104 | tf_op jit(solution)/shard_map/ppermute | solution.py:404
  252.1 1.8 collective-permute-done.76
  254.1 1.3 copy.16
  (194 shorter events, 51.7 us)
Async XLA Ops:
  5.4 6.6 %collective-permute-start.6 = (bf16[7,128,128]{2,1,0:T(8,128)(2,1)S(1)}, bf16[7,128,128]{2,1,0:T(8,128)(2,1)S(1)}, u32[]{:S(2)}, u32[]{:S(2)}) collective-permute-start(bf16[7,128,128]{2,1,0:T(8,128)(2,1)S(1)} %get-tuple-element.266), channel_id=1, source_target_pairs={{0,4},{4,8},{8,12},{12,0},{1,5},{5,9},{9,13},{13,1},{2,6},{6,10},{... | collective-permute-start | bytes 688136 | tf_op jit(solution)/shard_map/ppermute | solution.py:356
  12.1 13.2 %collective-permute-start.7 = (bf16[7,128,128]{2,1,0:T(8,128)(2,1)S(1)}, bf16[7,128,128]{2,1,0:T(8,128)(2,1)S(1)}, u32[]{:S(2)}, u32[]{:S(2)}) collective-permute-start(bf16[7,128,128]{2,1,0:T(8,128)(2,1)S(1)} %get-tuple-element.269), channel_id=1, source_target_pairs={{0,8},{4,12},{8,0},{12,4},{1,9},{5,13},{9,1},{13,5},{2,10},{6,14},... | collective-permute-start | bytes 688136 | tf_op jit(solution)/shard_map/ppermute | solution.py:359
  14.3 11.0 %collective-permute-start.8 = (bf16[7,128,128]{2,1,0:T(8,128)(2,1)S(1)}, bf16[7,128,128]{2,1,0:T(8,128)(2,1)S(1)}, u32[]{:S(2)}, u32[]{:S(2)}) collective-permute-start(bf16[7,128,128]{2,1,0:T(8,128)(2,1)S(1)} %collective-permute-done.6.refs_0_), channel_id=1, source_target_pairs={{0,2},{1,3},{2,0},{3,1},{4,6},{5,7},{6,4},{7,5},{8,10},{9,11},{10,... | collective-permute-start | bytes 688136 | tf_op jit(solution)/shard_map/ppermute | solution.py:360
  15.6 8.8 %collective-permute-start.9 = (f32[2,128]{1,0:T(2,128)S(1)}, f32[2,128]{1,0:T(2,128)S(1)}, u32[]{:S(2)}, u32[]{:S(2)}) collective-permute-start(f32[2,128]{1,0:T(2,128)S(1)} %broadcast_in_dim.77), channel_id=1, source_target_pairs={{0,4},{4,8},{8,12},{12,0},{1,5},{5,9},{9,13},{13,1},{2,6},{6,10},{... | collective-permute-start | bytes 3080 | tf_op jit(solution)/shard_map/ppermute | solution.py:346
  16.6 7.9 %collective-permute-start.10 = (f32[2,128]{1,0:T(2,128)S(1)}, f32[2,128]{1,0:T(2,128)S(1)}, u32[]{:S(2)}, u32[]{:S(2)}) collective-permute-start(f32[2,128]{1,0:T(2,128)S(1)} %broadcast_in_dim.77), channel_id=1, source_target_pairs={{0,8},{4,12},{8,0},{12,4},{1,9},{5,13},{9,1},{13,5},{2,10},{6,14},... | collective-permute-start | bytes 3080 | tf_op jit(solution)/shard_map/ppermute | solution.py:346
  18.1 7.2 %collective-permute-start.11 = (f32[2,128]{1,0:T(2,128)S(1)}, f32[2,128]{1,0:T(2,128)S(1)}, u32[]{:S(2)}, u32[]{:S(2)}) collective-permute-start(f32[2,128]{1,0:T(2,128)S(1)} %broadcast_in_dim.77), channel_id=1, source_target_pairs={{0,12},{4,0},{8,4},{12,8},{1,13},{5,1},{9,5},{13,9},{2,14},{6,2},{... | collective-permute-start | bytes 3080 | tf_op jit(solution)/shard_map/ppermute | solution.py:346
  25.3 8.0 %collective-permute-start.12 = (bf16[7,128,128]{2,1,0:T(8,128)(2,1)S(1)}, bf16[7,128,128]{2,1,0:T(8,128)(2,1)S(1)}, u32[]{:S(2)}, u32[]{:S(2)}) collective-permute-start(bf16[7,128,128]{2,1,0:T(8,128)(2,1)S(1)} %get-tuple-element.272), channel_id=1, source_target_pairs={{0,12},{4,0},{8,4},{12,8},{1,13},{5,1},{9,5},{13,9},{2,14},{6,2},{... | collective-permute-start | bytes 688136 | tf_op jit(solution)/shard_map/ppermute | solution.py:362
  34.3 9.2 %collective-permute-start.16 = (bf16[7,128,128]{2,1,0:T(8,128)(2,1)S(1)}, bf16[7,128,128]{2,1,0:T(8,128)(2,1)S(1)}, u32[]{:S(2)}, u32[]{:S(2)}) collective-permute-start(bf16[7,128,128]{2,1,0:T(8,128)(2,1)S(1)} %collective-permute-done.7.refs_1_), channel_id=1, source_target_pairs={{0,1},{1,0},{2,3},{3,2},{4,5},{5,4},{6,7},{7,6},{8,9},{9,8},{10,11... | collective-permute-start | bytes 688136 | tf_op jit(solution)/shard_map/ppermute | solution.py:29
  36.3 7.2 %collective-permute-start.19 = (bf16[7,128,128]{2,1,0:T(8,128)(2,1)S(1)}, bf16[7,128,128]{2,1,0:T(8,128)(2,1)S(1)}, u32[]{:S(2)}, u32[]{:S(2)}) collective-permute-start(bf16[7,128,128]{2,1,0:T(8,128)(2,1)S(1)} %collective-permute-done.8.refs_6_), channel_id=1, source_target_pairs={{0,1},{1,0},{2,3},{3,2},{4,5},{5,4},{6,7},{7,6},{8,9},{9,8},{10,11... | collective-permute-start | bytes 688136 | tf_op jit(solution)/shard_map/ppermute | solution.py:29
  36.4 7.1 %collective-permute-start.17 = (bf16[7,128,128]{2,1,0:T(8,128)(2,1)S(1)}, bf16[7,128,128]{2,1,0:T(8,128)(2,1)S(1)}, u32[]{:S(2)}, u32[]{:S(2)}) collective-permute-start(bf16[7,128,128]{2,1,0:T(8,128)(2,1)S(1)} %collective-permute-done.12.refs_2_), channel_id=1, source_target_pairs={{0,1},{1,0},{2,3},{3,2},{4,5},{5,4},{6,7},{7,6},{8,9},{9,8},{10,11... | collective-permute-start | bytes 688136 | tf_op jit(solution)/shard_map/ppermute | solution.py:29
  36.8 6.7 %collective-permute-start.20 = (bf16[7,128,128]{2,1,0:T(8,128)(2,1)S(1)}, bf16[7,128,128]{2,1,0:T(8,128)(2,1)S(1)}, u32[]{:S(2)}, u32[]{:S(2)}) collective-permute-start(bf16[7,128,128]{2,1,0:T(8,128)(2,1)S(1)} %collective-permute-done.13.refs_7_), channel_id=1, source_target_pairs={{0,1},{1,0},{2,3},{3,2},{4,5},{5,4},{6,7},{7,6},{8,9},{9,8},{10,11... | collective-permute-start | bytes 688136 | tf_op jit(solution)/shard_map/ppermute | solution.py:29
  59.8 9.8 %collective-permute-start.22 = (f16[1024,128]{1,0:T(8,128)(2,1)S(1)}, f16[1024,128]{1,0:T(8,128)(2,1)S(1)}, u32[]{:S(2)}, u32[]{:S(2)}) collective-permute-start(f16[1024,128]{1,0:T(8,128)(2,1)S(1)} %get-tuple-element.401), channel_id=1, source_target_pairs={{0,4},{12,8},{1,5},{13,9},{2,6},{14,10},{3,7},{15,11},{16,20},{28,... | collective-permute-start | bytes 786440 | tf_op jit(solution)/shard_map/ppermute | solution.py:305
  61.2 14.3 %collective-permute-start.25 = (f16[1024,128]{1,0:T(8,128)(2,1)S(1)}, f16[1024,128]{1,0:T(8,128)(2,1)S(1)}, u32[]{:S(2)}, u32[]{:S(2)}) collective-permute-start(f16[1024,128]{1,0:T(8,128)(2,1)S(1)} %get-tuple-element.431), channel_id=1, source_target_pairs={{0,4},{12,8},{1,5},{13,9},{2,6},{14,10},{3,7},{15,11},{16,20},{28,... | collective-permute-start | bytes 786440 | tf_op jit(solution)/shard_map/ppermute | solution.py:305
  71.5 9.9 %collective-permute-start.23 = (f16[1024,128]{1,0:T(8,128)(2,1)S(1)}, f16[1024,128]{1,0:T(8,128)(2,1)S(1)}, u32[]{:S(2)}, u32[]{:S(2)}) collective-permute-start(f16[1024,128]{1,0:T(8,128)(2,1)S(1)} %broadcast_select_fusion.36), channel_id=1, source_target_pairs={{0,4},{12,8},{1,5},{13,9},{2,6},{14,10},{3,7},{15,11},{16,20},{28,... | collective-permute-start | bytes 786440 | tf_op jit(solution)/shard_map/ppermute | solution.py:305
  73.1 8.5 %collective-permute-start.24 = (f16[1024,128]{1,0:T(8,128)(2,1)S(1)}, f16[1024,128]{1,0:T(8,128)(2,1)S(1)}, u32[]{:S(2)}, u32[]{:S(2)}) collective-permute-start(f16[1024,128]{1,0:T(8,128)(2,1)S(1)} %get-tuple-element.398), channel_id=1, source_target_pairs={{4,8},{8,4},{5,9},{9,5},{6,10},{10,6},{7,11},{11,7},{20,24},{24,20... | collective-permute-start | bytes 786440 | tf_op jit(solution)/shard_map/ppermute | solution.py:305
  77.2 9.1 %collective-permute-start.28 = (f16[1024,128]{1,0:T(8,128)(2,1)S(1)}, f16[1024,128]{1,0:T(8,128)(2,1)S(1)}, u32[]{:S(2)}, u32[]{:S(2)}) collective-permute-start(f16[1024,128]{1,0:T(8,128)(2,1)S(1)} %get-tuple-element.395), channel_id=1, source_target_pairs={{0,4},{12,8},{1,5},{13,9},{2,6},{14,10},{3,7},{15,11},{16,20},{28,... | collective-permute-start | bytes 786440 | tf_op jit(solution)/shard_map/ppermute | solution.py:305
  78.6 9.0 %collective-permute-start.29 = (f16[1024,128]{1,0:T(8,128)(2,1)S(1)}, f16[1024,128]{1,0:T(8,128)(2,1)S(1)}, u32[]{:S(2)}, u32[]{:S(2)}) collective-permute-start(f16[1024,128]{1,0:T(8,128)(2,1)S(1)} %broadcast_select_fusion.32), channel_id=1, source_target_pairs={{4,8},{8,4},{5,9},{9,5},{6,10},{10,6},{7,11},{11,7},{20,24},{24,20... | collective-permute-start | bytes 786440 | tf_op jit(solution)/shard_map/ppermute | solution.py:305
  83.3 8.6 %collective-permute-start.26 = (f16[1024,128]{1,0:T(8,128)(2,1)S(1)}, f16[1024,128]{1,0:T(8,128)(2,1)S(1)}, u32[]{:S(2)}, u32[]{:S(2)}) collective-permute-start(f16[1024,128]{1,0:T(8,128)(2,1)S(1)} %broadcast_select_fusion.30), channel_id=1, source_target_pairs={{0,4},{4,0},{8,12},{12,8},{1,5},{5,1},{9,13},{13,9},{2,6},{6,2},{1... | collective-permute-start | bytes 786440 | tf_op jit(solution)/shard_map/ppermute | solution.py:305
  83.4 9.3 %collective-permute-start.27 = (f16[1024,128]{1,0:T(8,128)(2,1)S(1)}, f16[1024,128]{1,0:T(8,128)(2,1)S(1)}, u32[]{:S(2)}, u32[]{:S(2)}) collective-permute-start(f16[1024,128]{1,0:T(8,128)(2,1)S(1)} %get-tuple-element.392), channel_id=1, source_target_pairs={{4,8},{8,4},{5,9},{9,5},{6,10},{10,6},{7,11},{11,7},{20,24},{24,20... | collective-permute-start | bytes 786440 | tf_op jit(solution)/shard_map/ppermute | solution.py:305
  88.0 9.5 %collective-permute-start.30 = (f16[1024,128]{1,0:T(8,128)(2,1)S(1)}, f16[1024,128]{1,0:T(8,128)(2,1)S(1)}, u32[]{:S(2)}, u32[]{:S(2)}) collective-permute-start(f16[1024,128]{1,0:T(8,128)(2,1)S(1)} %broadcast_select_fusion.27), channel_id=1, source_target_pairs={{0,4},{4,0},{8,12},{12,8},{1,5},{5,1},{9,13},{13,9},{2,6},{6,2},{1... | collective-permute-start | bytes 786440 | tf_op jit(solution)/shard_map/ppermute | solution.py:305
  88.1 10.3 %collective-permute-start.31 = (f16[1024,128]{1,0:T(8,128)(2,1)S(1)}, f16[1024,128]{1,0:T(8,128)(2,1)S(1)}, u32[]{:S(2)}, u32[]{:S(2)}) collective-permute-start(f16[1024,128]{1,0:T(8,128)(2,1)S(1)} %get-tuple-element.389), channel_id=1, source_target_pairs={{4,8},{8,4},{5,9},{9,5},{6,10},{10,6},{7,11},{11,7},{20,24},{24,20... | collective-permute-start | bytes 786440 | tf_op jit(solution)/shard_map/ppermute | solution.py:305
  93.4 9.3 %collective-permute-start.32 = (f16[1024,128]{1,0:T(8,128)(2,1)S(1)}, f16[1024,128]{1,0:T(8,128)(2,1)S(1)}, u32[]{:S(2)}, u32[]{:S(2)}) collective-permute-start(f16[1024,128]{1,0:T(8,128)(2,1)S(1)} %get-tuple-element.379), channel_id=1, source_target_pairs={{0,4},{4,0},{8,12},{12,8},{1,5},{5,1},{9,13},{13,9},{2,6},{6,2},{1... | collective-permute-start | bytes 786440 | tf_op jit(solution)/shard_map/ppermute | solution.py:305
  93.5 9.9 %collective-permute-start.33 = (f16[1024,128]{1,0:T(8,128)(2,1)S(1)}, f16[1024,128]{1,0:T(8,128)(2,1)S(1)}, u32[]{:S(2)}, u32[]{:S(2)}) collective-permute-start(f16[1024,128]{1,0:T(8,128)(2,1)S(1)} %get-tuple-element.378), channel_id=1, source_target_pairs={{4,8},{8,4},{5,9},{9,5},{6,10},{10,6},{7,11},{11,7},{20,24},{24,20... | collective-permute-start | bytes 786440 | tf_op jit(solution)/shard_map/ppermute | solution.py:305
  99.0 9.3 %collective-permute-start.34 = (f16[1024,128]{1,0:T(8,128)(2,1)S(1)}, f16[1024,128]{1,0:T(8,128)(2,1)S(1)}, u32[]{:S(2)}, u32[]{:S(2)}) collective-permute-start(f16[1024,128]{1,0:T(8,128)(2,1)S(1)} %get-tuple-element.381), channel_id=1, source_target_pairs={{0,4},{4,0},{8,12},{12,8},{1,5},{5,1},{9,13},{13,9},{2,6},{6,2},{1... | collective-permute-start | bytes 786440 | tf_op jit(solution)/shard_map/ppermute | solution.py:305
  99.1 9.8 %collective-permute-start.35 = (f16[1024,128]{1,0:T(8,128)(2,1)S(1)}, f16[1024,128]{1,0:T(8,128)(2,1)S(1)}, u32[]{:S(2)}, u32[]{:S(2)}) collective-permute-start(f16[1024,128]{1,0:T(8,128)(2,1)S(1)} %get-tuple-element.382), channel_id=1, source_target_pairs={{4,8},{8,4},{5,9},{9,5},{6,10},{10,6},{7,11},{11,7},{20,24},{24,20... | collective-permute-start | bytes 786440 | tf_op jit(solution)/shard_map/ppermute | solution.py:305
  104.0 15.1 %collective-permute-start.36 = (f16[1024,128]{1,0:T(8,128)(2,1)S(1)}, f16[1024,128]{1,0:T(8,128)(2,1)S(1)}, u32[]{:S(2)}, u32[]{:S(2)}) collective-permute-start(f16[1024,128]{1,0:T(8,128)(2,1)S(1)} %get-tuple-element.385), channel_id=1, source_target_pairs={{0,4},{4,0},{8,12},{12,8},{1,5},{5,1},{9,13},{13,9},{2,6},{6,2},{1... | collective-permute-start | bytes 786440 | tf_op jit(solution)/shard_map/ppermute | solution.py:305
  104.1 17.7 %collective-permute-start.37 = (f16[1024,128]{1,0:T(8,128)(2,1)S(1)}, f16[1024,128]{1,0:T(8,128)(2,1)S(1)}, u32[]{:S(2)}, u32[]{:S(2)}) collective-permute-start(f16[1024,128]{1,0:T(8,128)(2,1)S(1)} %get-tuple-element.384), channel_id=1, source_target_pairs={{4,8},{8,4},{5,9},{9,5},{6,10},{10,6},{7,11},{11,7},{20,24},{24,20... | collective-permute-start | bytes 786440 | tf_op jit(solution)/shard_map/ppermute | solution.py:305
  112.8 19.9 %collective-permute-start.52 = (bf16[1024,128]{0,1:T(8,128)(2,1)S(1)}, bf16[1024,128]{0,1:T(8,128)(2,1)S(1)}, u32[]{:S(2)}, u32[]{:S(2)}) collective-permute-start(bf16[1024,128]{0,1:T(8,128)(2,1)S(1)} %fusion.1), channel_id=1, source_target_pairs={{0,1},{1,0},{2,3},{3,2},{4,5},{5,4},{6,7},{7,6},{8,9},{9,8},{10,11... | collective-permute-start | bytes 786440 | tf_op jit(solution)/shard_map/ppermute | solution.py:29
  118.3 11.8 %collective-permute-start.55 = (bf16[1024,128]{0,1:T(8,128)(2,1)S(1)}, bf16[1024,128]{0,1:T(8,128)(2,1)S(1)}, u32[]{:S(2)}, u32[]{:S(2)}) collective-permute-start(bf16[1024,128]{0,1:T(8,128)(2,1)S(1)} %fusion.1), channel_id=1, source_target_pairs={{0,2},{1,3},{2,0},{3,1},{4,6},{5,7},{6,4},{7,5},{8,10},{9,11},{10,... | collective-permute-start | bytes 786440 | tf_op jit(solution)/shard_map/ppermute | solution.py:29
  119.1 7.5 %collective-permute-start.38 = (f16[1024,128]{1,0:T(8,128)(2,1)S(1)}, f16[1024,128]{1,0:T(8,128)(2,1)S(1)}, u32[]{:S(2)}, u32[]{:S(2)}) collective-permute-start(f16[1024,128]{1,0:T(8,128)(2,1)S(1)} %get-tuple-element.388), channel_id=1, source_target_pairs={{0,4},{4,0},{8,12},{12,8},{1,5},{5,1},{9,13},{13,9},{2,6},{6,2},{1... | collective-permute-start | bytes 786440 | tf_op jit(solution)/shard_map/ppermute | solution.py:305
  119.1 10.2 %collective-permute-start.39 = (f16[1024,128]{1,0:T(8,128)(2,1)S(1)}, f16[1024,128]{1,0:T(8,128)(2,1)S(1)}, u32[]{:S(2)}, u32[]{:S(2)}) collective-permute-start(f16[1024,128]{1,0:T(8,128)(2,1)S(1)} %get-tuple-element.387), channel_id=1, source_target_pairs={{4,8},{8,4},{5,9},{9,5},{6,10},{10,6},{7,11},{11,7},{20,24},{24,20... | collective-permute-start | bytes 786440 | tf_op jit(solution)/shard_map/ppermute | solution.py:305
  122.4 12.9 %collective-permute-start.40 = (f16[1024,128]{1,0:T(8,128)(2,1)S(1)}, f16[1024,128]{1,0:T(8,128)(2,1)S(1)}, u32[]{:S(2)}, u32[]{:S(2)}) collective-permute-start(f16[1024,128]{1,0:T(8,128)(2,1)S(1)} %get-tuple-element.367), channel_id=1, source_target_pairs={{0,4},{4,0},{8,12},{12,8},{1,5},{5,1},{9,13},{13,9},{2,6},{6,2},{1... | collective-permute-start | bytes 786440 | tf_op jit(solution)/shard_map/ppermute | solution.py:305
  126.7 8.7 %collective-permute-start.41 = (f16[1024,128]{1,0:T(8,128)(2,1)S(1)}, f16[1024,128]{1,0:T(8,128)(2,1)S(1)}, u32[]{:S(2)}, u32[]{:S(2)}) collective-permute-start(f16[1024,128]{1,0:T(8,128)(2,1)S(1)} %get-tuple-element.366), channel_id=1, source_target_pairs={{4,8},{8,4},{5,9},{9,5},{6,10},{10,6},{7,11},{11,7},{20,24},{24,20... | collective-permute-start | bytes 786440 | tf_op jit(solution)/shard_map/ppermute | solution.py:305
  130.0 8.8 %collective-permute-start.42 = (f16[1024,128]{1,0:T(8,128)(2,1)S(1)}, f16[1024,128]{1,0:T(8,128)(2,1)S(1)}, u32[]{:S(2)}, u32[]{:S(2)}) collective-permute-start(f16[1024,128]{1,0:T(8,128)(2,1)S(1)} %get-tuple-element.369), channel_id=1, source_target_pairs={{0,4},{4,0},{8,12},{12,8},{1,5},{5,1},{9,13},{13,9},{2,6},{6,2},{1... | collective-permute-start | bytes 786440 | tf_op jit(solution)/shard_map/ppermute | solution.py:305
  130.1 10.2 %collective-permute-start.43 = (f16[1024,128]{1,0:T(8,128)(2,1)S(1)}, f16[1024,128]{1,0:T(8,128)(2,1)S(1)}, u32[]{:S(2)}, u32[]{:S(2)}) collective-permute-start(f16[1024,128]{1,0:T(8,128)(2,1)S(1)} %get-tuple-element.370), channel_id=1, source_target_pairs={{4,8},{8,4},{5,9},{9,5},{6,10},{10,6},{7,11},{11,7},{20,24},{24,20... | collective-permute-start | bytes 786440 | tf_op jit(solution)/shard_map/ppermute | solution.py:305
  132.7 16.5 %collective-permute-start.58 = (bf16[1024,128]{0,1:T(8,128)(2,1)S(1)}, bf16[1024,128]{0,1:T(8,128)(2,1)S(1)}, u32[]{:S(2)}, u32[]{:S(2)}) collective-permute-start(bf16[1024,128]{0,1:T(8,128)(2,1)S(1)} %collective-permute-done.55), channel_id=1, source_target_pairs={{0,1},{1,0},{2,3},{3,2},{4,5},{5,4},{6,7},{7,6},{8,9},{9,8},{10,11... | collective-permute-start | bytes 786440 | tf_op jit(solution)/shard_map/ppermute | solution.py:29
  136.0 13.3 %collective-permute-start.44 = (f16[1024,128]{1,0:T(8,128)(2,1)S(1)}, f16[1024,128]{1,0:T(8,128)(2,1)S(1)}, u32[]{:S(2)}, u32[]{:S(2)}) collective-permute-start(f16[1024,128]{1,0:T(8,128)(2,1)S(1)} %get-tuple-element.373), channel_id=1, source_target_pairs={{0,4},{4,0},{8,12},{12,8},{1,5},{5,1},{9,13},{13,9},{2,6},{6,2},{1... | collective-permute-start | bytes 786440 | tf_op jit(solution)/shard_map/ppermute | solution.py:305
  136.0 15.6 %collective-permute-start.45 = (f16[1024,128]{1,0:T(8,128)(2,1)S(1)}, f16[1024,128]{1,0:T(8,128)(2,1)S(1)}, u32[]{:S(2)}, u32[]{:S(2)}) collective-permute-start(f16[1024,128]{1,0:T(8,128)(2,1)S(1)} %get-tuple-element.372), channel_id=1, source_target_pairs={{4,8},{8,4},{5,9},{9,5},{6,10},{10,6},{7,11},{11,7},{20,24},{24,20... | collective-permute-start | bytes 786440 | tf_op jit(solution)/shard_map/ppermute | solution.py:305
  144.2 18.7 %collective-permute-start.53 = (bf16[1024,128]{0,1:T(8,128)(2,1)S(1)}, bf16[1024,128]{0,1:T(8,128)(2,1)S(1)}, u32[]{:S(2)}, u32[]{:S(2)}) collective-permute-start(bf16[1024,128]{0,1:T(8,128)(2,1)S(1)} %fusion.2), channel_id=1, source_target_pairs={{0,1},{1,0},{2,3},{3,2},{4,5},{5,4},{6,7},{7,6},{8,9},{9,8},{10,11... | collective-permute-start | bytes 786440 | tf_op jit(solution)/shard_map/ppermute | solution.py:29
  148.6 11.2 %collective-permute-start.56 = (bf16[1024,128]{0,1:T(8,128)(2,1)S(1)}, bf16[1024,128]{0,1:T(8,128)(2,1)S(1)}, u32[]{:S(2)}, u32[]{:S(2)}) collective-permute-start(bf16[1024,128]{0,1:T(8,128)(2,1)S(1)} %fusion.2), channel_id=1, source_target_pairs={{0,2},{1,3},{2,0},{3,1},{4,6},{5,7},{6,4},{7,5},{8,10},{9,11},{10,... | collective-permute-start | bytes 786440 | tf_op jit(solution)/shard_map/ppermute | solution.py:29
  149.3 7.5 %collective-permute-start.46 = (f16[1024,128]{1,0:T(8,128)(2,1)S(1)}, f16[1024,128]{1,0:T(8,128)(2,1)S(1)}, u32[]{:S(2)}, u32[]{:S(2)}) collective-permute-start(f16[1024,128]{1,0:T(8,128)(2,1)S(1)} %get-tuple-element.376), channel_id=1, source_target_pairs={{0,4},{4,0},{8,12},{12,8},{1,5},{5,1},{9,13},{13,9},{2,6},{6,2},{1... | collective-permute-start | bytes 786440 | tf_op jit(solution)/shard_map/ppermute | solution.py:305
  149.3 9.8 %collective-permute-start.47 = (f16[1024,128]{1,0:T(8,128)(2,1)S(1)}, f16[1024,128]{1,0:T(8,128)(2,1)S(1)}, u32[]{:S(2)}, u32[]{:S(2)}) collective-permute-start(f16[1024,128]{1,0:T(8,128)(2,1)S(1)} %get-tuple-element.375), channel_id=1, source_target_pairs={{4,8},{8,4},{5,9},{9,5},{6,10},{10,6},{7,11},{11,7},{20,24},{24,20... | collective-permute-start | bytes 786440 | tf_op jit(solution)/shard_map/ppermute | solution.py:305
  152.3 13.2 %collective-permute-start.48 = (f16[1024,128]{1,0:T(8,128)(2,1)S(1)}, f16[1024,128]{1,0:T(8,128)(2,1)S(1)}, u32[]{:S(2)}, u32[]{:S(2)}) collective-permute-start(f16[1024,128]{1,0:T(8,128)(2,1)S(1)} %get-tuple-element.355), channel_id=1, source_target_pairs={{0,4},{4,0},{8,12},{12,8},{1,5},{5,1},{9,13},{13,9},{2,6},{6,2},{1... | collective-permute-start | bytes 786440 | tf_op jit(solution)/shard_map/ppermute | solution.py:305
  156.8 8.7 %collective-permute-start.49 = (f16[1024,128]{1,0:T(8,128)(2,1)S(1)}, f16[1024,128]{1,0:T(8,128)(2,1)S(1)}, u32[]{:S(2)}, u32[]{:S(2)}) collective-permute-start(f16[1024,128]{1,0:T(8,128)(2,1)S(1)} %get-tuple-element.354), channel_id=1, source_target_pairs={{4,8},{8,4},{5,9},{9,5},{6,10},{10,6},{7,11},{11,7},{20,24},{24,20... | collective-permute-start | bytes 786440 | tf_op jit(solution)/shard_map/ppermute | solution.py:305
  159.8 10.6 %collective-permute-start.50 = (f16[1024,128]{1,0:T(8,128)(2,1)S(1)}, f16[1024,128]{1,0:T(8,128)(2,1)S(1)}, u32[]{:S(2)}, u32[]{:S(2)}) collective-permute-start(f16[1024,128]{1,0:T(8,128)(2,1)S(1)} %get-tuple-element.357), channel_id=1, source_target_pairs={{0,4},{4,0},{8,12},{12,8},{1,5},{5,1},{9,13},{13,9},{2,6},{6,2},{1... | collective-permute-start | bytes 786440 | tf_op jit(solution)/shard_map/ppermute | solution.py:305
  159.9 10.5 %collective-permute-start.51 = (f16[1024,128]{1,0:T(8,128)(2,1)S(1)}, f16[1024,128]{1,0:T(8,128)(2,1)S(1)}, u32[]{:S(2)}, u32[]{:S(2)}) collective-permute-start(f16[1024,128]{1,0:T(8,128)(2,1)S(1)} %get-tuple-element.358), channel_id=1, source_target_pairs={{4,8},{8,4},{5,9},{9,5},{6,10},{10,6},{7,11},{11,7},{20,24},{24,20... | collective-permute-start | bytes 786440 | tf_op jit(solution)/shard_map/ppermute | solution.py:305
  162.9 16.8 %collective-permute-start.59 = (bf16[1024,128]{0,1:T(8,128)(2,1)S(1)}, bf16[1024,128]{0,1:T(8,128)(2,1)S(1)}, u32[]{:S(2)}, u32[]{:S(2)}) collective-permute-start(bf16[1024,128]{0,1:T(8,128)(2,1)S(1)} %collective-permute-done.56), channel_id=1, source_target_pairs={{0,1},{1,0},{2,3},{3,2},{4,5},{5,4},{6,7},{7,6},{8,9},{9,8},{10,11... | collective-permute-start | bytes 786440 | tf_op jit(solution)/shard_map/ppermute | solution.py:29
  166.1 15.5 %collective-permute-start.64 = (f16[1024,128]{1,0:T(8,128)(2,1)S(1)}, f16[1024,128]{1,0:T(8,128)(2,1)S(1)}, u32[]{:S(2)}, u32[]{:S(2)}) collective-permute-start(f16[1024,128]{1,0:T(8,128)(2,1)S(1)} %get-tuple-element.361), channel_id=1, source_target_pairs={{4,0},{8,12},{5,1},{9,13},{6,2},{10,14},{7,3},{11,15},{20,16},{24,... | collective-permute-start | bytes 786440 | tf_op jit(solution)/shard_map/ppermute | solution.py:305
  167.4 16.7 %collective-permute-start.65 = (f16[1024,128]{1,0:T(8,128)(2,1)S(1)}, f16[1024,128]{1,0:T(8,128)(2,1)S(1)}, u32[]{:S(2)}, u32[]{:S(2)}) collective-permute-start(f16[1024,128]{1,0:T(8,128)(2,1)S(1)} %get-tuple-element.360), channel_id=1, source_target_pairs={{4,8},{8,4},{5,9},{9,5},{6,10},{10,6},{7,11},{11,7},{20,24},{24,20... | collective-permute-start | bytes 786440 | tf_op jit(solution)/shard_map/ppermute | solution.py:305
  174.3 18.6 %collective-permute-start.54 = (bf16[1024,128]{0,1:T(8,128)(2,1)S(1)}, bf16[1024,128]{0,1:T(8,128)(2,1)S(1)}, u32[]{:S(2)}, u32[]{:S(2)}) collective-permute-start(bf16[1024,128]{0,1:T(8,128)(2,1)S(1)} %fusion.3), channel_id=1, source_target_pairs={{0,1},{1,0},{2,3},{3,2},{4,5},{5,4},{6,7},{7,6},{8,9},{9,8},{10,11... | collective-permute-start | bytes 786440 | tf_op jit(solution)/shard_map/ppermute | solution.py:29
  178.1 15.5 %collective-permute-start.57 = (bf16[1024,128]{0,1:T(8,128)(2,1)S(1)}, bf16[1024,128]{0,1:T(8,128)(2,1)S(1)}, u32[]{:S(2)}, u32[]{:S(2)}) collective-permute-start(bf16[1024,128]{0,1:T(8,128)(2,1)S(1)} %fusion.3), channel_id=1, source_target_pairs={{0,2},{1,3},{2,0},{3,1},{4,6},{5,7},{6,4},{7,5},{8,10},{9,11},{10,... | collective-permute-start | bytes 786440 | tf_op jit(solution)/shard_map/ppermute | solution.py:29
  179.7 6.9 %collective-permute-start.66 = (f16[1024,128]{1,0:T(8,128)(2,1)S(1)}, f16[1024,128]{1,0:T(8,128)(2,1)S(1)}, u32[]{:S(2)}, u32[]{:S(2)}) collective-permute-start(f16[1024,128]{1,0:T(8,128)(2,1)S(1)} %get-tuple-element.364), channel_id=1, source_target_pairs={{4,0},{8,12},{5,1},{9,13},{6,2},{10,14},{7,3},{11,15},{20,16},{24,... | collective-permute-start | bytes 786440 | tf_op jit(solution)/shard_map/ppermute | solution.py:305
  181.6 9.4 %collective-permute-start.67 = (f16[1024,128]{1,0:T(8,128)(2,1)S(1)}, f16[1024,128]{1,0:T(8,128)(2,1)S(1)}, u32[]{:S(2)}, u32[]{:S(2)}) collective-permute-start(f16[1024,128]{1,0:T(8,128)(2,1)S(1)} %get-tuple-element.363), channel_id=1, source_target_pairs={{4,8},{8,4},{5,9},{9,5},{6,10},{10,6},{7,11},{11,7},{20,24},{24,20... | collective-permute-start | bytes 786440 | tf_op jit(solution)/shard_map/ppermute | solution.py:305
  184.7 11.9 %collective-permute-start.68 = (f16[1024,128]{1,0:T(8,128)(2,1)S(1)}, f16[1024,128]{1,0:T(8,128)(2,1)S(1)}, u32[]{:S(2)}, u32[]{:S(2)}) collective-permute-start(f16[1024,128]{1,0:T(8,128)(2,1)S(1)} %get-tuple-element.346), channel_id=1, source_target_pairs={{4,0},{8,12},{5,1},{9,13},{6,2},{10,14},{7,3},{11,15},{20,16},{24,... | collective-permute-start | bytes 786440 | tf_op jit(solution)/shard_map/ppermute | solution.py:305
  201.5 30.8 %collective-permute-start.74 = (bf16[1024,128]{0,1:T(8,128)(2,1)S(1)}, bf16[1024,128]{0,1:T(8,128)(2,1)S(1)}, u32[]{:S(2)}, u32[]{:S(2)}) collective-permute-start(bf16[1024,128]{0,1:T(8,128)(2,1)S(1)} %bitcast.146), channel_id=1, source_target_pairs={{0,2},{1,3},{2,0},{3,1},{4,6},{5,7},{6,4},{7,5},{8,10},{9,11},{10,... | collective-permute-start | bytes 786440 | tf_op jit(solution)/shard_map/ppermute | solution.py:29
  202.0 32.2 %collective-permute-start.73 = (bf16[1024,128]{0,1:T(8,128)(2,1)S(1)}, bf16[1024,128]{0,1:T(8,128)(2,1)S(1)}, u32[]{:S(2)}, u32[]{:S(2)}) collective-permute-start(bf16[1024,128]{0,1:T(8,128)(2,1)S(1)} %bitcast.147), channel_id=1, source_target_pairs={{0,1},{1,0},{2,3},{3,2},{4,5},{5,4},{6,7},{7,6},{8,9},{9,8},{10,11... | collective-permute-start | bytes 786440 | tf_op jit(solution)/shard_map/ppermute | solution.py:29
  207.7 7.4 %collective-permute-start.71 = (bf16[384,128]{0,1:T(8,128)(2,1)S(1)}, bf16[384,128]{0,1:T(8,128)(2,1)S(1)}, u32[]{:S(2)}, u32[]{:S(2)}) collective-permute-start(bf16[384,128]{0,1:T(8,128)(2,1)S(1)} %get-tuple-element.450), channel_id=1, source_target_pairs={{0,8},{4,12},{8,0},{12,4},{1,9},{5,13},{9,1},{13,5},{2,10},{6,14},... | collective-permute-start | bytes 294920 | tf_op jit(solution)/shard_map/ppermute | solution.py:404
  208.8 21.1 %collective-permute-start.70 = (bf16[384,128]{0,1:T(8,128)(2,1)S(1)}, bf16[384,128]{0,1:T(8,128)(2,1)S(1)}, u32[]{:S(2)}, u32[]{:S(2)}) collective-permute-start(bf16[384,128]{0,1:T(8,128)(2,1)S(1)} %get-tuple-element.448), channel_id=1, source_target_pairs={{0,4},{4,8},{8,12},{12,0},{1,5},{5,9},{9,13},{13,1},{2,6},{6,10},{... | collective-permute-start | bytes 294920 | tf_op jit(solution)/shard_map/ppermute | solution.py:404
  211.5 25.8 %collective-permute-start.63 = (bf16[384,384]{0,1:T(8,128)(2,1)S(1)}, bf16[384,384]{0,1:T(8,128)(2,1)S(1)}, u32[]{:S(2)}, u32[]{:S(2)}) collective-permute-start(bf16[384,384]{0,1:T(8,128)(2,1)S(1)} %get-tuple-element.433), channel_id=1, source_target_pairs={{0,12},{4,0},{8,4},{12,8},{1,13},{5,1},{9,5},{13,9},{2,14},{6,2},{... | collective-permute-start | bytes 884744 | tf_op jit(solution)/shard_map/ppermute | solution.py:404
  215.1 22.2 %collective-permute-start.62 = (bf16[384,384]{0,1:T(8,128)(2,1)S(1)}, bf16[384,384]{0,1:T(8,128)(2,1)S(1)}, u32[]{:S(2)}, u32[]{:S(2)}) collective-permute-start(bf16[384,384]{0,1:T(8,128)(2,1)S(1)} %get-tuple-element.434), channel_id=1, source_target_pairs={{0,8},{4,12},{8,0},{12,4},{1,9},{5,13},{9,1},{13,5},{2,10},{6,14},... | collective-permute-start | bytes 884744 | tf_op jit(solution)/shard_map/ppermute | solution.py:404
  229.9 18.4 %collective-permute-start.61 = (bf16[384,384]{0,1:T(8,128)(2,1)S(1)}, bf16[384,384]{0,1:T(8,128)(2,1)S(1)}, u32[]{:S(2)}, u32[]{:S(2)}) collective-permute-start(bf16[384,384]{0,1:T(8,128)(2,1)S(1)} %get-tuple-element.435), channel_id=1, source_target_pairs={{0,4},{4,8},{8,12},{12,0},{1,5},{5,9},{9,13},{13,1},{2,6},{6,10},{... | collective-permute-start | bytes 884744 | tf_op jit(solution)/shard_map/ppermute | solution.py:404
  235.5 16.6 %collective-permute-start.78 = (bf16[128,512]{0,1:T(8,128)(2,1)S(1)}, bf16[128,512]{0,1:T(8,128)(2,1)S(1)}, u32[]{:S(2)}, u32[]{:S(2)}) collective-permute-start(bf16[128,512]{0,1:T(8,128)(2,1)S(1)} %get-tuple-element.440), channel_id=1, source_target_pairs={{0,12},{4,0},{8,4},{12,8},{1,13},{5,1},{9,5},{13,9},{2,14},{6,2},{... | collective-permute-start | bytes 393224 | tf_op jit(solution)/shard_map/ppermute | solution.py:404
  235.6 16.5 %collective-permute-start.77 = (bf16[128,512]{0,1:T(8,128)(2,1)S(1)}, bf16[128,512]{0,1:T(8,128)(2,1)S(1)}, u32[]{:S(2)}, u32[]{:S(2)}) collective-permute-start(bf16[128,512]{0,1:T(8,128)(2,1)S(1)} %get-tuple-element.441), channel_id=1, source_target_pairs={{0,8},{4,12},{8,0},{12,4},{1,9},{5,13},{9,1},{13,5},{2,10},{6,14},... | collective-permute-start | bytes 393224 | tf_op jit(solution)/shard_map/ppermute | solution.py:404
  237.3 16.6 %collective-permute-start.76 = (bf16[128,512]{0,1:T(8,128)(2,1)S(1)}, bf16[128,512]{0,1:T(8,128)(2,1)S(1)}, u32[]{:S(2)}, u32[]{:S(2)}) collective-permute-start(bf16[128,512]{0,1:T(8,128)(2,1)S(1)} %get-tuple-element.439), channel_id=1, source_target_pairs={{0,4},{4,8},{8,12},{12,0},{1,5},{5,9},{9,13},{13,1},{2,6},{6,10},{... | collective-permute-start | bytes 393224 | tf_op jit(solution)/shard_map/ppermute | solution.py:404
  (17 other events, 99.8 us)
where the time goes:
time: 258 us; the launch traced here: 255 us
  starting transfers between devices  114 us (44%)
  waiting for transfers between devices  74.2 us (29%)
  other arithmetic  21.4 us (8%)
  Pallas kernels  17.4 us (7%)
  matrix products  17.1 us (7%)
  between operations  6.58 us (3%)
  local copies, waits for them, and re-layouts  5.08 us (2%)
    ppermute x36, starting transfers between devices, all_planes(): lax.ppermute(p, 'aux', pairs)  54.9 us
    ppermute x18, starting transfers between devices, over_members(): lax.ppermute(a, axis, flipped(size, bit))  34.1 us
    ppermute x9, waiting for transfers between devices, scatter(): lax.ppermute(t, 'aux', rotation(planes, by))  31.7 us
    ppermute x36, waiting for transfers between devices, all_planes(): lax.ppermute(p, 'aux', pairs)  31.2 us
    pallas_call x1, Pallas kernels, spread(): pl.pallas_call(functools.partial(spread_kernel, planes, across, cap), out...  13.5 us
    ppermute x9, starting transfers between devices, scatter(): lax.ppermute(t, 'aux', rotation(planes, by))  12.8 us
    dot_general x4, matrix products, consume(): jnp.dot(fit_rows, rounded, preferred_element_type=jnp.float32)  11.5 us
    select_n x9, other arithmetic, payloads(): return (jnp.where(even, right, left), jnp.where(even, left, right))  7.76 us
  transfers between devices with their start and end apart: 73, of which 29 were waited for; matrix products, arithmetic and copies ran while one was open for 13% of the time, Pallas kernels for 2%

commit v1 on v0

--- a/solution.py
+++ b/solution.py
@@ -276,9 +276,9 @@
         left = payload(s, mirrored, left_before, right_paid)
         return jnp.where(even, right, left), jnp.where(even, left, right)
 
-    def finished(group):
+    def finished(first, last):
         pieces = []
-        for k in range(group * per_group, (group + 1) * per_group):
+        for k in range(first * per_group, last * per_group):
             chunk = None
             for r in range(half, planes):
                 over_even, over_odd = paid[k + LAG * r]
@@ -286,9 +286,11 @@
                 chunk = this if chunk is None else jnp.where(far == r, this, chunk)
             pieces.append(chunk)
         whole = jnp.concatenate(pieces, axis=0).astype(jnp.float32)
-        return lax.optimization_barrier((whole * (1.0 / scale)).astype(jnp.bfloat16))
-
-    waiting = []
+        whole = (whole * (1.0 / scale)).astype(jnp.bfloat16)
+        whole = [whole[g * rows : (g + 1) * rows] for g in range(last - first)]
+        return lax.optimization_barrier(jnp.concatenate(whole, axis=1))
+
+    waiting, taken = [], 0
     for s in range(total_steps):
         if s - LAG in got:
             got[s - LAG], *_ = lax.optimization_barrier((got[s - LAG], paid[s - 1], *waiting))
@@ -305,8 +307,10 @@
                 lax.ppermute(p, "aux", pairs) if pairs else jnp.zeros_like(p) for p, pairs in zip(paid[s], links)
             )
         group, rest = divmod(s - LAG * hops + 1, per_group)
-        if group > 0 and rest == 0:
-            waiting.append(consume(group - 1, finished(group - 1)))
+        if rest == 0 and group > max(0, groups - 3):
+            whole = finished(taken, group)
+            waiting.append(consume(group == groups, whole))
+            taken = group
         waiting += at_step(total_steps - s)
 
 
@@ -388,7 +392,7 @@
     partial = partial.reshape(-1, LANES)
     column_groups = width // LANES
     fitted, wide = [], []
-    square = planes == across
+    square = planes == across == 4
     blocks = {}
 
     def product(left, right):
@@ -400,14 +404,16 @@
         def to(plane):
             return lax.dynamic_index_in_dim(stacked, plane ^ member, 0, keepdims=False)
 
-        sent = [to((position + by) % planes).astype(jnp.bfloat16) for by in range(1, planes)]
-        return [to(position)] + [lax.ppermute(t, "aux", rotation(planes, by)) for by, t in enumerate(sent, 1)], sent
+        neighbour = position ^ 1
+        sent = jnp.stack([to(neighbour), to(planes - 1 - neighbour)]).astype(jnp.bfloat16)
+        near = lax.ppermute(sent, "aux", flipped(planes, 1))
+        far = (to(planes - 1 - position) + near[1].astype(jnp.float32)).astype(jnp.bfloat16)
+        return [to(position), near[0], lax.ppermute(far, "aux", flipped(planes, planes - 1))], sent
 
     def total(terms):
         return sum((t.astype(jnp.float32) for t in terms[1:]), terms[0])
 
-    def consume(g, rounded):
-        last = g == column_groups - 1
+    def consume(last, rounded):
         if square and last:
             rounded, _ = lax.optimization_barrier((rounded, blocks["corner_sent"]))
         own = jnp.dot(fit_rows, rounded, preferred_element_type=jnp.float32).astype(jnp.bfloat16)
@@ -416,7 +422,7 @@
         fitted.append(own)
         if square:
             wide.append(over_members(own, "orb", across))
-        if square and g == column_groups - 2:
+        if square and not last and len(fitted) == 2:
             blocks["early"] = [jnp.concatenate([w[e] for w in wide], axis=1) for e in range(across)]
             inner = jnp.concatenate(fitted, axis=1)
             blocks["terms"] = [product(w, inner) for w in blocks["early"]]

time: 258 us -> 247 us (0.957)
  starting transfers between devices: 114 us -> 102 us
  waiting for transfers between devices: 74.2 us -> 77.8 us
  matrix products: 17.1 us -> 13.8 us
    ppermute x18 -> x15, starting transfers between devices: 34.1 us -> 24.4 us  [over_members(): lax.ppermute(a, axis, flipped(size, bit))]
    ppermute x36, waiting for transfers between devices: 31.2 us -> 37.1 us  [all_planes(): lax.ppermute(p, 'aux', pairs)]
    ppermute x9 -> x6, starting transfers between devices: 12.8 us -> 6.99 us  [the longest x3 4.97 us: scatter(): near = lax.ppermute(sent, 'aux', flipped(planes, 1))]
    ppermute x36, starting transfers between devices: 54.9 us -> 59.1 us  [all_planes(): lax.ppermute(p, 'aux', pairs)]
    dot_general x4 -> x3, matrix products: 11.5 us -> 8.19 us  [consume(): jnp.dot(fit_rows, rounded, preferred_element_type=jnp.float32)]
    ppermute x9 -> x6, waiting for transfers between devices: 31.7 us -> 30 us  [the longest x3 18.2 us: scatter(): near = lax.ppermute(sent, 'aux', flipped(planes, 1))]
  transfers between devices with their start and end apart: 73 -> 67, of which waited for: 29 -> 35; matrix products, arithmetic and copies ran while one was open for 13% -> 12% of each run, Pallas kernels for 2% -> 2%
where the time goes in v1:
time: 247 us; the launch traced here: 244 us
  starting transfers between devices  102 us (41%)
  waiting for transfers between devices  77.8 us (31%)
  other arithmetic  21.6 us (9%)
  Pallas kernels  15.1 us (6%)
  matrix products  13.8 us (6%)
  local copies, waits for them, and re-layouts  7.21 us (3%)
  between operations  6.26 us (3%)
    ppermute x36, starting transfers between devices, all_planes(): lax.ppermute(p, 'aux', pairs)  59.1 us
    ppermute x36, waiting for transfers between devices, all_planes(): lax.ppermute(p, 'aux', pairs)  37.1 us
    ppermute x15, starting transfers between devices, over_members(): lax.ppermute(a, axis, flipped(size, bit))  24.4 us
    ppermute x3, waiting for transfers between devices, scatter(): near = lax.ppermute(sent, 'aux', flipped(planes, 1))  18.2 us
    ppermute x3, waiting for transfers between devices, scatter(): lax.ppermute(far, 'aux', flipped(planes, planes - 1))  11.8 us
    pallas_call x1, Pallas kernels, spread(): pl.pallas_call(functools.partial(spread_kernel, planes, across, cap), out...  11.1 us
    dot_general x3, matrix products, consume(): jnp.dot(fit_rows, rounded, preferred_element_type=jnp.float32)  8.19 us
    select_n x9, other arithmetic, payloads(): return (jnp.where(even, right, left), jnp.where(even, left, right))  7.7 us
  transfers between devices with their start and end apart: 67, of which 35 were waited for; matrix products, arithmetic and copies ran while one was open for 12% of the time, Pallas kernels for 2%

profile of v1, /device:TPU:13, one launch (start us, length us, event | category | flops | bytes accessed | tf_op | source)
XLA Modules:
  0.0 244.1 jit_solution(13029994243756587979)
XLA Ops:
  4.0 1.2 constant_dynamic-slice_fusion.3
  5.2 1.3 collective-permute-start.6
  7.9 4.0 %shard_map.64 = f32[2,16,128]{2,1,0:T(8,128)S(1)} custom-call(bf16[64,128,128]{2,1,0:T(8,128)(2,1)} %own_tiles.1, bf16[7680,512]{1,0:T(8,128)(2,1)} %refs_13_.1), custom_call_target="tpu_custom_call" | custom-call | bytes 10485760 | tf_op jit(solution)/shard_map/pallas_call | solution.py:217
  11.9 2.1 collective-permute-start.7
  14.0 1.2 collective-permute-start.8
  16.4 1.6 collective-permute-start.10
  18.0 6.2 %collective-permute-done.9 = f32[2,128]{1,0:T(2,128)S(1)} collective-permute-done((f32[2,128]{1,0:T(2,128)S(1)}, f32[2,128]{1,0:T(2,128)S(1)}, u32[]{:S(2)}, u32[]{:S(2)}) %collective-permute-start.9) | collective-permute-done | bytes 1056 | tf_op jit(solution)/shard_map/ppermute | solution.py:350
  25.1 1.5 collective-permute-start.12
  26.7 1.2 collective-permute-start.13
  31.2 2.0 collective-permute-start.15
  34.2 2.0 collective-permute-start.16
  36.8 2.1 collective-permute-done.18.refs_8_
  38.9 2.4 collective-permute-start.21
  44.1 11.1 %shard_map.66 = f32[4,4096,128]{2,1,0:T(8,128)} custom-call(s32[3]{0:T(128)S(1)} %pad_add_fusion.place, s32[4,64]{1,0:T(4,128)S(1)} %copy-done.1, s32[4,64]{1,0:T(4,128)S(1)} %copy-done, s32[4,4]{1,0:T(4,128)S(1)} %get-tuple-element.327.begins, s32[4,4]{1,0:T(4,128)S(1)} %get-tuple-element.326.counts, bf16[64,128,128]{2,1,0:T(8,128)(2,1)} %get-tuple-element.578, ...), custom_call_target="tpu_custom_call" | custom-call | flops 1073741824 | bytes 25165824 | tf_op jit(solution)/shard_map/pallas_call | solution.py:156
  55.2 2.0 broadcast_select_fusion.39
  57.1 1.3 collective-permute-start.22
  58.6 1.3 collective-permute-start.25
  59.9 8.4 %collective-permute-done.22 = f16[1024,128]{1,0:T(8,128)(2,1)S(1)} collective-permute-done((f16[1024,128]{1,0:T(8,128)(2,1)S(1)}, f16[1024,128]{1,0:T(8,128)(2,1)S(1)}, u32[]{:S(2)}, u32[]{:S(2)}) %collective-permute-start.22) | collective-permute-done | bytes 262176 | tf_op jit(solution)/shard_map/ppermute | solution.py:307
  68.3 1.8 broadcast_select_fusion.35
  70.2 1.6 collective-permute-start.23
  71.8 2.3 collective-permute-start.24
  74.1 1.6 broadcast_select_fusion.33
  75.7 1.3 collective-permute-start.28
  77.1 3.0 %collective-permute-start.29 = (f16[1024,128]{1,0:T(8,128)(2,1)S(1)}, f16[1024,128]{1,0:T(8,128)(2,1)S(1)}, u32[]{:S(2)}, u32[]{:S(2)}) collective-permute-start(f16[1024,128]{1,0:T(8,128)(2,1)S(1)} %broadcast_select_fusion.32), channel_id=1, source_target_pairs={{4,8},{8,4},{5,9},{9,5},{6,10},{10,6},{7,11},{11,7},{20,24},{24,20... | collective-permute-start | bytes 786440 | tf_op jit(solution)/shard_map/ppermute | solution.py:307
  80.7 1.6 broadcast_select_fusion.29
  82.5 2.3 collective-permute-start.27
  85.1 1.2 collective-permute-done.29
  86.9 2.4 collective-permute-start.31
  89.3 1.4 collective-permute-done.26
  92.0 3.2 %collective-permute-start.33 = (f16[1024,128]{1,0:T(8,128)(2,1)S(1)}, f16[1024,128]{1,0:T(8,128)(2,1)S(1)}, u32[]{:S(2)}, u32[]{:S(2)}) collective-permute-start(f16[1024,128]{1,0:T(8,128)(2,1)S(1)} %get-tuple-element.387), channel_id=1, source_target_pairs={{4,8},{8,4},{5,9},{9,5},{6,10},{10,6},{7,11},{11,7},{20,24},{24,20... | collective-permute-start | bytes 786440 | tf_op jit(solution)/shard_map/ppermute | solution.py:307
  97.9 3.0 %collective-permute-start.35 = (f16[1024,128]{1,0:T(8,128)(2,1)S(1)}, f16[1024,128]{1,0:T(8,128)(2,1)S(1)}, u32[]{:S(2)}, u32[]{:S(2)}) collective-permute-start(f16[1024,128]{1,0:T(8,128)(2,1)S(1)} %get-tuple-element.385), channel_id=1, source_target_pairs={{4,8},{8,4},{5,9},{9,5},{6,10},{10,6},{7,11},{11,7},{20,24},{24,20... | collective-permute-start | bytes 786440 | tf_op jit(solution)/shard_map/ppermute | solution.py:307
  102.9 3.0 %collective-permute-start.37 = (f16[1024,128]{1,0:T(8,128)(2,1)S(1)}, f16[1024,128]{1,0:T(8,128)(2,1)S(1)}, u32[]{:S(2)}, u32[]{:S(2)}) collective-permute-start(f16[1024,128]{1,0:T(8,128)(2,1)S(1)} %get-tuple-element.381), channel_id=1, source_target_pairs={{4,8},{8,4},{5,9},{9,5},{6,10},{10,6},{7,11},{11,7},{20,24},{24,20... | collective-permute-start | bytes 786440 | tf_op jit(solution)/shard_map/ppermute | solution.py:307
  105.9 1.2 collective-permute-done.34
  108.5 3.1 %collective-permute-start.39 = (f16[1024,128]{1,0:T(8,128)(2,1)S(1)}, f16[1024,128]{1,0:T(8,128)(2,1)S(1)}, u32[]{:S(2)}, u32[]{:S(2)}) collective-permute-start(f16[1024,128]{1,0:T(8,128)(2,1)S(1)} %get-tuple-element.378), channel_id=1, source_target_pairs={{4,8},{8,4},{5,9},{9,5},{6,10},{10,6},{7,11},{11,7},{20,24},{24,20... | collective-permute-start | bytes 786440 | tf_op jit(solution)/shard_map/ppermute | solution.py:307
  113.9 3.2 %collective-permute-start.41 = (f16[1024,128]{1,0:T(8,128)(2,1)S(1)}, f16[1024,128]{1,0:T(8,128)(2,1)S(1)}, u32[]{:S(2)}, u32[]{:S(2)}) collective-permute-start(f16[1024,128]{1,0:T(8,128)(2,1)S(1)} %get-tuple-element.375), channel_id=1, source_target_pairs={{4,8},{8,4},{5,9},{9,5},{6,10},{10,6},{7,11},{11,7},{20,24},{24,20... | collective-permute-start | bytes 786440 | tf_op jit(solution)/shard_map/ppermute | solution.py:307
  119.2 2.9 %collective-permute-start.43 = (f16[1024,128]{1,0:T(8,128)(2,1)S(1)}, f16[1024,128]{1,0:T(8,128)(2,1)S(1)}, u32[]{:S(2)}, u32[]{:S(2)}) collective-permute-start(f16[1024,128]{1,0:T(8,128)(2,1)S(1)} %get-tuple-element.373), channel_id=1, source_target_pairs={{4,8},{8,4},{5,9},{9,5},{6,10},{10,6},{7,11},{11,7},{20,24},{24,20... | collective-permute-start | bytes 786440 | tf_op jit(solution)/shard_map/ppermute | solution.py:307
  124.7 2.8 %collective-permute-start.45 = (f16[1024,128]{1,0:T(8,128)(2,1)S(1)}, f16[1024,128]{1,0:T(8,128)(2,1)S(1)}, u32[]{:S(2)}, u32[]{:S(2)}) collective-permute-start(f16[1024,128]{1,0:T(8,128)(2,1)S(1)} %get-tuple-element.369), channel_id=1, source_target_pairs={{4,8},{8,4},{5,9},{9,5},{6,10},{10,6},{7,11},{11,7},{20,24},{24,20... | collective-permute-start | bytes 786440 | tf_op jit(solution)/shard_map/ppermute | solution.py:307
  131.6 1.4 slice-done.1
  133.0 2.4 fusion.1
  135.4 6.5 %collective-permute-start.52 = (bf16[1024,256]{0,1:T(8,128)(2,1)S(1)}, bf16[1024,256]{0,1:T(8,128)(2,1)S(1)}, u32[]{:S(2)}, u32[]{:S(2)}) collective-permute-start(bf16[1024,256]{0,1:T(8,128)(2,1)S(1)} %fusion.1), channel_id=1, source_target_pairs={{0,1},{1,0},{2,3},{3,2},{4,5},{5,4},{6,7},{7,6},{8,9},{9,8},{10,11... | collective-permute-start | bytes 1572872 | tf_op jit(solution)/shard_map/ppermute | solution.py:29
  142.8 2.6 %collective-permute-start.47 = (f16[1024,128]{1,0:T(8,128)(2,1)S(1)}, f16[1024,128]{1,0:T(8,128)(2,1)S(1)}, u32[]{:S(2)}, u32[]{:S(2)}) collective-permute-start(f16[1024,128]{1,0:T(8,128)(2,1)S(1)} %get-tuple-element.366), channel_id=1, source_target_pairs={{4,8},{8,4},{5,9},{9,5},{6,10},{10,6},{7,11},{11,7},{20,24},{24,20... | collective-permute-start | bytes 786440 | tf_op jit(solution)/shard_map/ppermute | solution.py:307
  146.1 4.2 %collective-permute-done.46 = f16[1024,128]{1,0:T(8,128)(2,1)S(1)} collective-permute-done((f16[1024,128]{1,0:T(8,128)(2,1)S(1)}, f16[1024,128]{1,0:T(8,128)(2,1)S(1)}, u32[]{:S(2)}, u32[]{:S(2)}) %collective-permute-start.46) | collective-permute-done | bytes 262176 | tf_op jit(solution)/shard_map/ppermute | solution.py:307
  150.3 2.6 %collective-permute-start.49 = (f16[1024,128]{1,0:T(8,128)(2,1)S(1)}, f16[1024,128]{1,0:T(8,128)(2,1)S(1)}, u32[]{:S(2)}, u32[]{:S(2)}) collective-permute-start(f16[1024,128]{1,0:T(8,128)(2,1)S(1)} %get-tuple-element.354), channel_id=1, source_target_pairs={{4,8},{8,4},{5,9},{9,5},{6,10},{10,6},{7,11},{11,7},{20,24},{24,20... | collective-permute-start | bytes 786440 | tf_op jit(solution)/shard_map/ppermute | solution.py:307
  153.6 2.3 collective-permute-done.48
  156.0 2.6 %collective-permute-start.51 = (f16[1024,128]{1,0:T(8,128)(2,1)S(1)}, f16[1024,128]{1,0:T(8,128)(2,1)S(1)}, u32[]{:S(2)}, u32[]{:S(2)}) collective-permute-start(f16[1024,128]{1,0:T(8,128)(2,1)S(1)} %get-tuple-element.358), channel_id=1, source_target_pairs={{4,8},{8,4},{5,9},{9,5},{6,10},{10,6},{7,11},{11,7},{20,24},{24,20... | collective-permute-start | bytes 786440 | tf_op jit(solution)/shard_map/ppermute | solution.py:307
  159.2 1.3 collective-permute-start.60
  160.5 2.7 %collective-permute-start.61 = (f16[1024,128]{1,0:T(8,128)(2,1)S(1)}, f16[1024,128]{1,0:T(8,128)(2,1)S(1)}, u32[]{:S(2)}, u32[]{:S(2)}) collective-permute-start(f16[1024,128]{1,0:T(8,128)(2,1)S(1)} %get-tuple-element.360), channel_id=1, source_target_pairs={{4,8},{8,4},{5,9},{9,5},{6,10},{10,6},{7,11},{11,7},{20,24},{24,20... | collective-permute-start | bytes 786440 | tf_op jit(solution)/shard_map/ppermute | solution.py:307
  165.1 2.9 %fusion.2 = bf16[1024,128]{0,1:T(8,128)(2,1)S(1)} fusion(bf16[4096,128]{1,0:T(8,128)(2,1)S(1)} %multiply_convert_fusion.2, bf16[1024,4096]{1,0:T(8,128)(2,1)S(1)} %bitcast.114), kind=kOutput, calls=%fused_computation.21 | convolution fusion | flops 1073872896 | bytes 9699328 | tf_op jit(solution)/shard_map/dot_general | solution.py:419
  168.0 3.5 %collective-permute-start.53 = (bf16[1024,128]{0,1:T(8,128)(2,1)S(1)}, bf16[1024,128]{0,1:T(8,128)(2,1)S(1)}, u32[]{:S(2)}, u32[]{:S(2)}) collective-permute-start(bf16[1024,128]{0,1:T(8,128)(2,1)S(1)} %fusion.2), channel_id=1, source_target_pairs={{0,1},{1,0},{2,3},{3,2},{4,5},{5,4},{6,7},{7,6},{8,9},{9,8},{10,11... | collective-permute-start | bytes 786440 | tf_op jit(solution)/shard_map/ppermute | solution.py:29
  172.0 1.5 collective-permute-start.62
  174.2 2.8 %collective-permute-start.63 = (f16[1024,128]{1,0:T(8,128)(2,1)S(1)}, f16[1024,128]{1,0:T(8,128)(2,1)S(1)}, u32[]{:S(2)}, u32[]{:S(2)}) collective-permute-start(f16[1024,128]{1,0:T(8,128)(2,1)S(1)} %get-tuple-element.363), channel_id=1, source_target_pairs={{4,8},{8,4},{5,9},{9,5},{6,10},{10,6},{7,11},{11,7},{20,24},{24,20... | collective-permute-start | bytes 786440 | tf_op jit(solution)/shard_map/ppermute | solution.py:307
  178.9 4.1 %collective-permute-start.64 = (f16[1024,128]{1,0:T(8,128)(2,1)S(1)}, f16[1024,128]{1,0:T(8,128)(2,1)S(1)}, u32[]{:S(2)}, u32[]{:S(2)}) collective-permute-start(f16[1024,128]{1,0:T(8,128)(2,1)S(1)} %get-tuple-element.346), channel_id=1, source_target_pairs={{4,0},{8,12},{5,1},{9,13},{6,2},{10,14},{7,3},{11,15},{20,16},{24,... | collective-permute-start | bytes 786440 | tf_op jit(solution)/shard_map/ppermute | solution.py:307
  184.2 1.3 collective-permute-start.65
  185.5 1.2 collective-permute-start.57
  189.2 4.2 %collective-permute-done.65 = f16[1024,128]{1,0:T(8,128)(2,1)S(1)} collective-permute-done((f16[1024,128]{1,0:T(8,128)(2,1)S(1)}, f16[1024,128]{1,0:T(8,128)(2,1)S(1)}, u32[]{:S(2)}, u32[]{:S(2)}) %collective-permute-start.65) | collective-permute-done | bytes 262176 | tf_op jit(solution)/shard_map/ppermute | solution.py:307
  194.4 2.9 %convolution_convert_fusion.1 = bf16[128,1024]{1,0:T(8,128)(2,1)S(1)} fusion(bf16[4096,128]{1,0:T(8,128)(2,1)S(1)} %multiply_convert_fusion.1, bf16[1024,4096]{1,0:T(8,128)(2,1)S(1)} %bitcast.114), kind=kOutput, calls=%fused_computation.15 | convolution fusion | flops 1073872896 | bytes 9699328 | tf_op jit(solution)/shard_map/dot_general | solution.py:419
  198.4 2.0 collective-permute-start.68
  202.1 2.3 collective-permute-start.66
  204.9 4.8 %collective-permute-done.66 = bf16[2,384,128]{1,2,0:T(8,128)(2,1)S(1)} collective-permute-done((bf16[2,384,128]{1,2,0:T(8,128)(2,1)S(1)}, bf16[2,384,128]{1,2,0:T(8,128)(2,1)S(1)}, u32[]{:S(2)}, u32[]{:S(2)}) %collective-permute-start.66) | collective-permute-done | bytes 196640 | tf_op jit(solution)/shard_map/ppermute | solution.py:409
  213.2 2.6 %collective-permute-start.71 = (bf16[2,128,512]{1,2,0:T(8,128)(2,1)S(1)}, bf16[2,128,512]{1,2,0:T(8,128)(2,1)S(1)}, u32[]{:S(2)}, u32[]{:S(2)}) collective-permute-start(bf16[2,128,512]{1,2,0:T(8,128)(2,1)S(1)} %pad_maximum_fusion.8), channel_id=1, source_target_pairs={{0,4},{4,0},{8,12},{12,8},{1,5},{5,1},{9,13},{13,9},{2,6},{6,2},{1... | collective-permute-start | bytes 786440 | tf_op jit(solution)/shard_map/ppermute | solution.py:409
  215.8 6.5 %collective-permute-done.58 = bf16[2,384,384]{1,2,0:T(8,128)(2,1)S(1)} collective-permute-done((bf16[2,384,384]{1,2,0:T(8,128)(2,1)S(1)}, bf16[2,384,384]{1,2,0:T(8,128)(2,1)S(1)}, u32[]{:S(2)}, u32[]{:S(2)}) %collective-permute-start.58) | collective-permute-done | bytes 589856 | tf_op jit(solution)/shard_map/ppermute | solution.py:409
  223.1 6.9 %collective-permute-done.71 = bf16[2,128,512]{1,2,0:T(8,128)(2,1)S(1)} collective-permute-done((bf16[2,128,512]{1,2,0:T(8,128)(2,1)S(1)}, bf16[2,128,512]{1,2,0:T(8,128)(2,1)S(1)}, u32[]{:S(2)}, u32[]{:S(2)}) %collective-permute-start.71) | collective-permute-done | bytes 262176 | tf_op jit(solution)/shard_map/ppermute | solution.py:409
  230.9 11.8 %collective-permute-done.72 = bf16[128,512]{0,1:T(8,128)(2,1)S(1)} collective-permute-done((bf16[128,512]{0,1:T(8,128)(2,1)S(1)}, bf16[128,512]{0,1:T(8,128)(2,1)S(1)}, u32[]{:S(2)}, u32[]{:S(2)}) %collective-permute-start.72) | collective-permute-done | bytes 131104 | tf_op jit(solution)/shard_map/ppermute | solution.py:411
  242.8 1.3 copy.16
  (185 shorter events, 50.8 us)
Async XLA Ops:
  5.2 6.8 %collective-permute-start.6 = (bf16[7,128,128]{2,1,0:T(8,128)(2,1)S(1)}, bf16[7,128,128]{2,1,0:T(8,128)(2,1)S(1)}, u32[]{:S(2)}, u32[]{:S(2)}) collective-permute-start(bf16[7,128,128]{2,1,0:T(8,128)(2,1)S(1)} %get-tuple-element.266), channel_id=1, source_target_pairs={{0,4},{4,8},{8,12},{12,0},{1,5},{5,9},{9,13},{13,1},{2,6},{6,10},{... | collective-permute-start | bytes 688136 | tf_op jit(solution)/shard_map/ppermute | solution.py:360
  11.9 13.2 %collective-permute-start.7 = (bf16[7,128,128]{2,1,0:T(8,128)(2,1)S(1)}, bf16[7,128,128]{2,1,0:T(8,128)(2,1)S(1)}, u32[]{:S(2)}, u32[]{:S(2)}) collective-permute-start(bf16[7,128,128]{2,1,0:T(8,128)(2,1)S(1)} %get-tuple-element.269), channel_id=1, source_target_pairs={{0,8},{4,12},{8,0},{12,4},{1,9},{5,13},{9,1},{13,5},{2,10},{6,14},... | collective-permute-start | bytes 688136 | tf_op jit(solution)/shard_map/ppermute | solution.py:363
  14.0 11.1 %collective-permute-start.8 = (bf16[7,128,128]{2,1,0:T(8,128)(2,1)S(1)}, bf16[7,128,128]{2,1,0:T(8,128)(2,1)S(1)}, u32[]{:S(2)}, u32[]{:S(2)}) collective-permute-start(bf16[7,128,128]{2,1,0:T(8,128)(2,1)S(1)} %collective-permute-done.6.refs_0_), channel_id=1, source_target_pairs={{0,2},{1,3},{2,0},{3,1},{4,6},{5,7},{6,4},{7,5},{8,10},{9,11},{10,... | collective-permute-start | bytes 688136 | tf_op jit(solution)/shard_map/ppermute | solution.py:364
  15.4 8.7 %collective-permute-start.9 = (f32[2,128]{1,0:T(2,128)S(1)}, f32[2,128]{1,0:T(2,128)S(1)}, u32[]{:S(2)}, u32[]{:S(2)}) collective-permute-start(f32[2,128]{1,0:T(2,128)S(1)} %broadcast_in_dim.77), channel_id=1, source_target_pairs={{0,4},{4,8},{8,12},{12,0},{1,5},{5,9},{9,13},{13,1},{2,6},{6,10},{... | collective-permute-start | bytes 3080 | tf_op jit(solution)/shard_map/ppermute | solution.py:350
  16.4 7.8 %collective-permute-start.10 = (f32[2,128]{1,0:T(2,128)S(1)}, f32[2,128]{1,0:T(2,128)S(1)}, u32[]{:S(2)}, u32[]{:S(2)}) collective-permute-start(f32[2,128]{1,0:T(2,128)S(1)} %broadcast_in_dim.77), channel_id=1, source_target_pairs={{0,8},{4,12},{8,0},{12,4},{1,9},{5,13},{9,1},{13,5},{2,10},{6,14},... | collective-permute-start | bytes 3080 | tf_op jit(solution)/shard_map/ppermute | solution.py:350
  18.0 7.2 %collective-permute-start.11 = (f32[2,128]{1,0:T(2,128)S(1)}, f32[2,128]{1,0:T(2,128)S(1)}, u32[]{:S(2)}, u32[]{:S(2)}) collective-permute-start(f32[2,128]{1,0:T(2,128)S(1)} %broadcast_in_dim.77), channel_id=1, source_target_pairs={{0,12},{4,0},{8,4},{12,8},{1,13},{5,1},{9,5},{13,9},{2,14},{6,2},{... | collective-permute-start | bytes 3080 | tf_op jit(solution)/shard_map/ppermute | solution.py:350
  25.1 8.0 %collective-permute-start.12 = (bf16[7,128,128]{2,1,0:T(8,128)(2,1)S(1)}, bf16[7,128,128]{2,1,0:T(8,128)(2,1)S(1)}, u32[]{:S(2)}, u32[]{:S(2)}) collective-permute-start(bf16[7,128,128]{2,1,0:T(8,128)(2,1)S(1)} %get-tuple-element.272), channel_id=1, source_target_pairs={{0,12},{4,0},{8,4},{12,8},{1,13},{5,1},{9,5},{13,9},{2,14},{6,2},{... | collective-permute-start | bytes 688136 | tf_op jit(solution)/shard_map/ppermute | solution.py:366
  26.7 6.5 %collective-permute-start.13 = (bf16[7,128,128]{2,1,0:T(8,128)(2,1)S(1)}, bf16[7,128,128]{2,1,0:T(8,128)(2,1)S(1)}, u32[]{:S(2)}, u32[]{:S(2)}) collective-permute-start(bf16[7,128,128]{2,1,0:T(8,128)(2,1)S(1)} %collective-permute-done.7.refs_1_), channel_id=1, source_target_pairs={{0,2},{1,3},{2,0},{3,1},{4,6},{5,7},{6,4},{7,5},{8,10},{9,11},{10,... | collective-permute-start | bytes 688136 | tf_op jit(solution)/shard_map/ppermute | solution.py:367
  31.2 5.5 %collective-permute-start.15 = (bf16[7,128,128]{2,1,0:T(8,128)(2,1)S(1)}, bf16[7,128,128]{2,1,0:T(8,128)(2,1)S(1)}, u32[]{:S(2)}, u32[]{:S(2)}) collective-permute-start(bf16[7,128,128]{2,1,0:T(8,128)(2,1)S(1)} %collective-permute-done.6.refs_0_), channel_id=1, source_target_pairs={{0,1},{1,0},{2,3},{3,2},{4,5},{5,4},{6,7},{7,6},{8,9},{9,8},{10,11... | collective-permute-start | bytes 688136 | tf_op jit(solution)/shard_map/ppermute | solution.py:29
  33.2 5.7 %collective-permute-start.18 = (bf16[7,128,128]{2,1,0:T(8,128)(2,1)S(1)}, bf16[7,128,128]{2,1,0:T(8,128)(2,1)}, u32[]{:S(2)}, u32[]{:S(2)}) collective-permute-start(bf16[7,128,128]{2,1,0:T(8,128)(2,1)S(1)} %collective-permute-done.12.refs_2_), channel_id=1, source_target_pairs={{0,2},{1,3},{2,0},{3,1},{4,6},{5,7},{6,4},{7,5},{8,10},{9,11},{10,... | collective-permute-start | bytes 688136 | tf_op jit(solution)/shard_map/ppermute | solution.py:369
  34.2 9.1 %collective-permute-start.16 = (bf16[7,128,128]{2,1,0:T(8,128)(2,1)S(1)}, bf16[7,128,128]{2,1,0:T(8,128)(2,1)S(1)}, u32[]{:S(2)}, u32[]{:S(2)}) collective-permute-start(bf16[7,128,128]{2,1,0:T(8,128)(2,1)S(1)} %collective-permute-done.7.refs_1_), channel_id=1, source_target_pairs={{0,1},{1,0},{2,3},{3,2},{4,5},{5,4},{6,7},{7,6},{8,9},{9,8},{10,11... | collective-permute-start | bytes 688136 | tf_op jit(solution)/shard_map/ppermute | solution.py:29
  36.2 7.1 %collective-permute-start.19 = (bf16[7,128,128]{2,1,0:T(8,128)(2,1)S(1)}, bf16[7,128,128]{2,1,0:T(8,128)(2,1)S(1)}, u32[]{:S(2)}, u32[]{:S(2)}) collective-permute-start(bf16[7,128,128]{2,1,0:T(8,128)(2,1)S(1)} %collective-permute-done.8.refs_6_), channel_id=1, source_target_pairs={{0,1},{1,0},{2,3},{3,2},{4,5},{5,4},{6,7},{7,6},{8,9},{9,8},{10,11... | collective-permute-start | bytes 688136 | tf_op jit(solution)/shard_map/ppermute | solution.py:29
  36.2 7.0 %collective-permute-start.17 = (bf16[7,128,128]{2,1,0:T(8,128)(2,1)S(1)}, bf16[7,128,128]{2,1,0:T(8,128)(2,1)S(1)}, u32[]{:S(2)}, u32[]{:S(2)}) collective-permute-start(bf16[7,128,128]{2,1,0:T(8,128)(2,1)S(1)} %collective-permute-done.12.refs_2_), channel_id=1, source_target_pairs={{0,1},{1,0},{2,3},{3,2},{4,5},{5,4},{6,7},{7,6},{8,9},{9,8},{10,11... | collective-permute-start | bytes 688136 | tf_op jit(solution)/shard_map/ppermute | solution.py:29
  36.7 6.6 %collective-permute-start.20 = (bf16[7,128,128]{2,1,0:T(8,128)(2,1)S(1)}, bf16[7,128,128]{2,1,0:T(8,128)(2,1)S(1)}, u32[]{:S(2)}, u32[]{:S(2)}) collective-permute-start(bf16[7,128,128]{2,1,0:T(8,128)(2,1)S(1)} %collective-permute-done.13.refs_7_), channel_id=1, source_target_pairs={{0,1},{1,0},{2,3},{3,2},{4,5},{5,4},{6,7},{7,6},{8,9},{9,8},{10,11... | collective-permute-start | bytes 688136 | tf_op jit(solution)/shard_map/ppermute | solution.py:29
  38.9 4.4 %collective-permute-start.21 = (bf16[7,128,128]{2,1,0:T(8,128)(2,1)}, bf16[7,128,128]{2,1,0:T(8,128)(2,1)S(1)}, u32[]{:S(2)}, u32[]{:S(2)}) collective-permute-start(bf16[7,128,128]{2,1,0:T(8,128)(2,1)} %collective-permute-done.18.refs_8_), channel_id=1, source_target_pairs={{0,1},{1,0},{2,3},{3,2},{4,5},{5,4},{6,7},{7,6},{8,9},{9,8},{10,11... | collective-permute-start | bytes 688136 | tf_op jit(solution)/shard_map/ppermute | solution.py:29
  57.1 11.1 %collective-permute-start.22 = (f16[1024,128]{1,0:T(8,128)(2,1)S(1)}, f16[1024,128]{1,0:T(8,128)(2,1)S(1)}, u32[]{:S(2)}, u32[]{:S(2)}) collective-permute-start(f16[1024,128]{1,0:T(8,128)(2,1)S(1)} %get-tuple-element.433), channel_id=1, source_target_pairs={{0,4},{12,8},{1,5},{13,9},{2,6},{14,10},{3,7},{15,11},{16,20},{28,... | collective-permute-start | bytes 786440 | tf_op jit(solution)/shard_map/ppermute | solution.py:307
  58.6 15.5 %collective-permute-start.25 = (f16[1024,128]{1,0:T(8,128)(2,1)S(1)}, f16[1024,128]{1,0:T(8,128)(2,1)S(1)}, u32[]{:S(2)}, u32[]{:S(2)}) collective-permute-start(f16[1024,128]{1,0:T(8,128)(2,1)S(1)} %get-tuple-element.432), channel_id=1, source_target_pairs={{0,4},{12,8},{1,5},{13,9},{2,6},{14,10},{3,7},{15,11},{16,20},{28,... | collective-permute-start | bytes 786440 | tf_op jit(solution)/shard_map/ppermute | solution.py:307
  70.2 9.9 %collective-permute-start.23 = (f16[1024,128]{1,0:T(8,128)(2,1)S(1)}, f16[1024,128]{1,0:T(8,128)(2,1)S(1)}, u32[]{:S(2)}, u32[]{:S(2)}) collective-permute-start(f16[1024,128]{1,0:T(8,128)(2,1)S(1)} %broadcast_select_fusion.36), channel_id=1, source_target_pairs={{0,4},{12,8},{1,5},{13,9},{2,6},{14,10},{3,7},{15,11},{16,20},{28,... | collective-permute-start | bytes 786440 | tf_op jit(solution)/shard_map/ppermute | solution.py:307
  71.8 8.9 %collective-permute-start.24 = (f16[1024,128]{1,0:T(8,128)(2,1)S(1)}, f16[1024,128]{1,0:T(8,128)(2,1)S(1)}, u32[]{:S(2)}, u32[]{:S(2)}) collective-permute-start(f16[1024,128]{1,0:T(8,128)(2,1)S(1)} %get-tuple-element.398), channel_id=1, source_target_pairs={{4,8},{8,4},{5,9},{9,5},{6,10},{10,6},{7,11},{11,7},{20,24},{24,20... | collective-permute-start | bytes 786440 | tf_op jit(solution)/shard_map/ppermute | solution.py:307
  75.7 9.4 %collective-permute-start.28 = (f16[1024,128]{1,0:T(8,128)(2,1)S(1)}, f16[1024,128]{1,0:T(8,128)(2,1)S(1)}, u32[]{:S(2)}, u32[]{:S(2)}) collective-permute-start(f16[1024,128]{1,0:T(8,128)(2,1)S(1)} %get-tuple-element.395), channel_id=1, source_target_pairs={{0,4},{12,8},{1,5},{13,9},{2,6},{14,10},{3,7},{15,11},{16,20},{28,... | collective-permute-start | bytes 786440 | tf_op jit(solution)/shard_map/ppermute | solution.py:307
  77.1 9.2 %collective-permute-start.29 = (f16[1024,128]{1,0:T(8,128)(2,1)S(1)}, f16[1024,128]{1,0:T(8,128)(2,1)S(1)}, u32[]{:S(2)}, u32[]{:S(2)}) collective-permute-start(f16[1024,128]{1,0:T(8,128)(2,1)S(1)} %broadcast_select_fusion.32), channel_id=1, source_target_pairs={{4,8},{8,4},{5,9},{9,5},{6,10},{10,6},{7,11},{11,7},{20,24},{24,20... | collective-permute-start | bytes 786440 | tf_op jit(solution)/shard_map/ppermute | solution.py:307
  82.4 8.2 %collective-permute-start.26 = (f16[1024,128]{1,0:T(8,128)(2,1)S(1)}, f16[1024,128]{1,0:T(8,128)(2,1)S(1)}, u32[]{:S(2)}, u32[]{:S(2)}) collective-permute-start(f16[1024,128]{1,0:T(8,128)(2,1)S(1)} %broadcast_select_fusion.30), channel_id=1, source_target_pairs={{0,4},{4,0},{8,12},{12,8},{1,5},{5,1},{9,13},{13,9},{2,6},{6,2},{1... | collective-permute-start | bytes 786440 | tf_op jit(solution)/shard_map/ppermute | solution.py:307
  82.5 8.9 %collective-permute-start.27 = (f16[1024,128]{1,0:T(8,128)(2,1)S(1)}, f16[1024,128]{1,0:T(8,128)(2,1)S(1)}, u32[]{:S(2)}, u32[]{:S(2)}) collective-permute-start(f16[1024,128]{1,0:T(8,128)(2,1)S(1)} %get-tuple-element.392), channel_id=1, source_target_pairs={{4,8},{8,4},{5,9},{9,5},{6,10},{10,6},{7,11},{11,7},{20,24},{24,20... | collective-permute-start | bytes 786440 | tf_op jit(solution)/shard_map/ppermute | solution.py:307
  86.8 9.5 %collective-permute-start.30 = (f16[1024,128]{1,0:T(8,128)(2,1)S(1)}, f16[1024,128]{1,0:T(8,128)(2,1)S(1)}, u32[]{:S(2)}, u32[]{:S(2)}) collective-permute-start(f16[1024,128]{1,0:T(8,128)(2,1)S(1)} %broadcast_select_fusion.27), channel_id=1, source_target_pairs={{0,4},{4,0},{8,12},{12,8},{1,5},{5,1},{9,13},{13,9},{2,6},{6,2},{1... | collective-permute-start | bytes 786440 | tf_op jit(solution)/shard_map/ppermute | solution.py:307
  86.9 10.3 %collective-permute-start.31 = (f16[1024,128]{1,0:T(8,128)(2,1)S(1)}, f16[1024,128]{1,0:T(8,128)(2,1)S(1)}, u32[]{:S(2)}, u32[]{:S(2)}) collective-permute-start(f16[1024,128]{1,0:T(8,128)(2,1)S(1)} %get-tuple-element.389), channel_id=1, source_target_pairs={{4,8},{8,4},{5,9},{9,5},{6,10},{10,6},{7,11},{11,7},{20,24},{24,20... | collective-permute-start | bytes 786440 | tf_op jit(solution)/shard_map/ppermute | solution.py:307
  92.0 9.5 %collective-permute-start.32 = (f16[1024,128]{1,0:T(8,128)(2,1)S(1)}, f16[1024,128]{1,0:T(8,128)(2,1)S(1)}, u32[]{:S(2)}, u32[]{:S(2)}) collective-permute-start(f16[1024,128]{1,0:T(8,128)(2,1)S(1)} %get-tuple-element.388), channel_id=1, source_target_pairs={{0,4},{4,0},{8,12},{12,8},{1,5},{5,1},{9,13},{13,9},{2,6},{6,2},{1... | collective-permute-start | bytes 786440 | tf_op jit(solution)/shard_map/ppermute | solution.py:307
  92.0 10.1 %collective-permute-start.33 = (f16[1024,128]{1,0:T(8,128)(2,1)S(1)}, f16[1024,128]{1,0:T(8,128)(2,1)S(1)}, u32[]{:S(2)}, u32[]{:S(2)}) collective-permute-start(f16[1024,128]{1,0:T(8,128)(2,1)S(1)} %get-tuple-element.387), channel_id=1, source_target_pairs={{4,8},{8,4},{5,9},{9,5},{6,10},{10,6},{7,11},{11,7},{20,24},{24,20... | collective-permute-start | bytes 786440 | tf_op jit(solution)/shard_map/ppermute | solution.py:307
  97.8 9.3 %collective-permute-start.34 = (f16[1024,128]{1,0:T(8,128)(2,1)S(1)}, f16[1024,128]{1,0:T(8,128)(2,1)S(1)}, u32[]{:S(2)}, u32[]{:S(2)}) collective-permute-start(f16[1024,128]{1,0:T(8,128)(2,1)S(1)} %get-tuple-element.384), channel_id=1, source_target_pairs={{0,4},{4,0},{8,12},{12,8},{1,5},{5,1},{9,13},{13,9},{2,6},{6,2},{1... | collective-permute-start | bytes 786440 | tf_op jit(solution)/shard_map/ppermute | solution.py:307
  97.9 9.9 %collective-permute-start.35 = (f16[1024,128]{1,0:T(8,128)(2,1)S(1)}, f16[1024,128]{1,0:T(8,128)(2,1)S(1)}, u32[]{:S(2)}, u32[]{:S(2)}) collective-permute-start(f16[1024,128]{1,0:T(8,128)(2,1)S(1)} %get-tuple-element.385), channel_id=1, source_target_pairs={{4,8},{8,4},{5,9},{9,5},{6,10},{10,6},{7,11},{11,7},{20,24},{24,20... | collective-permute-start | bytes 786440 | tf_op jit(solution)/shard_map/ppermute | solution.py:307
  102.8 9.6 %collective-permute-start.36 = (f16[1024,128]{1,0:T(8,128)(2,1)S(1)}, f16[1024,128]{1,0:T(8,128)(2,1)S(1)}, u32[]{:S(2)}, u32[]{:S(2)}) collective-permute-start(f16[1024,128]{1,0:T(8,128)(2,1)S(1)} %get-tuple-element.382), channel_id=1, source_target_pairs={{0,4},{4,0},{8,12},{12,8},{1,5},{5,1},{9,13},{13,9},{2,6},{6,2},{1... | collective-permute-start | bytes 786440 | tf_op jit(solution)/shard_map/ppermute | solution.py:307
  102.9 10.3 %collective-permute-start.37 = (f16[1024,128]{1,0:T(8,128)(2,1)S(1)}, f16[1024,128]{1,0:T(8,128)(2,1)S(1)}, u32[]{:S(2)}, u32[]{:S(2)}) collective-permute-start(f16[1024,128]{1,0:T(8,128)(2,1)S(1)} %get-tuple-element.381), channel_id=1, source_target_pairs={{4,8},{8,4},{5,9},{9,5},{6,10},{10,6},{7,11},{11,7},{20,24},{24,20... | collective-permute-start | bytes 786440 | tf_op jit(solution)/shard_map/ppermute | solution.py:307
  108.4 9.3 %collective-permute-start.38 = (f16[1024,128]{1,0:T(8,128)(2,1)S(1)}, f16[1024,128]{1,0:T(8,128)(2,1)S(1)}, u32[]{:S(2)}, u32[]{:S(2)}) collective-permute-start(f16[1024,128]{1,0:T(8,128)(2,1)S(1)} %get-tuple-element.379), channel_id=1, source_target_pairs={{0,4},{4,0},{8,12},{12,8},{1,5},{5,1},{9,13},{13,9},{2,6},{6,2},{1... | collective-permute-start | bytes 786440 | tf_op jit(solution)/shard_map/ppermute | solution.py:307
  108.5 10.0 %collective-permute-start.39 = (f16[1024,128]{1,0:T(8,128)(2,1)S(1)}, f16[1024,128]{1,0:T(8,128)(2,1)S(1)}, u32[]{:S(2)}, u32[]{:S(2)}) collective-permute-start(f16[1024,128]{1,0:T(8,128)(2,1)S(1)} %get-tuple-element.378), channel_id=1, source_target_pairs={{4,8},{8,4},{5,9},{9,5},{6,10},{10,6},{7,11},{11,7},{20,24},{24,20... | collective-permute-start | bytes 786440 | tf_op jit(solution)/shard_map/ppermute | solution.py:307
  113.8 9.3 %collective-permute-start.40 = (f16[1024,128]{1,0:T(8,128)(2,1)S(1)}, f16[1024,128]{1,0:T(8,128)(2,1)S(1)}, u32[]{:S(2)}, u32[]{:S(2)}) collective-permute-start(f16[1024,128]{1,0:T(8,128)(2,1)S(1)} %get-tuple-element.376), channel_id=1, source_target_pairs={{0,4},{4,0},{8,12},{12,8},{1,5},{5,1},{9,13},{13,9},{2,6},{6,2},{1... | collective-permute-start | bytes 786440 | tf_op jit(solution)/shard_map/ppermute | solution.py:307
  113.9 10.2 %collective-permute-start.41 = (f16[1024,128]{1,0:T(8,128)(2,1)S(1)}, f16[1024,128]{1,0:T(8,128)(2,1)S(1)}, u32[]{:S(2)}, u32[]{:S(2)}) collective-permute-start(f16[1024,128]{1,0:T(8,128)(2,1)S(1)} %get-tuple-element.375), channel_id=1, source_target_pairs={{4,8},{8,4},{5,9},{9,5},{6,10},{10,6},{7,11},{11,7},{20,24},{24,20... | collective-permute-start | bytes 786440 | tf_op jit(solution)/shard_map/ppermute | solution.py:307
  119.1 9.3 %collective-permute-start.42 = (f16[1024,128]{1,0:T(8,128)(2,1)S(1)}, f16[1024,128]{1,0:T(8,128)(2,1)S(1)}, u32[]{:S(2)}, u32[]{:S(2)}) collective-permute-start(f16[1024,128]{1,0:T(8,128)(2,1)S(1)} %get-tuple-element.372), channel_id=1, source_target_pairs={{0,4},{4,0},{8,12},{12,8},{1,5},{5,1},{9,13},{13,9},{2,6},{6,2},{1... | collective-permute-start | bytes 786440 | tf_op jit(solution)/shard_map/ppermute | solution.py:307
  119.2 10.1 %collective-permute-start.43 = (f16[1024,128]{1,0:T(8,128)(2,1)S(1)}, f16[1024,128]{1,0:T(8,128)(2,1)S(1)}, u32[]{:S(2)}, u32[]{:S(2)}) collective-permute-start(f16[1024,128]{1,0:T(8,128)(2,1)S(1)} %get-tuple-element.373), channel_id=1, source_target_pairs={{4,8},{8,4},{5,9},{9,5},{6,10},{10,6},{7,11},{11,7},{20,24},{24,20... | collective-permute-start | bytes 786440 | tf_op jit(solution)/shard_map/ppermute | solution.py:307
  124.6 18.2 %collective-permute-start.44 = (f16[1024,128]{1,0:T(8,128)(2,1)S(1)}, f16[1024,128]{1,0:T(8,128)(2,1)S(1)}, u32[]{:S(2)}, u32[]{:S(2)}) collective-permute-start(f16[1024,128]{1,0:T(8,128)(2,1)S(1)} %get-tuple-element.370), channel_id=1, source_target_pairs={{0,4},{4,0},{8,12},{12,8},{1,5},{5,1},{9,13},{13,9},{2,6},{6,2},{1... | collective-permute-start | bytes 786440 | tf_op jit(solution)/shard_map/ppermute | solution.py:307
  124.7 20.7 %collective-permute-start.45 = (f16[1024,128]{1,0:T(8,128)(2,1)S(1)}, f16[1024,128]{1,0:T(8,128)(2,1)S(1)}, u32[]{:S(2)}, u32[]{:S(2)}) collective-permute-start(f16[1024,128]{1,0:T(8,128)(2,1)S(1)} %get-tuple-element.369), channel_id=1, source_target_pairs={{4,8},{8,4},{5,9},{9,5},{6,10},{10,6},{7,11},{11,7},{20,24},{24,20... | collective-permute-start | bytes 786440 | tf_op jit(solution)/shard_map/ppermute | solution.py:307
  135.4 36.1 %collective-permute-start.52 = (bf16[1024,256]{0,1:T(8,128)(2,1)S(1)}, bf16[1024,256]{0,1:T(8,128)(2,1)S(1)}, u32[]{:S(2)}, u32[]{:S(2)}) collective-permute-start(bf16[1024,256]{0,1:T(8,128)(2,1)S(1)} %fusion.1), channel_id=1, source_target_pairs={{0,1},{1,0},{2,3},{3,2},{4,5},{5,4},{6,7},{7,6},{8,9},{9,8},{10,11... | collective-permute-start | bytes 1572872 | tf_op jit(solution)/shard_map/ppermute | solution.py:29
  141.8 30.2 %collective-permute-start.54 = (bf16[1024,256]{0,1:T(8,128)(2,1)S(1)}, bf16[1024,256]{0,1:T(8,128)(2,1)S(1)}, u32[]{:S(2)}, u32[]{:S(2)}) collective-permute-start(bf16[1024,256]{0,1:T(8,128)(2,1)S(1)} %fusion.1), channel_id=1, source_target_pairs={{0,2},{1,3},{2,0},{3,1},{4,6},{5,7},{6,4},{7,5},{8,10},{9,11},{10,... | collective-permute-start | bytes 1572872 | tf_op jit(solution)/shard_map/ppermute | solution.py:29
  142.8 7.5 %collective-permute-start.46 = (f16[1024,128]{1,0:T(8,128)(2,1)S(1)}, f16[1024,128]{1,0:T(8,128)(2,1)S(1)}, u32[]{:S(2)}, u32[]{:S(2)}) collective-permute-start(f16[1024,128]{1,0:T(8,128)(2,1)S(1)} %get-tuple-element.367), channel_id=1, source_target_pairs={{0,4},{4,0},{8,12},{12,8},{1,5},{5,1},{9,13},{13,9},{2,6},{6,2},{1... | collective-permute-start | bytes 786440 | tf_op jit(solution)/shard_map/ppermute | solution.py:307
  142.8 10.1 %collective-permute-start.47 = (f16[1024,128]{1,0:T(8,128)(2,1)S(1)}, f16[1024,128]{1,0:T(8,128)(2,1)S(1)}, u32[]{:S(2)}, u32[]{:S(2)}) collective-permute-start(f16[1024,128]{1,0:T(8,128)(2,1)S(1)} %get-tuple-element.366), channel_id=1, source_target_pairs={{4,8},{8,4},{5,9},{9,5},{6,10},{10,6},{7,11},{11,7},{20,24},{24,20... | collective-permute-start | bytes 786440 | tf_op jit(solution)/shard_map/ppermute | solution.py:307
  146.0 9.9 %collective-permute-start.48 = (f16[1024,128]{1,0:T(8,128)(2,1)S(1)}, f16[1024,128]{1,0:T(8,128)(2,1)S(1)}, u32[]{:S(2)}, u32[]{:S(2)}) collective-permute-start(f16[1024,128]{1,0:T(8,128)(2,1)S(1)} %get-tuple-element.355), channel_id=1, source_target_pairs={{0,4},{4,0},{8,12},{12,8},{1,5},{5,1},{9,13},{13,9},{2,6},{6,2},{1... | collective-permute-start | bytes 786440 | tf_op jit(solution)/shard_map/ppermute | solution.py:307
  150.3 8.2 %collective-permute-start.49 = (f16[1024,128]{1,0:T(8,128)(2,1)S(1)}, f16[1024,128]{1,0:T(8,128)(2,1)S(1)}, u32[]{:S(2)}, u32[]{:S(2)}) collective-permute-start(f16[1024,128]{1,0:T(8,128)(2,1)S(1)} %get-tuple-element.354), channel_id=1, source_target_pairs={{4,8},{8,4},{5,9},{9,5},{6,10},{10,6},{7,11},{11,7},{20,24},{24,20... | collective-permute-start | bytes 786440 | tf_op jit(solution)/shard_map/ppermute | solution.py:307
  153.6 6.9 %collective-permute-start.50 = (f16[1024,128]{1,0:T(8,128)(2,1)S(1)}, f16[1024,128]{1,0:T(8,128)(2,1)S(1)}, u32[]{:S(2)}, u32[]{:S(2)}) collective-permute-start(f16[1024,128]{1,0:T(8,128)(2,1)S(1)} %get-tuple-element.357), channel_id=1, source_target_pairs={{0,4},{4,0},{8,12},{12,8},{1,5},{5,1},{9,13},{13,9},{2,6},{6,2},{1... | collective-permute-start | bytes 786440 | tf_op jit(solution)/shard_map/ppermute | solution.py:307
  156.0 8.2 %collective-permute-start.51 = (f16[1024,128]{1,0:T(8,128)(2,1)S(1)}, f16[1024,128]{1,0:T(8,128)(2,1)S(1)}, u32[]{:S(2)}, u32[]{:S(2)}) collective-permute-start(f16[1024,128]{1,0:T(8,128)(2,1)S(1)} %get-tuple-element.358), channel_id=1, source_target_pairs={{4,8},{8,4},{5,9},{9,5},{6,10},{10,6},{7,11},{11,7},{20,24},{24,20... | collective-permute-start | bytes 786440 | tf_op jit(solution)/shard_map/ppermute | solution.py:307
  159.2 15.0 %collective-permute-start.60 = (f16[1024,128]{1,0:T(8,128)(2,1)S(1)}, f16[1024,128]{1,0:T(8,128)(2,1)S(1)}, u32[]{:S(2)}, u32[]{:S(2)}) collective-permute-start(f16[1024,128]{1,0:T(8,128)(2,1)S(1)} %get-tuple-element.361), channel_id=1, source_target_pairs={{4,0},{8,12},{5,1},{9,13},{6,2},{10,14},{7,3},{11,15},{20,16},{24,... | collective-permute-start | bytes 786440 | tf_op jit(solution)/shard_map/ppermute | solution.py:307
  160.5 16.5 %collective-permute-start.61 = (f16[1024,128]{1,0:T(8,128)(2,1)S(1)}, f16[1024,128]{1,0:T(8,128)(2,1)S(1)}, u32[]{:S(2)}, u32[]{:S(2)}) collective-permute-start(f16[1024,128]{1,0:T(8,128)(2,1)S(1)} %get-tuple-element.360), channel_id=1, source_target_pairs={{4,8},{8,4},{5,9},{9,5},{6,10},{10,6},{7,11},{11,7},{20,24},{24,20... | collective-permute-start | bytes 786440 | tf_op jit(solution)/shard_map/ppermute | solution.py:307
  168.0 18.7 %collective-permute-start.53 = (bf16[1024,128]{0,1:T(8,128)(2,1)S(1)}, bf16[1024,128]{0,1:T(8,128)(2,1)S(1)}, u32[]{:S(2)}, u32[]{:S(2)}) collective-permute-start(bf16[1024,128]{0,1:T(8,128)(2,1)S(1)} %fusion.2), channel_id=1, source_target_pairs={{0,1},{1,0},{2,3},{3,2},{4,5},{5,4},{6,7},{7,6},{8,9},{9,8},{10,11... | collective-permute-start | bytes 786440 | tf_op jit(solution)/shard_map/ppermute | solution.py:29
  171.5 14.0 %collective-permute-start.55 = (bf16[1024,128]{0,1:T(8,128)(2,1)S(1)}, bf16[1024,128]{0,1:T(8,128)(2,1)S(1)}, u32[]{:S(2)}, u32[]{:S(2)}) collective-permute-start(bf16[1024,128]{0,1:T(8,128)(2,1)S(1)} %fusion.2), channel_id=1, source_target_pairs={{0,2},{1,3},{2,0},{3,1},{4,6},{5,7},{6,4},{7,5},{8,10},{9,11},{10,... | collective-permute-start | bytes 786440 | tf_op jit(solution)/shard_map/ppermute | solution.py:29
  172.0 6.9 %collective-permute-start.62 = (f16[1024,128]{1,0:T(8,128)(2,1)S(1)}, f16[1024,128]{1,0:T(8,128)(2,1)S(1)}, u32[]{:S(2)}, u32[]{:S(2)}) collective-permute-start(f16[1024,128]{1,0:T(8,128)(2,1)S(1)} %get-tuple-element.364), channel_id=1, source_target_pairs={{4,0},{8,12},{5,1},{9,13},{6,2},{10,14},{7,3},{11,15},{20,16},{24,... | collective-permute-start | bytes 786440 | tf_op jit(solution)/shard_map/ppermute | solution.py:307
  174.2 9.4 %collective-permute-start.63 = (f16[1024,128]{1,0:T(8,128)(2,1)S(1)}, f16[1024,128]{1,0:T(8,128)(2,1)S(1)}, u32[]{:S(2)}, u32[]{:S(2)}) collective-permute-start(f16[1024,128]{1,0:T(8,128)(2,1)S(1)} %get-tuple-element.363), channel_id=1, source_target_pairs={{4,8},{8,4},{5,9},{9,5},{6,10},{10,6},{7,11},{11,7},{20,24},{24,20... | collective-permute-start | bytes 786440 | tf_op jit(solution)/shard_map/ppermute | solution.py:307
  177.0 11.0 %collective-permute-start.56 = (bf16[1024,256]{0,1:T(8,128)(2,1)S(1)}, bf16[1024,256]{0,1:T(8,128)(2,1)S(1)}, u32[]{:S(2)}, u32[]{:S(2)}) collective-permute-start(bf16[1024,256]{0,1:T(8,128)(2,1)S(1)} %collective-permute-done.54), channel_id=1, source_target_pairs={{0,1},{1,0},{2,3},{3,2},{4,5},{5,4},{6,7},{7,6},{8,9},{9,8},{10,11... | collective-permute-start | bytes 1572872 | tf_op jit(solution)/shard_map/ppermute | solution.py:29
  178.9 9.7 %collective-permute-start.64 = (f16[1024,128]{1,0:T(8,128)(2,1)S(1)}, f16[1024,128]{1,0:T(8,128)(2,1)S(1)}, u32[]{:S(2)}, u32[]{:S(2)}) collective-permute-start(f16[1024,128]{1,0:T(8,128)(2,1)S(1)} %get-tuple-element.346), channel_id=1, source_target_pairs={{4,0},{8,12},{5,1},{9,13},{6,2},{10,14},{7,3},{11,15},{20,16},{24,... | collective-permute-start | bytes 786440 | tf_op jit(solution)/shard_map/ppermute | solution.py:307
  184.2 9.2 %collective-permute-start.65 = (f16[1024,128]{1,0:T(8,128)(2,1)S(1)}, f16[1024,128]{1,0:T(8,128)(2,1)S(1)}, u32[]{:S(2)}, u32[]{:S(2)}) collective-permute-start(f16[1024,128]{1,0:T(8,128)(2,1)S(1)} %get-tuple-element.348), channel_id=1, source_target_pairs={{4,0},{8,12},{5,1},{9,13},{6,2},{10,14},{7,3},{11,15},{20,16},{24,... | collective-permute-start | bytes 786440 | tf_op jit(solution)/shard_map/ppermute | solution.py:307
  197.3 13.0 %collective-permute-start.69 = (bf16[1024,128]{0,1:T(8,128)(2,1)S(1)}, bf16[1024,128]{0,1:T(8,128)(2,1)S(1)}, u32[]{:S(2)}, u32[]{:S(2)}) collective-permute-start(bf16[1024,128]{0,1:T(8,128)(2,1)S(1)} %bitcast.118), channel_id=1, source_target_pairs={{0,2},{1,3},{2,0},{3,1},{4,6},{5,7},{6,4},{7,5},{8,10},{9,11},{10,... | collective-permute-start | bytes 786440 | tf_op jit(solution)/shard_map/ppermute | solution.py:29
  198.4 13.4 %collective-permute-start.68 = (bf16[1024,128]{0,1:T(8,128)(2,1)S(1)}, bf16[1024,128]{0,1:T(8,128)(2,1)S(1)}, u32[]{:S(2)}, u32[]{:S(2)}) collective-permute-start(bf16[1024,128]{0,1:T(8,128)(2,1)S(1)} %bitcast.119), channel_id=1, source_target_pairs={{0,1},{1,0},{2,3},{3,2},{4,5},{5,4},{6,7},{7,6},{8,9},{9,8},{10,11... | collective-permute-start | bytes 786440 | tf_op jit(solution)/shard_map/ppermute | solution.py:29
  202.1 7.5 %collective-permute-start.66 = (bf16[2,384,128]{1,2,0:T(8,128)(2,1)S(1)}, bf16[2,384,128]{1,2,0:T(8,128)(2,1)S(1)}, u32[]{:S(2)}, u32[]{:S(2)}) collective-permute-start(bf16[2,384,128]{1,2,0:T(8,128)(2,1)S(1)} %pad_maximum_fusion.9), channel_id=1, source_target_pairs={{0,4},{4,0},{8,12},{12,8},{1,5},{5,1},{9,13},{13,9},{2,6},{6,2},{1... | collective-permute-start | bytes 589832 | tf_op jit(solution)/shard_map/ppermute | solution.py:409
  204.8 17.5 %collective-permute-start.58 = (bf16[2,384,384]{1,2,0:T(8,128)(2,1)S(1)}, bf16[2,384,384]{1,2,0:T(8,128)(2,1)S(1)}, u32[]{:S(2)}, u32[]{:S(2)}) collective-permute-start(bf16[2,384,384]{1,2,0:T(8,128)(2,1)S(1)} %pad_maximum_fusion.7), channel_id=1, source_target_pairs={{0,4},{4,0},{8,12},{12,8},{1,5},{5,1},{9,13},{13,9},{2,6},{6,2},{1... | collective-permute-start | bytes 1769480 | tf_op jit(solution)/shard_map/ppermute | solution.py:409
  209.7 13.4 %collective-permute-start.67 = (bf16[384,128]{0,1:T(8,128)(2,1)S(1)}, bf16[384,128]{0,1:T(8,128)(2,1)S(1)}, u32[]{:S(2)}, u32[]{:S(2)}) collective-permute-start(bf16[384,128]{0,1:T(8,128)(2,1)S(1)} %fusion.6), channel_id=1, source_target_pairs={{0,12},{4,8},{8,4},{12,0},{1,13},{5,9},{9,5},{13,1},{2,14},{6,10},... | collective-permute-start | bytes 294920 | tf_op jit(solution)/shard_map/ppermute | solution.py:411
  213.2 16.9 %collective-permute-start.71 = (bf16[2,128,512]{1,2,0:T(8,128)(2,1)S(1)}, bf16[2,128,512]{1,2,0:T(8,128)(2,1)S(1)}, u32[]{:S(2)}, u32[]{:S(2)}) collective-permute-start(bf16[2,128,512]{1,2,0:T(8,128)(2,1)S(1)} %pad_maximum_fusion.8), channel_id=1, source_target_pairs={{0,4},{4,0},{8,12},{12,8},{1,5},{5,1},{9,13},{13,9},{2,6},{6,2},{1... | collective-permute-start | bytes 786440 | tf_op jit(solution)/shard_map/ppermute | solution.py:409
  222.4 8.4 %collective-permute-start.59 = (bf16[384,384]{0,1:T(8,128)(2,1)S(1)}, bf16[384,384]{0,1:T(8,128)(2,1)S(1)}, u32[]{:S(2)}, u32[]{:S(2)}) collective-permute-start(bf16[384,384]{0,1:T(8,128)(2,1)S(1)} %fusion.3), channel_id=1, source_target_pairs={{0,12},{4,8},{8,4},{12,0},{1,13},{5,9},{9,5},{13,1},{2,14},{6,10},... | collective-permute-start | bytes 884744 | tf_op jit(solution)/shard_map/ppermute | solution.py:411
  230.1 12.6 %collective-permute-start.72 = (bf16[128,512]{0,1:T(8,128)(2,1)S(1)}, bf16[128,512]{0,1:T(8,128)(2,1)S(1)}, u32[]{:S(2)}, u32[]{:S(2)}) collective-permute-start(bf16[128,512]{0,1:T(8,128)(2,1)S(1)} %fusion.5), channel_id=1, source_target_pairs={{0,12},{4,8},{8,4},{12,0},{1,13},{5,9},{9,5},{13,1},{2,14},{6,10},... | collective-permute-start | bytes 393224 | tf_op jit(solution)/shard_map/ppermute | solution.py:411
  (11 other events, 52.7 us)

commit v2 on v1

--- a/solution.py
+++ b/solution.py
@@ -429,7 +429,7 @@
         return own
 
     def at_step(steps_left):
-        if "terms" in blocks and "corner" not in blocks and steps_left <= 3:
+        if "terms" in blocks and "corner" not in blocks and steps_left <= 4:
             blocks["corner"], blocks["corner_sent"] = scatter(blocks["terms"])
             return list(blocks["terms"])
         return []

time: 247 us -> 238 us (0.964)
  waiting for transfers between devices: 77.8 us -> 71.4 us
    ppermute x3, waiting for transfers between devices: 18.2 us -> 11.4 us  [scatter(): near = lax.ppermute(sent, 'aux', flipped(planes, 1))]
    ppermute x36, starting transfers between devices: 59.1 us -> 54.7 us  [all_planes(): lax.ppermute(p, 'aux', pairs)]
    ppermute x3, starting transfers between devices: 4.97 us -> 7.7 us  [scatter(): near = lax.ppermute(sent, 'aux', flipped(planes, 1))]
  transfers between devices with their start and end apart: 67 -> 67, of which waited for: 35 -> 36; matrix products, arithmetic and copies ran while one was open for 12% -> 14% of each run, Pallas kernels for 2% -> 2%
where the time goes in v2:
time: 238 us; the launch traced here: 237 us
  starting transfers between devices  101 us (42%)
  waiting for transfers between devices  71.4 us (30%)
  other arithmetic  21.6 us (9%)
  Pallas kernels  15.7 us (7%)
  matrix products  13.8 us (6%)
  local copies, waits for them, and re-layouts  7.21 us (3%)
  between operations  6.25 us (3%)
    ppermute x36, starting transfers between devices, all_planes(): lax.ppermute(p, 'aux', pairs)  54.7 us
    ppermute x36, waiting for transfers between devices, all_planes(): lax.ppermute(p, 'aux', pairs)  35.4 us
    ppermute x15, starting transfers between devices, over_members(): lax.ppermute(a, axis, flipped(size, bit))  24.1 us
    ppermute x3, waiting for transfers between devices, scatter(): lax.ppermute(far, 'aux', flipped(planes, planes - 1))  12.8 us
    pallas_call x1, Pallas kernels, spread(): pl.pallas_call(functools.partial(spread_kernel, planes, across, cap), out...  11.7 us
    ppermute x3, waiting for transfers between devices, scatter(): near = lax.ppermute(sent, 'aux', flipped(planes, 1))  11.4 us
    dot_general x3, matrix products, consume(): jnp.dot(fit_rows, rounded, preferred_element_type=jnp.float32)  8.18 us
    select_n x9, other arithmetic, payloads(): return (jnp.where(even, right, left), jnp.where(even, left, right))  7.7 us
  transfers between devices with their start and end apart: 67, of which 36 were waited for; matrix products, arithmetic and copies ran while one was open for 14% of the time, Pallas kernels for 2%

profile of v2, /device:TPU:13, one launch (start us, length us, event | category | flops | bytes accessed | tf_op | source)
XLA Modules:
  0.0 236.6 jit_solution(5956923315672513903)
XLA Ops:
  4.0 1.2 constant_dynamic-slice_fusion.3
  5.2 1.3 collective-permute-start.6
  7.9 4.0 %shard_map.64 = f32[2,16,128]{2,1,0:T(8,128)S(1)} custom-call(bf16[64,128,128]{2,1,0:T(8,128)(2,1)} %own_tiles.1, bf16[7680,512]{1,0:T(8,128)(2,1)} %refs_13_.1), custom_call_target="tpu_custom_call" | custom-call | bytes 10485760 | tf_op jit(solution)/shard_map/pallas_call | solution.py:217
  11.9 2.1 collective-permute-start.7
  16.4 1.6 collective-permute-start.10
  18.0 6.2 %collective-permute-done.9 = f32[2,128]{1,0:T(2,128)S(1)} collective-permute-done((f32[2,128]{1,0:T(2,128)S(1)}, f32[2,128]{1,0:T(2,128)S(1)}, u32[]{:S(2)}, u32[]{:S(2)}) %collective-permute-start.9) | collective-permute-done | bytes 1056 | tf_op jit(solution)/shard_map/ppermute | solution.py:350
  25.1 1.5 collective-permute-start.12
  31.2 2.0 collective-permute-start.15
  34.2 2.0 collective-permute-start.16
  36.8 2.1 collective-permute-done.18.refs_8_
  38.9 2.4 %collective-permute-start.21 = (bf16[7,128,128]{2,1,0:T(8,128)(2,1)}, bf16[7,128,128]{2,1,0:T(8,128)(2,1)S(1)}, u32[]{:S(2)}, u32[]{:S(2)}) collective-permute-start(bf16[7,128,128]{2,1,0:T(8,128)(2,1)} %collective-permute-done.18.refs_8_), channel_id=1, source_target_pairs={{0,1},{1,0},{2,3},{3,2},{4,5},{5,4},{6,7},{7,6},{8,9},{9,8},{10,11... | collective-permute-start | bytes 688136 | tf_op jit(solution)/shard_map/ppermute | solution.py:29
  44.1 11.7 %shard_map.66 = f32[4,4096,128]{2,1,0:T(8,128)} custom-call(s32[3]{0:T(128)S(1)} %pad_add_fusion.place, s32[4,64]{1,0:T(4,128)S(1)} %copy-done.1, s32[4,64]{1,0:T(4,128)S(1)} %copy-done, s32[4,4]{1,0:T(4,128)S(1)} %get-tuple-element.327.begins, s32[4,4]{1,0:T(4,128)S(1)} %get-tuple-element.326.counts, bf16[64,128,128]{2,1,0:T(8,128)(2,1)} %get-tuple-element.578, ...), custom_call_target="tpu_custom_call" | custom-call | flops 1073741824 | bytes 25165824 | tf_op jit(solution)/shard_map/pallas_call | solution.py:156
  55.8 2.0 broadcast_select_fusion.39
  57.8 1.3 collective-permute-start.22
  59.2 1.3 collective-permute-start.25
  60.5 7.1 %collective-permute-done.22 = f16[1024,128]{1,0:T(8,128)(2,1)S(1)} collective-permute-done((f16[1024,128]{1,0:T(8,128)(2,1)S(1)}, f16[1024,128]{1,0:T(8,128)(2,1)S(1)}, u32[]{:S(2)}, u32[]{:S(2)}) %collective-permute-start.22) | collective-permute-done | bytes 262176 | tf_op jit(solution)/shard_map/ppermute | solution.py:307
  67.7 1.8 broadcast_select_fusion.35
  69.6 1.6 collective-permute-start.23
  71.1 2.2 collective-permute-start.24
  73.3 1.6 broadcast_select_fusion.33
  74.9 1.3 collective-permute-start.28
  76.3 3.1 %collective-permute-start.29 = (f16[1024,128]{1,0:T(8,128)(2,1)S(1)}, f16[1024,128]{1,0:T(8,128)(2,1)S(1)}, u32[]{:S(2)}, u32[]{:S(2)}) collective-permute-start(f16[1024,128]{1,0:T(8,128)(2,1)S(1)} %broadcast_select_fusion.32), channel_id=1, source_target_pairs={{4,8},{8,4},{5,9},{9,5},{6,10},{10,6},{7,11},{11,7},{20,24},{24,20... | collective-permute-start | bytes 786440 | tf_op jit(solution)/shard_map/ppermute | solution.py:307
  79.6 1.6 broadcast_select_fusion.29
  81.4 2.6 %collective-permute-start.27 = (f16[1024,128]{1,0:T(8,128)(2,1)S(1)}, f16[1024,128]{1,0:T(8,128)(2,1)S(1)}, u32[]{:S(2)}, u32[]{:S(2)}) collective-permute-start(f16[1024,128]{1,0:T(8,128)(2,1)S(1)} %get-tuple-element.392), channel_id=1, source_target_pairs={{4,8},{8,4},{5,9},{9,5},{6,10},{10,6},{7,11},{11,7},{20,24},{24,20... | collective-permute-start | bytes 786440 | tf_op jit(solution)/shard_map/ppermute | solution.py:307
  86.4 1.9 collective-permute-start.31
  88.3 1.6 collective-permute-done.26
  91.2 3.2 %collective-permute-start.33 = (f16[1024,128]{1,0:T(8,128)(2,1)S(1)}, f16[1024,128]{1,0:T(8,128)(2,1)S(1)}, u32[]{:S(2)}, u32[]{:S(2)}) collective-permute-start(f16[1024,128]{1,0:T(8,128)(2,1)S(1)} %get-tuple-element.387), channel_id=1, source_target_pairs={{4,8},{8,4},{5,9},{9,5},{6,10},{10,6},{7,11},{11,7},{20,24},{24,20... | collective-permute-start | bytes 786440 | tf_op jit(solution)/shard_map/ppermute | solution.py:307
  97.4 2.7 %collective-permute-start.35 = (f16[1024,128]{1,0:T(8,128)(2,1)S(1)}, f16[1024,128]{1,0:T(8,128)(2,1)S(1)}, u32[]{:S(2)}, u32[]{:S(2)}) collective-permute-start(f16[1024,128]{1,0:T(8,128)(2,1)S(1)} %get-tuple-element.385), channel_id=1, source_target_pairs={{4,8},{8,4},{5,9},{9,5},{6,10},{10,6},{7,11},{11,7},{20,24},{24,20... | collective-permute-start | bytes 786440 | tf_op jit(solution)/shard_map/ppermute | solution.py:307
  102.4 2.7 %collective-permute-start.37 = (f16[1024,128]{1,0:T(8,128)(2,1)S(1)}, f16[1024,128]{1,0:T(8,128)(2,1)S(1)}, u32[]{:S(2)}, u32[]{:S(2)}) collective-permute-start(f16[1024,128]{1,0:T(8,128)(2,1)S(1)} %get-tuple-element.381), channel_id=1, source_target_pairs={{4,8},{8,4},{5,9},{9,5},{6,10},{10,6},{7,11},{11,7},{20,24},{24,20... | collective-permute-start | bytes 786440 | tf_op jit(solution)/shard_map/ppermute | solution.py:307
  105.1 1.5 collective-permute-done.34
  108.0 2.7 %collective-permute-start.39 = (f16[1024,128]{1,0:T(8,128)(2,1)S(1)}, f16[1024,128]{1,0:T(8,128)(2,1)S(1)}, u32[]{:S(2)}, u32[]{:S(2)}) collective-permute-start(f16[1024,128]{1,0:T(8,128)(2,1)S(1)} %get-tuple-element.378), channel_id=1, source_target_pairs={{4,8},{8,4},{5,9},{9,5},{6,10},{10,6},{7,11},{11,7},{20,24},{24,20... | collective-permute-start | bytes 786440 | tf_op jit(solution)/shard_map/ppermute | solution.py:307
  110.7 1.2 collective-permute-done.36
  113.4 2.9 %collective-permute-start.41 = (f16[1024,128]{1,0:T(8,128)(2,1)S(1)}, f16[1024,128]{1,0:T(8,128)(2,1)S(1)}, u32[]{:S(2)}, u32[]{:S(2)}) collective-permute-start(f16[1024,128]{1,0:T(8,128)(2,1)S(1)} %get-tuple-element.375), channel_id=1, source_target_pairs={{4,8},{8,4},{5,9},{9,5},{6,10},{10,6},{7,11},{11,7},{20,24},{24,20... | collective-permute-start | bytes 786440 | tf_op jit(solution)/shard_map/ppermute | solution.py:307
  118.6 2.7 %collective-permute-start.43 = (f16[1024,128]{1,0:T(8,128)(2,1)S(1)}, f16[1024,128]{1,0:T(8,128)(2,1)S(1)}, u32[]{:S(2)}, u32[]{:S(2)}) collective-permute-start(f16[1024,128]{1,0:T(8,128)(2,1)S(1)} %get-tuple-element.373), channel_id=1, source_target_pairs={{4,8},{8,4},{5,9},{9,5},{6,10},{10,6},{7,11},{11,7},{20,24},{24,20... | collective-permute-start | bytes 786440 | tf_op jit(solution)/shard_map/ppermute | solution.py:307
  121.4 1.2 collective-permute-done.40
  124.2 2.7 %collective-permute-start.45 = (f16[1024,128]{1,0:T(8,128)(2,1)S(1)}, f16[1024,128]{1,0:T(8,128)(2,1)S(1)}, u32[]{:S(2)}, u32[]{:S(2)}) collective-permute-start(f16[1024,128]{1,0:T(8,128)(2,1)S(1)} %get-tuple-element.369), channel_id=1, source_target_pairs={{4,8},{8,4},{5,9},{9,5},{6,10},{10,6},{7,11},{11,7},{20,24},{24,20... | collective-permute-start | bytes 786440 | tf_op jit(solution)/shard_map/ppermute | solution.py:307
  131.1 1.4 slice-done.1
  132.5 2.4 %fusion.1 = bf16[1024,256]{0,1:T(8,128)(2,1)S(1)} fusion(bf16[4096,256]{1,0:T(8,128)(2,1)S(1)} %pad_maximum_fusion.1, bf16[1024,4096]{1,0:T(8,128)(2,1)S(1)} %bitcast.114), kind=kOutput, calls=%fused_computation.14 | convolution fusion | flops 2147745792 | bytes 11010048 | tf_op jit(solution)/shard_map/dot_general | solution.py:419
  134.9 6.3 %collective-permute-start.52 = (bf16[1024,256]{0,1:T(8,128)(2,1)S(1)}, bf16[1024,256]{0,1:T(8,128)(2,1)S(1)}, u32[]{:S(2)}, u32[]{:S(2)}) collective-permute-start(bf16[1024,256]{0,1:T(8,128)(2,1)S(1)} %fusion.1), channel_id=1, source_target_pairs={{0,1},{1,0},{2,3},{3,2},{4,5},{5,4},{6,7},{7,6},{8,9},{9,8},{10,11... | collective-permute-start | bytes 1572872 | tf_op jit(solution)/shard_map/ppermute | solution.py:29
  142.2 2.7 %collective-permute-start.47 = (f16[1024,128]{1,0:T(8,128)(2,1)S(1)}, f16[1024,128]{1,0:T(8,128)(2,1)S(1)}, u32[]{:S(2)}, u32[]{:S(2)}) collective-permute-start(f16[1024,128]{1,0:T(8,128)(2,1)S(1)} %get-tuple-element.366), channel_id=1, source_target_pairs={{4,8},{8,4},{5,9},{9,5},{6,10},{10,6},{7,11},{11,7},{20,24},{24,20... | collective-permute-start | bytes 786440 | tf_op jit(solution)/shard_map/ppermute | solution.py:307
  145.6 4.1 %collective-permute-done.46 = f16[1024,128]{1,0:T(8,128)(2,1)S(1)} collective-permute-done((f16[1024,128]{1,0:T(8,128)(2,1)S(1)}, f16[1024,128]{1,0:T(8,128)(2,1)S(1)}, u32[]{:S(2)}, u32[]{:S(2)}) %collective-permute-start.46) | collective-permute-done | bytes 262176 | tf_op jit(solution)/shard_map/ppermute | solution.py:307
  149.7 2.7 %collective-permute-start.49 = (f16[1024,128]{1,0:T(8,128)(2,1)S(1)}, f16[1024,128]{1,0:T(8,128)(2,1)S(1)}, u32[]{:S(2)}, u32[]{:S(2)}) collective-permute-start(f16[1024,128]{1,0:T(8,128)(2,1)S(1)} %get-tuple-element.354), channel_id=1, source_target_pairs={{4,8},{8,4},{5,9},{9,5},{6,10},{10,6},{7,11},{11,7},{20,24},{24,20... | collective-permute-start | bytes 786440 | tf_op jit(solution)/shard_map/ppermute | solution.py:307
  153.1 2.2 collective-permute-done.48
  155.4 2.7 %collective-permute-start.51 = (f16[1024,128]{1,0:T(8,128)(2,1)S(1)}, f16[1024,128]{1,0:T(8,128)(2,1)S(1)}, u32[]{:S(2)}, u32[]{:S(2)}) collective-permute-start(f16[1024,128]{1,0:T(8,128)(2,1)S(1)} %get-tuple-element.358), channel_id=1, source_target_pairs={{4,8},{8,4},{5,9},{9,5},{6,10},{10,6},{7,11},{11,7},{20,24},{24,20... | collective-permute-start | bytes 786440 | tf_op jit(solution)/shard_map/ppermute | solution.py:307
  158.7 1.3 collective-permute-start.60
  160.0 2.6 %collective-permute-start.61 = (f16[1024,128]{1,0:T(8,128)(2,1)S(1)}, f16[1024,128]{1,0:T(8,128)(2,1)S(1)}, u32[]{:S(2)}, u32[]{:S(2)}) collective-permute-start(f16[1024,128]{1,0:T(8,128)(2,1)S(1)} %get-tuple-element.360), channel_id=1, source_target_pairs={{4,8},{8,4},{5,9},{9,5},{6,10},{10,6},{7,11},{11,7},{20,24},{24,20... | collective-permute-start | bytes 786440 | tf_op jit(solution)/shard_map/ppermute | solution.py:307
  164.6 2.9 %fusion.2 = bf16[1024,128]{0,1:T(8,128)(2,1)S(1)} fusion(bf16[4096,128]{1,0:T(8,128)(2,1)S(1)} %multiply_convert_fusion.2, bf16[1024,4096]{1,0:T(8,128)(2,1)S(1)} %bitcast.114), kind=kOutput, calls=%fused_computation.21 | convolution fusion | flops 1073872896 | bytes 9699328 | tf_op jit(solution)/shard_map/dot_general | solution.py:419
  167.5 3.3 %collective-permute-start.53 = (bf16[1024,128]{0,1:T(8,128)(2,1)S(1)}, bf16[1024,128]{0,1:T(8,128)(2,1)S(1)}, u32[]{:S(2)}, u32[]{:S(2)}) collective-permute-start(bf16[1024,128]{0,1:T(8,128)(2,1)S(1)} %fusion.2), channel_id=1, source_target_pairs={{0,1},{1,0},{2,3},{3,2},{4,5},{5,4},{6,7},{7,6},{8,9},{9,8},{10,11... | collective-permute-start | bytes 786440 | tf_op jit(solution)/shard_map/ppermute | solution.py:29
  171.4 1.5 collective-permute-start.62
  173.5 2.8 %collective-permute-start.63 = (f16[1024,128]{1,0:T(8,128)(2,1)S(1)}, f16[1024,128]{1,0:T(8,128)(2,1)S(1)}, u32[]{:S(2)}, u32[]{:S(2)}) collective-permute-start(f16[1024,128]{1,0:T(8,128)(2,1)S(1)} %get-tuple-element.363), channel_id=1, source_target_pairs={{4,8},{8,4},{5,9},{9,5},{6,10},{10,6},{7,11},{11,7},{20,24},{24,20... | collective-permute-start | bytes 786440 | tf_op jit(solution)/shard_map/ppermute | solution.py:307
  178.7 1.3 collective-permute-start.64
  183.5 1.3 collective-permute-start.65
  185.4 2.3 collective-permute-start.58
  188.1 2.9 %collective-permute-done.65 = f16[1024,128]{1,0:T(8,128)(2,1)S(1)} collective-permute-done((f16[1024,128]{1,0:T(8,128)(2,1)S(1)}, f16[1024,128]{1,0:T(8,128)(2,1)S(1)}, u32[]{:S(2)}, u32[]{:S(2)}) %collective-permute-start.65) | collective-permute-done | bytes 262176 | tf_op jit(solution)/shard_map/ppermute | solution.py:307
  191.7 2.9 %convolution_convert_fusion.1 = bf16[128,1024]{1,0:T(8,128)(2,1)S(1)} fusion(bf16[4096,128]{1,0:T(8,128)(2,1)S(1)} %multiply_convert_fusion.1, bf16[1024,4096]{1,0:T(8,128)(2,1)S(1)} %bitcast.114), kind=kOutput, calls=%fused_computation.15 | convolution fusion | flops 1073872896 | bytes 9699328 | tf_op jit(solution)/shard_map/dot_general | solution.py:419
  194.7 3.0 %collective-permute-start.68 = (bf16[1024,128]{0,1:T(8,128)(2,1)S(1)}, bf16[1024,128]{0,1:T(8,128)(2,1)S(1)}, u32[]{:S(2)}, u32[]{:S(2)}) collective-permute-start(bf16[1024,128]{0,1:T(8,128)(2,1)S(1)} %bitcast.119), channel_id=1, source_target_pairs={{0,1},{1,0},{2,3},{3,2},{4,5},{5,4},{6,7},{7,6},{8,9},{9,8},{10,11... | collective-permute-start | bytes 786440 | tf_op jit(solution)/shard_map/ppermute | solution.py:29
  199.3 2.3 collective-permute-start.66
  202.1 5.8 %collective-permute-done.66 = bf16[2,384,128]{1,2,0:T(8,128)(2,1)S(1)} collective-permute-done((bf16[2,384,128]{1,2,0:T(8,128)(2,1)S(1)}, bf16[2,384,128]{1,2,0:T(8,128)(2,1)S(1)}, u32[]{:S(2)}, u32[]{:S(2)}) %collective-permute-start.66) | collective-permute-done | bytes 196640 | tf_op jit(solution)/shard_map/ppermute | solution.py:409
  208.8 1.4 collective-permute-start.70
  212.0 3.2 %collective-permute-start.71 = (bf16[2,128,512]{1,2,0:T(8,128)(2,1)S(1)}, bf16[2,128,512]{1,2,0:T(8,128)(2,1)S(1)}, u32[]{:S(2)}, u32[]{:S(2)}) collective-permute-start(bf16[2,128,512]{1,2,0:T(8,128)(2,1)S(1)} %pad_maximum_fusion.8), channel_id=1, source_target_pairs={{0,4},{4,0},{8,12},{12,8},{1,5},{5,1},{9,13},{13,9},{2,6},{6,2},{1... | collective-permute-start | bytes 786440 | tf_op jit(solution)/shard_map/ppermute | solution.py:409
  215.9 5.6 %collective-permute-done.71 = bf16[2,128,512]{1,2,0:T(8,128)(2,1)S(1)} collective-permute-done((bf16[2,128,512]{1,2,0:T(8,128)(2,1)S(1)}, bf16[2,128,512]{1,2,0:T(8,128)(2,1)S(1)}, u32[]{:S(2)}, u32[]{:S(2)}) %collective-permute-start.71) | collective-permute-done | bytes 262176 | tf_op jit(solution)/shard_map/ppermute | solution.py:409
  222.2 10.1 %collective-permute-done.59 = bf16[384,384]{0,1:T(8,128)(2,1)S(1)} collective-permute-done((bf16[384,384]{0,1:T(8,128)(2,1)S(1)}, bf16[384,384]{0,1:T(8,128)(2,1)S(1)}, u32[]{:S(2)}, u32[]{:S(2)}) %collective-permute-start.59) | collective-permute-done | bytes 294944 | tf_op jit(solution)/shard_map/ppermute | solution.py:411
  232.4 2.7 %collective-permute-done.72 = bf16[128,512]{0,1:T(8,128)(2,1)S(1)} collective-permute-done((bf16[128,512]{0,1:T(8,128)(2,1)S(1)}, bf16[128,512]{0,1:T(8,128)(2,1)S(1)}, u32[]{:S(2)}, u32[]{:S(2)}) %collective-permute-start.72) | collective-permute-done | bytes 131104 | tf_op jit(solution)/shard_map/ppermute | solution.py:411
  235.3 1.3 copy.16
  (185 shorter events, 52.8 us)
Async XLA Ops:
  5.2 6.8 %collective-permute-start.6 = (bf16[7,128,128]{2,1,0:T(8,128)(2,1)S(1)}, bf16[7,128,128]{2,1,0:T(8,128)(2,1)S(1)}, u32[]{:S(2)}, u32[]{:S(2)}) collective-permute-start(bf16[7,128,128]{2,1,0:T(8,128)(2,1)S(1)} %get-tuple-element.266), channel_id=1, source_target_pairs={{0,4},{4,8},{8,12},{12,0},{1,5},{5,9},{9,13},{13,1},{2,6},{6,10},{... | collective-permute-start | bytes 688136 | tf_op jit(solution)/shard_map/ppermute | solution.py:360
  11.9 13.2 %collective-permute-start.7 = (bf16[7,128,128]{2,1,0:T(8,128)(2,1)S(1)}, bf16[7,128,128]{2,1,0:T(8,128)(2,1)S(1)}, u32[]{:S(2)}, u32[]{:S(2)}) collective-permute-start(bf16[7,128,128]{2,1,0:T(8,128)(2,1)S(1)} %get-tuple-element.269), channel_id=1, source_target_pairs={{0,8},{4,12},{8,0},{12,4},{1,9},{5,13},{9,1},{13,5},{2,10},{6,14},... | collective-permute-start | bytes 688136 | tf_op jit(solution)/shard_map/ppermute | solution.py:363
  14.0 11.1 %collective-permute-start.8 = (bf16[7,128,128]{2,1,0:T(8,128)(2,1)S(1)}, bf16[7,128,128]{2,1,0:T(8,128)(2,1)S(1)}, u32[]{:S(2)}, u32[]{:S(2)}) collective-permute-start(bf16[7,128,128]{2,1,0:T(8,128)(2,1)S(1)} %collective-permute-done.6.refs_0_), channel_id=1, source_target_pairs={{0,2},{1,3},{2,0},{3,1},{4,6},{5,7},{6,4},{7,5},{8,10},{9,11},{10,... | collective-permute-start | bytes 688136 | tf_op jit(solution)/shard_map/ppermute | solution.py:364
  15.4 8.7 %collective-permute-start.9 = (f32[2,128]{1,0:T(2,128)S(1)}, f32[2,128]{1,0:T(2,128)S(1)}, u32[]{:S(2)}, u32[]{:S(2)}) collective-permute-start(f32[2,128]{1,0:T(2,128)S(1)} %broadcast_in_dim.77), channel_id=1, source_target_pairs={{0,4},{4,8},{8,12},{12,0},{1,5},{5,9},{9,13},{13,1},{2,6},{6,10},{... | collective-permute-start | bytes 3080 | tf_op jit(solution)/shard_map/ppermute | solution.py:350
  16.4 7.8 %collective-permute-start.10 = (f32[2,128]{1,0:T(2,128)S(1)}, f32[2,128]{1,0:T(2,128)S(1)}, u32[]{:S(2)}, u32[]{:S(2)}) collective-permute-start(f32[2,128]{1,0:T(2,128)S(1)} %broadcast_in_dim.77), channel_id=1, source_target_pairs={{0,8},{4,12},{8,0},{12,4},{1,9},{5,13},{9,1},{13,5},{2,10},{6,14},... | collective-permute-start | bytes 3080 | tf_op jit(solution)/shard_map/ppermute | solution.py:350
  18.0 7.2 %collective-permute-start.11 = (f32[2,128]{1,0:T(2,128)S(1)}, f32[2,128]{1,0:T(2,128)S(1)}, u32[]{:S(2)}, u32[]{:S(2)}) collective-permute-start(f32[2,128]{1,0:T(2,128)S(1)} %broadcast_in_dim.77), channel_id=1, source_target_pairs={{0,12},{4,0},{8,4},{12,8},{1,13},{5,1},{9,5},{13,9},{2,14},{6,2},{... | collective-permute-start | bytes 3080 | tf_op jit(solution)/shard_map/ppermute | solution.py:350
  25.1 8.0 %collective-permute-start.12 = (bf16[7,128,128]{2,1,0:T(8,128)(2,1)S(1)}, bf16[7,128,128]{2,1,0:T(8,128)(2,1)S(1)}, u32[]{:S(2)}, u32[]{:S(2)}) collective-permute-start(bf16[7,128,128]{2,1,0:T(8,128)(2,1)S(1)} %get-tuple-element.272), channel_id=1, source_target_pairs={{0,12},{4,0},{8,4},{12,8},{1,13},{5,1},{9,5},{13,9},{2,14},{6,2},{... | collective-permute-start | bytes 688136 | tf_op jit(solution)/shard_map/ppermute | solution.py:366
  26.7 6.5 %collective-permute-start.13 = (bf16[7,128,128]{2,1,0:T(8,128)(2,1)S(1)}, bf16[7,128,128]{2,1,0:T(8,128)(2,1)S(1)}, u32[]{:S(2)}, u32[]{:S(2)}) collective-permute-start(bf16[7,128,128]{2,1,0:T(8,128)(2,1)S(1)} %collective-permute-done.7.refs_1_), channel_id=1, source_target_pairs={{0,2},{1,3},{2,0},{3,1},{4,6},{5,7},{6,4},{7,5},{8,10},{9,11},{10,... | collective-permute-start | bytes 688136 | tf_op jit(solution)/shard_map/ppermute | solution.py:367
  31.2 5.5 %collective-permute-start.15 = (bf16[7,128,128]{2,1,0:T(8,128)(2,1)S(1)}, bf16[7,128,128]{2,1,0:T(8,128)(2,1)S(1)}, u32[]{:S(2)}, u32[]{:S(2)}) collective-permute-start(bf16[7,128,128]{2,1,0:T(8,128)(2,1)S(1)} %collective-permute-done.6.refs_0_), channel_id=1, source_target_pairs={{0,1},{1,0},{2,3},{3,2},{4,5},{5,4},{6,7},{7,6},{8,9},{9,8},{10,11... | collective-permute-start | bytes 688136 | tf_op jit(solution)/shard_map/ppermute | solution.py:29
  33.2 5.7 %collective-permute-start.18 = (bf16[7,128,128]{2,1,0:T(8,128)(2,1)S(1)}, bf16[7,128,128]{2,1,0:T(8,128)(2,1)}, u32[]{:S(2)}, u32[]{:S(2)}) collective-permute-start(bf16[7,128,128]{2,1,0:T(8,128)(2,1)S(1)} %collective-permute-done.12.refs_2_), channel_id=1, source_target_pairs={{0,2},{1,3},{2,0},{3,1},{4,6},{5,7},{6,4},{7,5},{8,10},{9,11},{10,... | collective-permute-start | bytes 688136 | tf_op jit(solution)/shard_map/ppermute | solution.py:369
  34.2 9.1 %collective-permute-start.16 = (bf16[7,128,128]{2,1,0:T(8,128)(2,1)S(1)}, bf16[7,128,128]{2,1,0:T(8,128)(2,1)S(1)}, u32[]{:S(2)}, u32[]{:S(2)}) collective-permute-start(bf16[7,128,128]{2,1,0:T(8,128)(2,1)S(1)} %collective-permute-done.7.refs_1_), channel_id=1, source_target_pairs={{0,1},{1,0},{2,3},{3,2},{4,5},{5,4},{6,7},{7,6},{8,9},{9,8},{10,11... | collective-permute-start | bytes 688136 | tf_op jit(solution)/shard_map/ppermute | solution.py:29
  36.2 7.1 %collective-permute-start.19 = (bf16[7,128,128]{2,1,0:T(8,128)(2,1)S(1)}, bf16[7,128,128]{2,1,0:T(8,128)(2,1)S(1)}, u32[]{:S(2)}, u32[]{:S(2)}) collective-permute-start(bf16[7,128,128]{2,1,0:T(8,128)(2,1)S(1)} %collective-permute-done.8.refs_6_), channel_id=1, source_target_pairs={{0,1},{1,0},{2,3},{3,2},{4,5},{5,4},{6,7},{7,6},{8,9},{9,8},{10,11... | collective-permute-start | bytes 688136 | tf_op jit(solution)/shard_map/ppermute | solution.py:29
  36.2 7.0 %collective-permute-start.17 = (bf16[7,128,128]{2,1,0:T(8,128)(2,1)S(1)}, bf16[7,128,128]{2,1,0:T(8,128)(2,1)S(1)}, u32[]{:S(2)}, u32[]{:S(2)}) collective-permute-start(bf16[7,128,128]{2,1,0:T(8,128)(2,1)S(1)} %collective-permute-done.12.refs_2_), channel_id=1, source_target_pairs={{0,1},{1,0},{2,3},{3,2},{4,5},{5,4},{6,7},{7,6},{8,9},{9,8},{10,11... | collective-permute-start | bytes 688136 | tf_op jit(solution)/shard_map/ppermute | solution.py:29
  36.7 6.6 %collective-permute-start.20 = (bf16[7,128,128]{2,1,0:T(8,128)(2,1)S(1)}, bf16[7,128,128]{2,1,0:T(8,128)(2,1)S(1)}, u32[]{:S(2)}, u32[]{:S(2)}) collective-permute-start(bf16[7,128,128]{2,1,0:T(8,128)(2,1)S(1)} %collective-permute-done.13.refs_7_), channel_id=1, source_target_pairs={{0,1},{1,0},{2,3},{3,2},{4,5},{5,4},{6,7},{7,6},{8,9},{9,8},{10,11... | collective-permute-start | bytes 688136 | tf_op jit(solution)/shard_map/ppermute | solution.py:29
  38.9 4.4 %collective-permute-start.21 = (bf16[7,128,128]{2,1,0:T(8,128)(2,1)}, bf16[7,128,128]{2,1,0:T(8,128)(2,1)S(1)}, u32[]{:S(2)}, u32[]{:S(2)}) collective-permute-start(bf16[7,128,128]{2,1,0:T(8,128)(2,1)} %collective-permute-done.18.refs_8_), channel_id=1, source_target_pairs={{0,1},{1,0},{2,3},{3,2},{4,5},{5,4},{6,7},{7,6},{8,9},{9,8},{10,11... | collective-permute-start | bytes 688136 | tf_op jit(solution)/shard_map/ppermute | solution.py:29
  57.8 9.8 %collective-permute-start.22 = (f16[1024,128]{1,0:T(8,128)(2,1)S(1)}, f16[1024,128]{1,0:T(8,128)(2,1)S(1)}, u32[]{:S(2)}, u32[]{:S(2)}) collective-permute-start(f16[1024,128]{1,0:T(8,128)(2,1)S(1)} %get-tuple-element.433), channel_id=1, source_target_pairs={{0,4},{12,8},{1,5},{13,9},{2,6},{14,10},{3,7},{15,11},{16,20},{28,... | collective-permute-start | bytes 786440 | tf_op jit(solution)/shard_map/ppermute | solution.py:307
  59.2 14.1 %collective-permute-start.25 = (f16[1024,128]{1,0:T(8,128)(2,1)S(1)}, f16[1024,128]{1,0:T(8,128)(2,1)S(1)}, u32[]{:S(2)}, u32[]{:S(2)}) collective-permute-start(f16[1024,128]{1,0:T(8,128)(2,1)S(1)} %get-tuple-element.432), channel_id=1, source_target_pairs={{0,4},{12,8},{1,5},{13,9},{2,6},{14,10},{3,7},{15,11},{16,20},{28,... | collective-permute-start | bytes 786440 | tf_op jit(solution)/shard_map/ppermute | solution.py:307
  69.6 9.9 %collective-permute-start.23 = (f16[1024,128]{1,0:T(8,128)(2,1)S(1)}, f16[1024,128]{1,0:T(8,128)(2,1)S(1)}, u32[]{:S(2)}, u32[]{:S(2)}) collective-permute-start(f16[1024,128]{1,0:T(8,128)(2,1)S(1)} %broadcast_select_fusion.36), channel_id=1, source_target_pairs={{0,4},{12,8},{1,5},{13,9},{2,6},{14,10},{3,7},{15,11},{16,20},{28,... | collective-permute-start | bytes 786440 | tf_op jit(solution)/shard_map/ppermute | solution.py:307
  71.1 8.5 %collective-permute-start.24 = (f16[1024,128]{1,0:T(8,128)(2,1)S(1)}, f16[1024,128]{1,0:T(8,128)(2,1)S(1)}, u32[]{:S(2)}, u32[]{:S(2)}) collective-permute-start(f16[1024,128]{1,0:T(8,128)(2,1)S(1)} %get-tuple-element.398), channel_id=1, source_target_pairs={{4,8},{8,4},{5,9},{9,5},{6,10},{10,6},{7,11},{11,7},{20,24},{24,20... | collective-permute-start | bytes 786440 | tf_op jit(solution)/shard_map/ppermute | solution.py:307
  74.9 9.7 %collective-permute-start.28 = (f16[1024,128]{1,0:T(8,128)(2,1)S(1)}, f16[1024,128]{1,0:T(8,128)(2,1)S(1)}, u32[]{:S(2)}, u32[]{:S(2)}) collective-permute-start(f16[1024,128]{1,0:T(8,128)(2,1)S(1)} %get-tuple-element.395), channel_id=1, source_target_pairs={{0,4},{12,8},{1,5},{13,9},{2,6},{14,10},{3,7},{15,11},{16,20},{28,... | collective-permute-start | bytes 786440 | tf_op jit(solution)/shard_map/ppermute | solution.py:307
  76.3 9.5 %collective-permute-start.29 = (f16[1024,128]{1,0:T(8,128)(2,1)S(1)}, f16[1024,128]{1,0:T(8,128)(2,1)S(1)}, u32[]{:S(2)}, u32[]{:S(2)}) collective-permute-start(f16[1024,128]{1,0:T(8,128)(2,1)S(1)} %broadcast_select_fusion.32), channel_id=1, source_target_pairs={{4,8},{8,4},{5,9},{9,5},{6,10},{10,6},{7,11},{11,7},{20,24},{24,20... | collective-permute-start | bytes 786440 | tf_op jit(solution)/shard_map/ppermute | solution.py:307
  81.3 8.5 %collective-permute-start.26 = (f16[1024,128]{1,0:T(8,128)(2,1)S(1)}, f16[1024,128]{1,0:T(8,128)(2,1)S(1)}, u32[]{:S(2)}, u32[]{:S(2)}) collective-permute-start(f16[1024,128]{1,0:T(8,128)(2,1)S(1)} %broadcast_select_fusion.30), channel_id=1, source_target_pairs={{0,4},{4,0},{8,12},{12,8},{1,5},{5,1},{9,13},{13,9},{2,6},{6,2},{1... | collective-permute-start | bytes 786440 | tf_op jit(solution)/shard_map/ppermute | solution.py:307
  81.4 9.1 %collective-permute-start.27 = (f16[1024,128]{1,0:T(8,128)(2,1)S(1)}, f16[1024,128]{1,0:T(8,128)(2,1)S(1)}, u32[]{:S(2)}, u32[]{:S(2)}) collective-permute-start(f16[1024,128]{1,0:T(8,128)(2,1)S(1)} %get-tuple-element.392), channel_id=1, source_target_pairs={{4,8},{8,4},{5,9},{9,5},{6,10},{10,6},{7,11},{11,7},{20,24},{24,20... | collective-permute-start | bytes 786440 | tf_op jit(solution)/shard_map/ppermute | solution.py:307
  86.3 9.2 %collective-permute-start.30 = (f16[1024,128]{1,0:T(8,128)(2,1)S(1)}, f16[1024,128]{1,0:T(8,128)(2,1)S(1)}, u32[]{:S(2)}, u32[]{:S(2)}) collective-permute-start(f16[1024,128]{1,0:T(8,128)(2,1)S(1)} %broadcast_select_fusion.27), channel_id=1, source_target_pairs={{0,4},{4,0},{8,12},{12,8},{1,5},{5,1},{9,13},{13,9},{2,6},{6,2},{1... | collective-permute-start | bytes 786440 | tf_op jit(solution)/shard_map/ppermute | solution.py:307
  86.4 10.3 %collective-permute-start.31 = (f16[1024,128]{1,0:T(8,128)(2,1)S(1)}, f16[1024,128]{1,0:T(8,128)(2,1)S(1)}, u32[]{:S(2)}, u32[]{:S(2)}) collective-permute-start(f16[1024,128]{1,0:T(8,128)(2,1)S(1)} %get-tuple-element.389), channel_id=1, source_target_pairs={{4,8},{8,4},{5,9},{9,5},{6,10},{10,6},{7,11},{11,7},{20,24},{24,20... | collective-permute-start | bytes 786440 | tf_op jit(solution)/shard_map/ppermute | solution.py:307
  91.2 9.8 %collective-permute-start.32 = (f16[1024,128]{1,0:T(8,128)(2,1)S(1)}, f16[1024,128]{1,0:T(8,128)(2,1)S(1)}, u32[]{:S(2)}, u32[]{:S(2)}) collective-permute-start(f16[1024,128]{1,0:T(8,128)(2,1)S(1)} %get-tuple-element.388), channel_id=1, source_target_pairs={{0,4},{4,0},{8,12},{12,8},{1,5},{5,1},{9,13},{13,9},{2,6},{6,2},{1... | collective-permute-start | bytes 786440 | tf_op jit(solution)/shard_map/ppermute | solution.py:307
  91.2 10.4 %collective-permute-start.33 = (f16[1024,128]{1,0:T(8,128)(2,1)S(1)}, f16[1024,128]{1,0:T(8,128)(2,1)S(1)}, u32[]{:S(2)}, u32[]{:S(2)}) collective-permute-start(f16[1024,128]{1,0:T(8,128)(2,1)S(1)} %get-tuple-element.387), channel_id=1, source_target_pairs={{4,8},{8,4},{5,9},{9,5},{6,10},{10,6},{7,11},{11,7},{20,24},{24,20... | collective-permute-start | bytes 786440 | tf_op jit(solution)/shard_map/ppermute | solution.py:307
  97.3 9.3 %collective-permute-start.34 = (f16[1024,128]{1,0:T(8,128)(2,1)S(1)}, f16[1024,128]{1,0:T(8,128)(2,1)S(1)}, u32[]{:S(2)}, u32[]{:S(2)}) collective-permute-start(f16[1024,128]{1,0:T(8,128)(2,1)S(1)} %get-tuple-element.384), channel_id=1, source_target_pairs={{0,4},{4,0},{8,12},{12,8},{1,5},{5,1},{9,13},{13,9},{2,6},{6,2},{1... | collective-permute-start | bytes 786440 | tf_op jit(solution)/shard_map/ppermute | solution.py:307
  97.4 9.9 %collective-permute-start.35 = (f16[1024,128]{1,0:T(8,128)(2,1)S(1)}, f16[1024,128]{1,0:T(8,128)(2,1)S(1)}, u32[]{:S(2)}, u32[]{:S(2)}) collective-permute-start(f16[1024,128]{1,0:T(8,128)(2,1)S(1)} %get-tuple-element.385), channel_id=1, source_target_pairs={{4,8},{8,4},{5,9},{9,5},{6,10},{10,6},{7,11},{11,7},{20,24},{24,20... | collective-permute-start | bytes 786440 | tf_op jit(solution)/shard_map/ppermute | solution.py:307
  102.3 9.6 %collective-permute-start.36 = (f16[1024,128]{1,0:T(8,128)(2,1)S(1)}, f16[1024,128]{1,0:T(8,128)(2,1)S(1)}, u32[]{:S(2)}, u32[]{:S(2)}) collective-permute-start(f16[1024,128]{1,0:T(8,128)(2,1)S(1)} %get-tuple-element.382), channel_id=1, source_target_pairs={{0,4},{4,0},{8,12},{12,8},{1,5},{5,1},{9,13},{13,9},{2,6},{6,2},{1... | collective-permute-start | bytes 786440 | tf_op jit(solution)/shard_map/ppermute | solution.py:307
  102.4 10.3 %collective-permute-start.37 = (f16[1024,128]{1,0:T(8,128)(2,1)S(1)}, f16[1024,128]{1,0:T(8,128)(2,1)S(1)}, u32[]{:S(2)}, u32[]{:S(2)}) collective-permute-start(f16[1024,128]{1,0:T(8,128)(2,1)S(1)} %get-tuple-element.381), channel_id=1, source_target_pairs={{4,8},{8,4},{5,9},{9,5},{6,10},{10,6},{7,11},{11,7},{20,24},{24,20... | collective-permute-start | bytes 786440 | tf_op jit(solution)/shard_map/ppermute | solution.py:307
  107.9 9.3 %collective-permute-start.38 = (f16[1024,128]{1,0:T(8,128)(2,1)S(1)}, f16[1024,128]{1,0:T(8,128)(2,1)S(1)}, u32[]{:S(2)}, u32[]{:S(2)}) collective-permute-start(f16[1024,128]{1,0:T(8,128)(2,1)S(1)} %get-tuple-element.379), channel_id=1, source_target_pairs={{0,4},{4,0},{8,12},{12,8},{1,5},{5,1},{9,13},{13,9},{2,6},{6,2},{1... | collective-permute-start | bytes 786440 | tf_op jit(solution)/shard_map/ppermute | solution.py:307
  108.0 9.9 %collective-permute-start.39 = (f16[1024,128]{1,0:T(8,128)(2,1)S(1)}, f16[1024,128]{1,0:T(8,128)(2,1)S(1)}, u32[]{:S(2)}, u32[]{:S(2)}) collective-permute-start(f16[1024,128]{1,0:T(8,128)(2,1)S(1)} %get-tuple-element.378), channel_id=1, source_target_pairs={{4,8},{8,4},{5,9},{9,5},{6,10},{10,6},{7,11},{11,7},{20,24},{24,20... | collective-permute-start | bytes 786440 | tf_op jit(solution)/shard_map/ppermute | solution.py:307
  113.3 9.3 %collective-permute-start.40 = (f16[1024,128]{1,0:T(8,128)(2,1)S(1)}, f16[1024,128]{1,0:T(8,128)(2,1)S(1)}, u32[]{:S(2)}, u32[]{:S(2)}) collective-permute-start(f16[1024,128]{1,0:T(8,128)(2,1)S(1)} %get-tuple-element.376), channel_id=1, source_target_pairs={{0,4},{4,0},{8,12},{12,8},{1,5},{5,1},{9,13},{13,9},{2,6},{6,2},{1... | collective-permute-start | bytes 786440 | tf_op jit(solution)/shard_map/ppermute | solution.py:307
  113.4 10.1 %collective-permute-start.41 = (f16[1024,128]{1,0:T(8,128)(2,1)S(1)}, f16[1024,128]{1,0:T(8,128)(2,1)S(1)}, u32[]{:S(2)}, u32[]{:S(2)}) collective-permute-start(f16[1024,128]{1,0:T(8,128)(2,1)S(1)} %get-tuple-element.375), channel_id=1, source_target_pairs={{4,8},{8,4},{5,9},{9,5},{6,10},{10,6},{7,11},{11,7},{20,24},{24,20... | collective-permute-start | bytes 786440 | tf_op jit(solution)/shard_map/ppermute | solution.py:307
  118.5 9.4 %collective-permute-start.42 = (f16[1024,128]{1,0:T(8,128)(2,1)S(1)}, f16[1024,128]{1,0:T(8,128)(2,1)S(1)}, u32[]{:S(2)}, u32[]{:S(2)}) collective-permute-start(f16[1024,128]{1,0:T(8,128)(2,1)S(1)} %get-tuple-element.372), channel_id=1, source_target_pairs={{0,4},{4,0},{8,12},{12,8},{1,5},{5,1},{9,13},{13,9},{2,6},{6,2},{1... | collective-permute-start | bytes 786440 | tf_op jit(solution)/shard_map/ppermute | solution.py:307
  118.6 10.3 %collective-permute-start.43 = (f16[1024,128]{1,0:T(8,128)(2,1)S(1)}, f16[1024,128]{1,0:T(8,128)(2,1)S(1)}, u32[]{:S(2)}, u32[]{:S(2)}) collective-permute-start(f16[1024,128]{1,0:T(8,128)(2,1)S(1)} %get-tuple-element.373), channel_id=1, source_target_pairs={{4,8},{8,4},{5,9},{9,5},{6,10},{10,6},{7,11},{11,7},{20,24},{24,20... | collective-permute-start | bytes 786440 | tf_op jit(solution)/shard_map/ppermute | solution.py:307
  124.1 18.1 %collective-permute-start.44 = (f16[1024,128]{1,0:T(8,128)(2,1)S(1)}, f16[1024,128]{1,0:T(8,128)(2,1)S(1)}, u32[]{:S(2)}, u32[]{:S(2)}) collective-permute-start(f16[1024,128]{1,0:T(8,128)(2,1)S(1)} %get-tuple-element.370), channel_id=1, source_target_pairs={{0,4},{4,0},{8,12},{12,8},{1,5},{5,1},{9,13},{13,9},{2,6},{6,2},{1... | collective-permute-start | bytes 786440 | tf_op jit(solution)/shard_map/ppermute | solution.py:307
  124.2 20.7 %collective-permute-start.45 = (f16[1024,128]{1,0:T(8,128)(2,1)S(1)}, f16[1024,128]{1,0:T(8,128)(2,1)S(1)}, u32[]{:S(2)}, u32[]{:S(2)}) collective-permute-start(f16[1024,128]{1,0:T(8,128)(2,1)S(1)} %get-tuple-element.369), channel_id=1, source_target_pairs={{4,8},{8,4},{5,9},{9,5},{6,10},{10,6},{7,11},{11,7},{20,24},{24,20... | collective-permute-start | bytes 786440 | tf_op jit(solution)/shard_map/ppermute | solution.py:307
  134.9 35.9 %collective-permute-start.52 = (bf16[1024,256]{0,1:T(8,128)(2,1)S(1)}, bf16[1024,256]{0,1:T(8,128)(2,1)S(1)}, u32[]{:S(2)}, u32[]{:S(2)}) collective-permute-start(bf16[1024,256]{0,1:T(8,128)(2,1)S(1)} %fusion.1), channel_id=1, source_target_pairs={{0,1},{1,0},{2,3},{3,2},{4,5},{5,4},{6,7},{7,6},{8,9},{9,8},{10,11... | collective-permute-start | bytes 1572872 | tf_op jit(solution)/shard_map/ppermute | solution.py:29
  141.2 30.2 %collective-permute-start.54 = (bf16[1024,256]{0,1:T(8,128)(2,1)S(1)}, bf16[1024,256]{0,1:T(8,128)(2,1)S(1)}, u32[]{:S(2)}, u32[]{:S(2)}) collective-permute-start(bf16[1024,256]{0,1:T(8,128)(2,1)S(1)} %fusion.1), channel_id=1, source_target_pairs={{0,2},{1,3},{2,0},{3,1},{4,6},{5,7},{6,4},{7,5},{8,10},{9,11},{10,... | collective-permute-start | bytes 1572872 | tf_op jit(solution)/shard_map/ppermute | solution.py:29
  142.2 7.5 %collective-permute-start.46 = (f16[1024,128]{1,0:T(8,128)(2,1)S(1)}, f16[1024,128]{1,0:T(8,128)(2,1)S(1)}, u32[]{:S(2)}, u32[]{:S(2)}) collective-permute-start(f16[1024,128]{1,0:T(8,128)(2,1)S(1)} %get-tuple-element.367), channel_id=1, source_target_pairs={{0,4},{4,0},{8,12},{12,8},{1,5},{5,1},{9,13},{13,9},{2,6},{6,2},{1... | collective-permute-start | bytes 786440 | tf_op jit(solution)/shard_map/ppermute | solution.py:307
  142.2 10.2 %collective-permute-start.47 = (f16[1024,128]{1,0:T(8,128)(2,1)S(1)}, f16[1024,128]{1,0:T(8,128)(2,1)S(1)}, u32[]{:S(2)}, u32[]{:S(2)}) collective-permute-start(f16[1024,128]{1,0:T(8,128)(2,1)S(1)} %get-tuple-element.366), channel_id=1, source_target_pairs={{4,8},{8,4},{5,9},{9,5},{6,10},{10,6},{7,11},{11,7},{20,24},{24,20... | collective-permute-start | bytes 786440 | tf_op jit(solution)/shard_map/ppermute | solution.py:307
  145.5 9.8 %collective-permute-start.48 = (f16[1024,128]{1,0:T(8,128)(2,1)S(1)}, f16[1024,128]{1,0:T(8,128)(2,1)S(1)}, u32[]{:S(2)}, u32[]{:S(2)}) collective-permute-start(f16[1024,128]{1,0:T(8,128)(2,1)S(1)} %get-tuple-element.355), channel_id=1, source_target_pairs={{0,4},{4,0},{8,12},{12,8},{1,5},{5,1},{9,13},{13,9},{2,6},{6,2},{1... | collective-permute-start | bytes 786440 | tf_op jit(solution)/shard_map/ppermute | solution.py:307
  149.7 8.3 %collective-permute-start.49 = (f16[1024,128]{1,0:T(8,128)(2,1)S(1)}, f16[1024,128]{1,0:T(8,128)(2,1)S(1)}, u32[]{:S(2)}, u32[]{:S(2)}) collective-permute-start(f16[1024,128]{1,0:T(8,128)(2,1)S(1)} %get-tuple-element.354), channel_id=1, source_target_pairs={{4,8},{8,4},{5,9},{9,5},{6,10},{10,6},{7,11},{11,7},{20,24},{24,20... | collective-permute-start | bytes 786440 | tf_op jit(solution)/shard_map/ppermute | solution.py:307
  153.1 6.9 %collective-permute-start.50 = (f16[1024,128]{1,0:T(8,128)(2,1)S(1)}, f16[1024,128]{1,0:T(8,128)(2,1)S(1)}, u32[]{:S(2)}, u32[]{:S(2)}) collective-permute-start(f16[1024,128]{1,0:T(8,128)(2,1)S(1)} %get-tuple-element.357), channel_id=1, source_target_pairs={{0,4},{4,0},{8,12},{12,8},{1,5},{5,1},{9,13},{13,9},{2,6},{6,2},{1... | collective-permute-start | bytes 786440 | tf_op jit(solution)/shard_map/ppermute | solution.py:307
  155.4 8.3 %collective-permute-start.51 = (f16[1024,128]{1,0:T(8,128)(2,1)S(1)}, f16[1024,128]{1,0:T(8,128)(2,1)S(1)}, u32[]{:S(2)}, u32[]{:S(2)}) collective-permute-start(f16[1024,128]{1,0:T(8,128)(2,1)S(1)} %get-tuple-element.358), channel_id=1, source_target_pairs={{4,8},{8,4},{5,9},{9,5},{6,10},{10,6},{7,11},{11,7},{20,24},{24,20... | collective-permute-start | bytes 786440 | tf_op jit(solution)/shard_map/ppermute | solution.py:307
  158.7 14.9 %collective-permute-start.60 = (f16[1024,128]{1,0:T(8,128)(2,1)S(1)}, f16[1024,128]{1,0:T(8,128)(2,1)S(1)}, u32[]{:S(2)}, u32[]{:S(2)}) collective-permute-start(f16[1024,128]{1,0:T(8,128)(2,1)S(1)} %get-tuple-element.361), channel_id=1, source_target_pairs={{4,0},{8,12},{5,1},{9,13},{6,2},{10,14},{7,3},{11,15},{20,16},{24,... | collective-permute-start | bytes 786440 | tf_op jit(solution)/shard_map/ppermute | solution.py:307
  160.0 16.3 %collective-permute-start.61 = (f16[1024,128]{1,0:T(8,128)(2,1)S(1)}, f16[1024,128]{1,0:T(8,128)(2,1)S(1)}, u32[]{:S(2)}, u32[]{:S(2)}) collective-permute-start(f16[1024,128]{1,0:T(8,128)(2,1)S(1)} %get-tuple-element.360), channel_id=1, source_target_pairs={{4,8},{8,4},{5,9},{9,5},{6,10},{10,6},{7,11},{11,7},{20,24},{24,20... | collective-permute-start | bytes 786440 | tf_op jit(solution)/shard_map/ppermute | solution.py:307
  167.5 12.5 %collective-permute-start.53 = (bf16[1024,128]{0,1:T(8,128)(2,1)S(1)}, bf16[1024,128]{0,1:T(8,128)(2,1)S(1)}, u32[]{:S(2)}, u32[]{:S(2)}) collective-permute-start(bf16[1024,128]{0,1:T(8,128)(2,1)S(1)} %fusion.2), channel_id=1, source_target_pairs={{0,1},{1,0},{2,3},{3,2},{4,5},{5,4},{6,7},{7,6},{8,9},{9,8},{10,11... | collective-permute-start | bytes 786440 | tf_op jit(solution)/shard_map/ppermute | solution.py:29
  170.8 7.9 %collective-permute-start.55 = (bf16[1024,128]{0,1:T(8,128)(2,1)S(1)}, bf16[1024,128]{0,1:T(8,128)(2,1)S(1)}, u32[]{:S(2)}, u32[]{:S(2)}) collective-permute-start(bf16[1024,128]{0,1:T(8,128)(2,1)S(1)} %fusion.2), channel_id=1, source_target_pairs={{0,2},{1,3},{2,0},{3,1},{4,6},{5,7},{6,4},{7,5},{8,10},{9,11},{10,... | collective-permute-start | bytes 786440 | tf_op jit(solution)/shard_map/ppermute | solution.py:29
  171.4 11.5 %collective-permute-start.62 = (f16[1024,128]{1,0:T(8,128)(2,1)S(1)}, f16[1024,128]{1,0:T(8,128)(2,1)S(1)}, u32[]{:S(2)}, u32[]{:S(2)}) collective-permute-start(f16[1024,128]{1,0:T(8,128)(2,1)S(1)} %get-tuple-element.364), channel_id=1, source_target_pairs={{4,0},{8,12},{5,1},{9,13},{6,2},{10,14},{7,3},{11,15},{20,16},{24,... | collective-permute-start | bytes 786440 | tf_op jit(solution)/shard_map/ppermute | solution.py:307
  173.5 9.4 %collective-permute-start.63 = (f16[1024,128]{1,0:T(8,128)(2,1)S(1)}, f16[1024,128]{1,0:T(8,128)(2,1)S(1)}, u32[]{:S(2)}, u32[]{:S(2)}) collective-permute-start(f16[1024,128]{1,0:T(8,128)(2,1)S(1)} %get-tuple-element.363), channel_id=1, source_target_pairs={{4,8},{8,4},{5,9},{9,5},{6,10},{10,6},{7,11},{11,7},{20,24},{24,20... | collective-permute-start | bytes 786440 | tf_op jit(solution)/shard_map/ppermute | solution.py:307
  176.3 5.8 %collective-permute-start.56 = (bf16[1024,256]{0,1:T(8,128)(2,1)S(1)}, bf16[1024,256]{0,1:T(8,128)(2,1)S(1)}, u32[]{:S(2)}, u32[]{:S(2)}) collective-permute-start(bf16[1024,256]{0,1:T(8,128)(2,1)S(1)} %collective-permute-done.54), channel_id=1, source_target_pairs={{0,1},{1,0},{2,3},{3,2},{4,5},{5,4},{6,7},{7,6},{8,9},{9,8},{10,11... | collective-permute-start | bytes 1572872 | tf_op jit(solution)/shard_map/ppermute | solution.py:29
  178.7 6.3 %collective-permute-start.64 = (f16[1024,128]{1,0:T(8,128)(2,1)S(1)}, f16[1024,128]{1,0:T(8,128)(2,1)S(1)}, u32[]{:S(2)}, u32[]{:S(2)}) collective-permute-start(f16[1024,128]{1,0:T(8,128)(2,1)S(1)} %get-tuple-element.346), channel_id=1, source_target_pairs={{4,0},{8,12},{5,1},{9,13},{6,2},{10,14},{7,3},{11,15},{20,16},{24,... | collective-permute-start | bytes 786440 | tf_op jit(solution)/shard_map/ppermute | solution.py:307
  183.5 7.5 %collective-permute-start.65 = (f16[1024,128]{1,0:T(8,128)(2,1)S(1)}, f16[1024,128]{1,0:T(8,128)(2,1)S(1)}, u32[]{:S(2)}, u32[]{:S(2)}) collective-permute-start(f16[1024,128]{1,0:T(8,128)(2,1)S(1)} %get-tuple-element.348), channel_id=1, source_target_pairs={{4,0},{8,12},{5,1},{9,13},{6,2},{10,14},{7,3},{11,15},{20,16},{24,... | collective-permute-start | bytes 786440 | tf_op jit(solution)/shard_map/ppermute | solution.py:307
  185.4 29.8 %collective-permute-start.58 = (bf16[2,384,384]{1,2,0:T(8,128)(2,1)S(1)}, bf16[2,384,384]{1,2,0:T(8,128)(2,1)S(1)}, u32[]{:S(2)}, u32[]{:S(2)}) collective-permute-start(bf16[2,384,384]{1,2,0:T(8,128)(2,1)S(1)} %pad_maximum_fusion.7), channel_id=1, source_target_pairs={{0,4},{4,0},{8,12},{12,8},{1,5},{5,1},{9,13},{13,9},{2,6},{6,2},{1... | collective-permute-start | bytes 1769480 | tf_op jit(solution)/shard_map/ppermute | solution.py:409
  194.6 14.2 %collective-permute-start.69 = (bf16[1024,128]{0,1:T(8,128)(2,1)S(1)}, bf16[1024,128]{0,1:T(8,128)(2,1)S(1)}, u32[]{:S(2)}, u32[]{:S(2)}) collective-permute-start(bf16[1024,128]{0,1:T(8,128)(2,1)S(1)} %bitcast.118), channel_id=1, source_target_pairs={{0,2},{1,3},{2,0},{3,1},{4,6},{5,7},{6,4},{7,5},{8,10},{9,11},{10,... | collective-permute-start | bytes 786440 | tf_op jit(solution)/shard_map/ppermute | solution.py:29
  194.7 16.0 %collective-permute-start.68 = (bf16[1024,128]{0,1:T(8,128)(2,1)S(1)}, bf16[1024,128]{0,1:T(8,128)(2,1)S(1)}, u32[]{:S(2)}, u32[]{:S(2)}) collective-permute-start(bf16[1024,128]{0,1:T(8,128)(2,1)S(1)} %bitcast.119), channel_id=1, source_target_pairs={{0,1},{1,0},{2,3},{3,2},{4,5},{5,4},{6,7},{7,6},{8,9},{9,8},{10,11... | collective-permute-start | bytes 786440 | tf_op jit(solution)/shard_map/ppermute | solution.py:29
  199.3 8.5 %collective-permute-start.66 = (bf16[2,384,128]{1,2,0:T(8,128)(2,1)S(1)}, bf16[2,384,128]{1,2,0:T(8,128)(2,1)S(1)}, u32[]{:S(2)}, u32[]{:S(2)}) collective-permute-start(bf16[2,384,128]{1,2,0:T(8,128)(2,1)S(1)} %pad_maximum_fusion.9), channel_id=1, source_target_pairs={{0,4},{4,0},{8,12},{12,8},{1,5},{5,1},{9,13},{13,9},{2,6},{6,2},{1... | collective-permute-start | bytes 589832 | tf_op jit(solution)/shard_map/ppermute | solution.py:409
  207.9 8.0 %collective-permute-start.67 = (bf16[384,128]{0,1:T(8,128)(2,1)S(1)}, bf16[384,128]{0,1:T(8,128)(2,1)S(1)}, u32[]{:S(2)}, u32[]{:S(2)}) collective-permute-start(bf16[384,128]{0,1:T(8,128)(2,1)S(1)} %fusion.6), channel_id=1, source_target_pairs={{0,12},{4,8},{8,4},{12,0},{1,13},{5,9},{9,5},{13,1},{2,14},{6,10},... | collective-permute-start | bytes 294920 | tf_op jit(solution)/shard_map/ppermute | solution.py:411
  212.0 9.5 %collective-permute-start.71 = (bf16[2,128,512]{1,2,0:T(8,128)(2,1)S(1)}, bf16[2,128,512]{1,2,0:T(8,128)(2,1)S(1)}, u32[]{:S(2)}, u32[]{:S(2)}) collective-permute-start(bf16[2,128,512]{1,2,0:T(8,128)(2,1)S(1)} %pad_maximum_fusion.8), channel_id=1, source_target_pairs={{0,4},{4,0},{8,12},{12,8},{1,5},{5,1},{9,13},{13,9},{2,6},{6,2},{1... | collective-permute-start | bytes 786440 | tf_op jit(solution)/shard_map/ppermute | solution.py:409
  215.2 17.1 %collective-permute-start.59 = (bf16[384,384]{0,1:T(8,128)(2,1)S(1)}, bf16[384,384]{0,1:T(8,128)(2,1)S(1)}, u32[]{:S(2)}, u32[]{:S(2)}) collective-permute-start(bf16[384,384]{0,1:T(8,128)(2,1)S(1)} %fusion.3), channel_id=1, source_target_pairs={{0,12},{4,8},{8,4},{12,0},{1,13},{5,9},{9,5},{13,1},{2,14},{6,10},... | collective-permute-start | bytes 884744 | tf_op jit(solution)/shard_map/ppermute | solution.py:411
  221.6 13.6 %collective-permute-start.72 = (bf16[128,512]{0,1:T(8,128)(2,1)S(1)}, bf16[128,512]{0,1:T(8,128)(2,1)S(1)}, u32[]{:S(2)}, u32[]{:S(2)}) collective-permute-start(bf16[128,512]{0,1:T(8,128)(2,1)S(1)} %fusion.5), channel_id=1, source_target_pairs={{0,12},{4,8},{8,4},{12,0},{1,13},{5,9},{9,5},{13,1},{2,14},{6,10},... | collective-permute-start | bytes 393224 | tf_op jit(solution)/shard_map/ppermute | solution.py:411
  (11 other events, 52.8 us)
